TPU v7x, 32 devices: a whole 2x2x4 slice. The times are simulated.
32 devices in a mesh: groups: 1, wide: 32 (over z, y, x, core).
Axes of the slice: x: 2, y: 2, z: 4, core: 2. Of those that a mesh axis runs over, the one named last changes fastest.
Arguments:
- inputs: bfloat16 [3, 128, 8192], P(None, 'groups', 'wide'), may hold values from -6 to 6
- base_weight: bfloat16 [8192, 8192], P('wide'), may hold values from -0.0625 to 0.0625
- shrink_table: bfloat16 [64, 64, 8192], P('wide'), may hold values from -0.0625 to 0.0625
- expand_table: bfloat16 [64, 64, 8192], P('wide'), may hold values from -0.75 to 0.75
- table_slot: int32 [64], replicated, may hold values from 0 to 63, each once
- adapter_ids: int32 [3, 128], P(None, 'groups'), may hold values from 0 to 63
Outputs:
- projected: bfloat16 [3, 128, 8192], P(None, 'groups', 'wide')
Inputs may be any that keep to these rules, and one draw needn't show every extreme that they name: `table_slot`: each table row holds exactly one adapter; table rows t * 2 to (t + 1) * 2 - 1 stand on index t of wide.
All inputs are finite; a program needn't handle non-finite values.
Results may differ from a plain program's by a relative error of at most 0.0048.
Values may be sent and summed in bfloat16 or wider, within the bound.
No kernel may reach another device: no remote copies, remote signals or barrier semaphores. Data moves between devices by JAX's collectives and lax.ppermute only.
A program may use at most 128 MiB of HBM per device.

v0:
```python
import jax
import jax.numpy as jnp
from jax import lax
from jax.sharding import PartitionSpec as P


def body(inputs, base_weight, shrink_table, expand_table, table_slot, adapter_ids):
    step_count, request_count, width_part = inputs.shape
    table_size = table_slot.shape[0]
    rank_size = shrink_table.shape[1]
    onehot = (adapter_ids[:, :, None] == jnp.arange(table_size, dtype=jnp.int32)).astype(jnp.int32)
    slot_rows = jnp.sum(onehot * table_slot, axis=-1)
    shrink_slices, expand_slices = (
        lax.all_to_all(shrink_table, "wide", split_axis=2, concat_axis=0, tiled=True),
        lax.all_to_all(expand_table, "wide", split_axis=2, concat_axis=0, tiled=True),
    )
    shrink_flat = shrink_slices.reshape(table_size * rank_size, width_part)
    expand_flat = expand_slices.reshape(table_size * rank_size, width_part)
    results = []
    for step_index in range(step_count):
        features = inputs[step_index]
        picked = slot_rows[step_index]
        select = (picked[:, None] == jnp.arange(table_size, dtype=jnp.int32)).astype(jnp.float32)
        base_out = lax.dot_general(
            lax.all_gather(features, "wide", axis=1, tiled=True),
            base_weight,
            (((1,), (1,)), ((), ())),
            preferred_element_type=jnp.float32,
        )
        every = lax.dot_general(
            features, shrink_flat, (((1,), (1,)), ((), ())), preferred_element_type=jnp.float32
        )
        every = every.reshape(request_count, table_size, rank_size)
        partial_sum = jnp.einsum("rak,ra->rk", every, select)
        low_rank = lax.psum(partial_sum, "wide").astype(jnp.bfloat16)
        weighted = low_rank[:, None, :] * select[:, :, None].astype(jnp.bfloat16)
        weighted = weighted.reshape(request_count, table_size * rank_size)
        adapter_out = jnp.dot(weighted, expand_flat, preferred_element_type=jnp.float32)
        results.append((base_out + 2.0 * adapter_out).astype(jnp.bfloat16))
    return jnp.stack(results)


def solution(mesh):
    return jax.shard_map(
        body,
        mesh=mesh,
        in_specs=(
            P(None, "groups", "wide"),
            P("wide", None),
            P("wide", None, None),
            P("wide", None, None),
            P(),
            P(None, "groups"),
        ),
        out_specs=P(None, "groups", "wide"),
        check_vma=False,
    )
```

profile of v0, /device:TPU:0, one launch (start us, length us, event | category | flops | bytes accessed | tf_op | source)
XLA Modules:
  0.0 243.1 jit_solution(15041134373883666494)
XLA Ops:
  6.5 0.0 all-gather.9.cloned.1.call-start
  6.5 1.6 fusion.45
  8.1 0.0 all-gather.9.cloned.1.call-update
  8.1 9.5 %copy.15 = bf16[2,64,8192]{1,0,2:T(2,128)(2,1)} copy(bf16[2,64,8192]{2,1,0:T(8,128)(2,1)} %param.8) | data formatting | bytes 4194304 | tf_op args[2]
  17.6 9.8 %reshape.153 = bf16[32,2,16384]{2,1,0:T(2,128)(2,1)} reshape(bf16[8192,2,64]{2,1,0:T(2,128)(2,1)} %bitcast.85) | data formatting | bytes 4194304
  27.4 7.3 %all-to-all-start = ((bf16[32,2,16384]{2,1,0:T(2,128)(2,1)}), bf16[32,2,16384]{2,1,0:T(2,128)(2,1)S(1)}, u32[]{:S(2)}, u32[]{:S(2)}) async-start(bf16[32,2,16384]{2,1,0:T(2,128)(2,1)} %reshape.153), calls=%async_computation | async-start | bytes 4194304 | tf_op jit(solution)/shard_map/all_to_all | solution.py:14
  34.7 0.0 all-gather.11.cloned.1.call-start
  34.8 0.7 all-gather.11.cloned.1.call-update
  35.5 9.5 %copy.18 = bf16[2,64,8192]{1,0,2:T(2,128)(2,1)} copy(bf16[2,64,8192]{2,1,0:T(8,128)(2,1)} %param.9) | data formatting | bytes 4194304 | tf_op args[3]
  45.0 9.8 %reshape.155 = bf16[32,2,16384]{2,1,0:T(2,128)(2,1)} reshape(bf16[8192,2,64]{2,1,0:T(2,128)(2,1)} %bitcast.86) | data formatting | bytes 4194304
  54.8 0.0 copy-start.2
  54.8 0.0 copy-start.3
  54.8 39.2 %all-to-all-done = bf16[32,2,16384]{2,1,0:T(2,128)(2,1)S(1)} async-done(((bf16[32,2,16384]{2,1,0:T(2,128)(2,1)}), bf16[32,2,16384]{2,1,0:T(2,128)(2,1)S(1)}, u32[]{:S(2)}, u32[]{:S(2)}) %all-to-all-start) | async-done | bytes 2097184 | tf_op jit(solution)/shard_map/all_to_all | solution.py:14
  94.0 4.3 %all-to-all-start.1 = ((bf16[32,2,16384]{2,1,0:T(2,128)(2,1)}), bf16[32,2,16384]{2,1,0:T(2,128)(2,1)}, u32[]{:S(2)}, u32[]{:S(2)}) async-start(bf16[32,2,16384]{2,1,0:T(2,128)(2,1)} %reshape.155), calls=%async_computation.1 | async-start | bytes 4194304 | tf_op jit(solution)/shard_map/all_to_all | solution.py:15
  98.3 0.0 all-gather.7.cloned.1.call-start
  98.3 0.7 all-gather.7.cloned.1.call-update
  99.0 0.0 copy-done.2
  99.0 0.0 copy-done.3
  99.0 0.1 select_reduce_fusion
  99.2 4.0 %reshape.154 = bf16[8192,2,64]{2,1,0:T(2,128)(2,1)} reshape(bf16[32,2,16384]{2,1,0:T(2,128)(2,1)S(1)} %all-to-all-done) | data formatting | bytes 4194304
  103.2 9.7 %copy.34 = bf16[2,64,32,256]{3,1,0,2:T(8,128)(2,1)} copy(bf16[2,64,32,256]{1,0,3,2:T(2,128)(2,1)} %bitcast.83) | data formatting | bytes 4194304 | tf_op jit(solution)/shard_map/all_to_all | solution.py:14
  112.9 45.5 %all-to-all-done.1 = bf16[32,2,16384]{2,1,0:T(2,128)(2,1)} async-done(((bf16[32,2,16384]{2,1,0:T(2,128)(2,1)}), bf16[32,2,16384]{2,1,0:T(2,128)(2,1)}, u32[]{:S(2)}, u32[]{:S(2)}) %all-to-all-start.1) | async-done | bytes 2097184 | tf_op jit(solution)/shard_map/all_to_all | solution.py:15
  158.4 9.7 %reshape.156 = bf16[8192,2,64]{2,1,0:T(2,128)(2,1)} reshape(bf16[32,2,16384]{2,1,0:T(2,128)(2,1)} %all-to-all-done.1) | data formatting | bytes 4194304
  168.1 0.0 copy-start.1
  168.1 9.3 %copy.36 = bf16[2,64,32,256]{3,1,0,2:T(8,128)(2,1)S(1)} copy(bf16[2,64,32,256]{1,0,3,2:T(2,128)(2,1)} %bitcast.84) | data formatting | bytes 4194304 | tf_op jit(solution)/shard_map/all_to_all | solution.py:15
  177.5 0.0 copy-start
  177.5 0.0 copy-done.1
  177.5 2.5 %multiply_reduce_fusion = f32[128,64]{0,1:T(8,128)S(1)} fusion(bf16[64,64,256]{2,1,0:T(8,128)(2,1)} %bitcast.90, f32[128,64]{0,1:T(8,128)S(1)} %get-tuple-element.18, bf16[3,128,256]{2,1,0:T(8,128)(2,1)S(1)} %copy-done.1), kind=kOutput, calls=%fused_computation.6 | convolution fusion | flops 269475840 | bytes 2228224 | tf_op jit(solution)/shard_map/dot_general | solution.py:30
  180.0 0.0 copy-done
  180.0 0.8 multiply_reduce_fusion.1
  180.8 0.8 multiply_reduce_fusion.2
  181.6 39.3 %all-reduce = (bf16[128,64]{0,1:T(8,128)(2,1)S(1)}, bf16[128,64]{0,1:T(8,128)(2,1)S(1)}, bf16[128,64]{0,1:T(8,128)(2,1)S(1)}) all-reduce(f32[128,64]{0,1:T(8,128)S(1)} %multiply_reduce_fusion, f32[128,64]{0,1:T(8,128)S(1)} %multiply_reduce_fusion.1, ...), channel_id=1, replica_groups=mesh['groups'=1,'wide'=32] {'wide'}, use_global_device_ids=true, to_apply=%region_3.0 | all-reduce | flops 24576 | bytes 147456 | tf_op jit(solution)/shard_map/psum | solution.py:35
  220.9 0.1 broadcast_multiply_fusion.1
  221.0 0.1 broadcast_multiply_fusion
  221.1 0.1 broadcast_multiply_fusion.2
  221.1 0.5 convolution_multiply_fusion.1
  221.7 0.5 convolution_multiply_fusion
  222.2 0.5 convolution_multiply_fusion.2
  222.7 0.0 all-gather.9.cloned.1.call-done
  222.8 4.4 %fusion.27 = bf16[1,128,256]{2,1,0:T(8,128)(2,1)S(1)} fusion(f32[128,256]{1,0:T(8,128)S(1)} %convolution_multiply_fusion.1, bf16[256,8192]{1,0:T(8,128)(2,1)} %param.7, bf16[1,128,8192]{2,1,0:T(8,128)(2,1)} %all-gather.9.cloned.1.call-done), kind=kOutput, calls=%fused_computation.19 | convolution fusion | flops 536936448 | bytes 6488064 | tf_op jit(solution)/shard_map/dot_general | solution.py:24
  227.1 0.0 all-gather.11.cloned.1.call-done
  227.1 4.4 %fusion.30 = bf16[1,128,256]{2,1,0:T(8,128)(2,1)S(1)} fusion(f32[128,256]{1,0:T(8,128)S(1)} %convolution_multiply_fusion, bf16[256,8192]{1,0:T(8,128)(2,1)} %param.7, bf16[1,128,8192]{2,1,0:T(8,128)(2,1)} %all-gather.11.cloned.1.call-done), kind=kOutput, calls=%fused_computation.20 | convolution fusion | flops 536936448 | bytes 6488064 | tf_op jit(solution)/shard_map/dot_general | solution.py:24
  231.5 0.0 all-gather.7.cloned.1.call-done
  231.5 4.4 %fusion.24 = bf16[1,128,256]{2,1,0:T(8,128)(2,1)S(1)} fusion(f32[128,256]{1,0:T(8,128)S(1)} %convolution_multiply_fusion.2, bf16[256,8192]{1,0:T(8,128)(2,1)} %param.7, bf16[1,128,8192]{2,1,0:T(8,128)(2,1)} %all-gather.7.cloned.1.call-done), kind=kOutput, calls=%fused_computation.18 | convolution fusion | flops 536936448 | bytes 6488064 | tf_op jit(solution)/shard_map/dot_general | solution.py:24
  235.9 0.7 pad_maximum_fusion
  (3 shorter events, 0.0 us)
Async XLA Ops:
  6.5 216.2 %all-gather.9.cloned.1.call-start = ((), (), s32[]{:S(2)}) async-start(), calls=%async_computation.3 | async-start | bytes 2162688 | tf_op jit(solution)/shard_map/all_gather | solution.py:25
  27.4 66.5 %all-to-all-start = ((bf16[32,2,16384]{2,1,0:T(2,128)(2,1)}), bf16[32,2,16384]{2,1,0:T(2,128)(2,1)S(1)}, u32[]{:S(2)}, u32[]{:S(2)}) async-start(bf16[32,2,16384]{2,1,0:T(2,128)(2,1)} %reshape.153), calls=%async_computation | async-start | bytes 4194304 | tf_op jit(solution)/shard_map/all_to_all | solution.py:14
  34.7 192.4 %all-gather.11.cloned.1.call-start = ((), (), s32[]{:S(2)}) async-start(), calls=%async_computation.4 | async-start | bytes 2162688 | tf_op jit(solution)/shard_map/all_gather | solution.py:25
  54.8 44.2 %copy-start.2 = (s32[3,128]{1,0:T(4,128)S(1)}, s32[3,128]{1,0:T(4,128)}, u32[]{:S(2)}) copy-start(s32[3,128]{1,0:T(4,128)} %param.11) | copy-start | bytes 4612
  54.8 44.2 %copy-start.3 = (s32[64]{0:T(128)S(1)}, s32[64]{0:T(128)}, u32[]{:S(2)}) copy-start(s32[64]{0:T(128)} %param.10) | copy-start | bytes 772
  94.0 64.4 %all-to-all-start.1 = ((bf16[32,2,16384]{2,1,0:T(2,128)(2,1)}), bf16[32,2,16384]{2,1,0:T(2,128)(2,1)}, u32[]{:S(2)}, u32[]{:S(2)}) async-start(bf16[32,2,16384]{2,1,0:T(2,128)(2,1)} %reshape.155), calls=%async_computation.1 | async-start | bytes 4194304 | tf_op jit(solution)/shard_map/all_to_all | solution.py:15
  98.3 133.3 %all-gather.7.cloned.1.call-start = ((), (), s32[]{:S(2)}) async-start(), calls=%async_computation.2 | async-start | bytes 2162688 | tf_op jit(solution)/shard_map/all_gather | solution.py:25
  168.1 9.3 %copy-start.1 = (bf16[3,128,256]{2,1,0:T(8,128)(2,1)S(1)}, bf16[3,128,256]{2,1,0:T(8,128)(2,1)}, u32[]{:S(2)}) copy-start(bf16[3,128,256]{2,1,0:T(8,128)(2,1)} %param.6) | copy-start | bytes 589828
  177.5 2.5 %copy-start = (bf16[2,64,32,256]{3,1,0,2:T(8,128)(2,1)S(1)}, bf16[2,64,32,256]{3,1,0,2:T(8,128)(2,1)}, u32[]{:S(2)}) copy-start(bf16[2,64,32,256]{3,1,0,2:T(8,128)(2,1)} %copy.34) | copy-start | bytes 6291460
Sparse Core Ops, SparseCore 0:
  10.2 77.7 all-gather.8
  90.9 65.9 all-gather.10
  159.8 59.3 all-gather.6
where the time goes:
time: 246 us; the launch traced here: 243 us
  waiting for transfers between devices  86.1 us (35%)
  local copies, waits for them, and re-layouts  73.1 us (30%)
  blocking collectives  39.3 us (16%)
  matrix products  18.7 us (8%)
  between operations  13.3 us (5%)
  starting transfers between devices  11.7 us (5%)
    unnamed x14, local copies, waits for them, and re-layouts  52.4 us
    all_to_all x1, waiting for transfers between devices, body(): lax.all_to_all(expand_table, 'wide', split_axis=2, concat_axis=0, tiled=T...  45.5 us
    psum x1, blocking collectives, body(): low_rank = lax.psum(partial_sum, 'wide').astype(jnp.bfloat16)  39.3 us
    all_to_all x1, waiting for transfers between devices, body(): lax.all_to_all(shrink_table, 'wide', split_axis=2, concat_axis=0, tiled=T...  39.2 us
    dot_general x3, matrix products, body(): lax.dot_general(lax.all_gather(features, 'wide', axis=1, tiled=True), bas...  13.1 us
    all_to_all x1, local copies, waits for them, and re-layouts, body(): lax.all_to_all(shrink_table, 'wide', split_axis=2, concat_axis=0, tiled=T...  9.74 us
    all_to_all x1, local copies, waits for them, and re-layouts, body(): lax.all_to_all(expand_table, 'wide', split_axis=2, concat_axis=0, tiled=T...  9.33 us
    all_to_all x1, starting transfers between devices, body(): lax.all_to_all(shrink_table, 'wide', split_axis=2, concat_axis=0, tiled=T...  7.3 us
  transfers between devices with their start and end apart: 5, of which 2 were waited for; matrix products, arithmetic and copies ran while one was open for 35% of the time, Pallas kernels for 0%

commit v1 on v0

v1 whole, which is shorter than its diff:
```python
import functools

import jax
import jax.numpy as jnp
from jax import lax
from jax.experimental import pallas as pl
from jax.experimental.pallas import tpu as pltpu
from jax.sharding import PartitionSpec as P

SLOTS = 32
NT = (((1,), (1,)), ((), ()))
F32 = jnp.float32
BF16 = jnp.bfloat16


def vmem(count):
    return [pl.BlockSpec(memory_space=pltpu.VMEM)] * count


def owner_kernel(rows_ref, mask_ref, s0_ref, s1_ref, e0_ref, e1_ref, out_ref):
    parts, _, width = rows_ref.shape
    half = s0_ref.shape[0]
    lows = []
    for index, table in enumerate((s0_ref, s1_ref)):
        total = jnp.zeros((rows_ref.shape[1], half), F32)
        for part in range(parts):
            total += lax.dot_general(
                rows_ref[part], table[:, part * width : (part + 1) * width], NT, preferred_element_type=F32
            )
        lows.append((total * mask_ref[:, index * half : (index + 1) * half]).astype(BF16))
    for part in range(parts):
        columns = slice(part * width, (part + 1) * width)
        value = jnp.dot(lows[0], e0_ref[:, columns], preferred_element_type=F32)
        value += jnp.dot(lows[1], e1_ref[:, columns], preferred_element_type=F32)
        out_ref[part] = value.astype(BF16)


def owner(rows, mask, s0, s1, e0, e1):
    return pl.pallas_call(
        owner_kernel,
        out_shape=jax.ShapeDtypeStruct(rows.shape, BF16),
        in_specs=vmem(6),
        out_specs=vmem(1)[0],
        compiler_params=pltpu.CompilerParams(vmem_limit_bytes=32 << 20),
        name="owner",
    )(rows, mask, s0, s1, e0, e1)


def base_kernel(whole, place_ref, *refs):
    *blocks, w0_ref, w1_ref, out0_ref, out1_ref = refs
    rows = out0_ref.shape[0]
    width = blocks[0].shape[1] // 2
    for w_ref, out_ref in ((w0_ref, out0_ref), (w1_ref, out1_ref)):
        total = jnp.zeros(out_ref.shape, F32)
        for part in range(len(whole)):
            first = whole[part]
            block = blocks[first][...]
            if block.shape[0] != rows:
                block = jnp.concatenate([block, blocks[first + 1][...]], axis=0)
            for side in range(2):
                start = pl.multiple_of(place_ref[2 * part + side], width)
                total += lax.dot_general(
                    block[:, side * width : (side + 1) * width],
                    w_ref[:, pl.ds(start, width)],
                    NT,
                    preferred_element_type=F32,
                )
        out_ref[...] = total


def base(places, blocks, whole, w0, w1):
    rows = blocks[0].shape[0]
    shape = jax.ShapeDtypeStruct((rows, w0.shape[0]), F32)
    return pl.pallas_call(
        functools.partial(base_kernel, whole),
        out_shape=(shape, shape),
        in_specs=[pl.BlockSpec(memory_space=pltpu.SMEM)] + vmem(len(blocks) + 2),
        out_specs=tuple(vmem(2)),
        compiler_params=pltpu.CompilerParams(vmem_limit_bytes=40 << 20),
        name="base",
    )(places, *blocks, w0, w1)


def body(groups, inputs, base_weight, shrink_table, expand_table, table_slot, adapter_ids):
    wide = lax.axis_size("wide")
    me = lax.axis_index("wide")
    core, chip = me % 2, me // 2
    chips = wide // 2
    steps, requests, width = inputs.shape
    count = steps * requests
    held, rank, _ = shrink_table.shape
    features = inputs.reshape(count, width)

    def move(value, target):
        pairs = [(2 * c + k, 2 * target(c) + k) for c in range(chips) for k in range(2)]
        return lax.ppermute(value, "wide", pairs)

    def swap(value):
        return lax.ppermute(value, "wide", [(i, i ^ 1) for i in range(wide)])

    def flip(bits):
        return lambda c: c ^ bits

    def shift(k):
        return lambda c: (c + 4 * k) % chips

    half = requests // 2
    split = inputs.reshape(steps, 2, half, width)
    own_half = lax.dynamic_index_in_dim(split, core, 1, keepdims=False).reshape(steps * half, width)
    other_half = lax.dynamic_index_in_dim(split, 1 - core, 1, keepdims=False).reshape(steps * half, width)
    block = jnp.concatenate([own_half, swap(other_half)], axis=1)

    table = table_slot.shape[0]
    ids = adapter_ids.reshape(count)
    slot = jnp.sum((ids[:, None] == jnp.arange(table, dtype=jnp.int32)) * table_slot, axis=1)
    holder = slot // (2 * held)
    earlier = jnp.arange(count)[:, None] > jnp.arange(count)
    order = jnp.sum((holder[:, None] == holder) & earlier, axis=1)
    local = (slot - me // 2 * (2 * held) - core * held) % (2 * held)
    per_chip = 2 * SLOTS

    shrink0 = shrink_table.reshape(held * rank, -1)
    expand0 = expand_table.reshape(held * rank, -1)
    shrink1, expand1 = swap(shrink0), swap(expand0)

    def exchange(value):
        return lax.all_to_all(value, "wide", split_axis=0, concat_axis=0, tiled=True)

    def round_of(index):
        rest = order - index * per_chip
        place = jnp.where((rest >= 0) & (rest < per_chip), holder * per_chip + rest, -1)
        pick = place == jnp.arange(wide * SLOTS)[:, None]
        pick = pick.astype(BF16)
        sent = jnp.dot(pick, features, preferred_element_type=F32).astype(BF16)
        rows = exchange(sent.reshape(wide, SLOTS, width))
        mine = place == (me * SLOTS + jnp.arange(SLOTS))[:, None]
        which = jnp.sum(jnp.where(mine, local + 1, 0), axis=1) - 1
        mask = (which[:, None] == jnp.arange(2 * held * rank) // rank).astype(F32)
        value = exchange(owner(rows, mask, shrink0, shrink1, expand0, expand1))
        return lax.dot_general(
            pick, value.reshape(wide * SLOTS, width), (((0,), (0,)), ((), ())), preferred_element_type=F32
        )

    adapter_out = round_of(0)

    weight1 = swap(base_weight)
    edge = block.shape[0] // 2
    blocks, whole, sources = [], [], []

    def add(source, *parts):
        whole.append(len(blocks))
        sources.append(source)
        blocks.extend(parts)

    shifts = list(range(chips // 4))
    columns = [block if k == 0 else move(block, shift(k)) for k in shifts]
    for k, column in zip(shifts, columns):
        source = (chip - 4 * k) % chips
        along_x = move(column, flip(1))
        along_y = move(column, flip(2))
        far0 = move(along_x[:edge], flip(2))
        far1 = move(along_y[edge:], flip(1))
        add(source, column)
        add(source ^ 1, along_x)
        add(source ^ 2, along_y)
        add(source ^ 3, far0, far1)
    places = jnp.stack([(2 * s + (core + side) % 2) * width for s in sources for side in range(2)])
    out0, out1 = base(places.astype(jnp.int32), blocks, tuple(whole), base_weight, weight1)
    got = swap(out1)

    rounds = (jnp.max(order) + per_chip) // per_chip
    if groups > 1:
        rounds = lax.pmax(rounds, "groups")
    _, adapter_out = lax.while_loop(
        lambda state: state[0] < rounds,
        lambda state: (state[0] + 1, state[1] + round_of(state[0])),
        (jnp.int32(1), adapter_out),
    )

    shape = (steps, half, width)
    a, b = out0.reshape(shape), got.reshape(shape)
    base_out = jnp.where(core == 0, jnp.stack([a, b], 1), jnp.stack([b, a], 1))
    result = base_out.reshape(count, width) + 2.0 * adapter_out
    return result.astype(BF16).reshape(steps, requests, width)


def solution(mesh):
    return jax.shard_map(
        functools.partial(body, mesh.shape["groups"]),
        mesh=mesh,
        in_specs=(
            P(None, "groups", "wide"),
            P("wide", None),
            P("wide", None, None),
            P("wide", None, None),
            P(),
            P(None, "groups"),
        ),
        out_specs=P(None, "groups", "wide"),
        check_vma=False,
    )
```

time: 246 us -> 99.9 us (0.41)
  local copies, waits for them, and re-layouts: 73.1 us -> 2.42 us
  waiting for transfers between devices: 86.1 us -> 38.4 us
  blocking collectives: 39.3 us -> 0 us
  starting transfers between devices: 11.7 us -> 38.5 us
  matrix products: 18.7 us -> 3.87 us
  between operations: 13.3 us -> 0.97 us
  Pallas kernels: 0 us -> 11.5 us
    all_to_all x2, waiting for transfers between devices: 84.6 us -> 15.2 us  [exchange(): lax.all_to_all(value, 'wide', split_axis=0, concat_axis=0, tiled=True)]
    unnamed x14 -> x8, local copies, waits for them, and re-layouts: 52.4 us -> 2.2 us
    psum x1 -> x0, blocking collectives: 39.3 us -> none  [body(): low_rank = lax.psum(partial_sum, 'wide').astype(jnp.bfloat16)]
    ppermute x0 -> x24, starting transfers between devices: none -> 28.2 us  [the longest x19 27.1 us: move(): return lax.ppermute(value, 'wide', pairs)]
    ppermute x0 -> x24, waiting for transfers between devices: none -> 23.2 us  [the longest x19 21.9 us: move(): return lax.ppermute(value, 'wide', pairs)]
    all_to_all x2 -> x0, local copies, waits for them, and re-layouts: 19.1 us -> none  [the longest x1 9.74 us: body(): lax.all_to_all(shrink_table, 'wide', split_axis=2, concat_axis=0, tiled=T...]
    dot_general x9 -> x2, matrix products: 18.7 us -> 3.87 us  [the longest x1 2.22 us: round_of(): sent = jnp.dot(pick, features, preferred_element_type=F32).astype(BF16)]
    pallas_call x0 -> x2, Pallas kernels: none -> 11.5 us  [the longest x1 6.4 us: owner(): pl.pallas_call(owner_kernel, out_shape=jax.ShapeDtypeStruct(rows.shape, B...]
  transfers between devices with their start and end apart: 5 -> 26, of which waited for: 2 -> 13; matrix products, arithmetic and copies ran while one was open for 35% -> 6% of each run, Pallas kernels for 0% -> 12%
where the time goes in v1:
time: 99.9 us; the launch traced here: 98.5 us
  starting transfers between devices  38.5 us (39%)
  waiting for transfers between devices  38.4 us (38%)
  Pallas kernels  11.5 us (12%)
  matrix products  3.87 us (4%)
  other arithmetic  2.79 us (3%)
  local copies, waits for them, and re-layouts  2.42 us (2%)
    ppermute x19, starting transfers between devices, move(): return lax.ppermute(value, 'wide', pairs)  27.1 us
    ppermute x19, waiting for transfers between devices, move(): return lax.ppermute(value, 'wide', pairs)  21.9 us
    all_to_all x2, waiting for transfers between devices, exchange(): lax.all_to_all(value, 'wide', split_axis=0, concat_axis=0, tiled=True)  15.2 us
    all_to_all x2, starting transfers between devices, exchange(): lax.all_to_all(value, 'wide', split_axis=0, concat_axis=0, tiled=True)  10.3 us
    pallas_call x1, Pallas kernels, owner(): pl.pallas_call(owner_kernel, out_shape=jax.ShapeDtypeStruct(rows.shape, B...  6.4 us
    pallas_call x1, Pallas kernels, base(): pl.pallas_call(functools.partial(base_kernel, whole), out_shape=(shape, s...  5.06 us
    dot_general x1, matrix products, round_of(): sent = jnp.dot(pick, features, preferred_element_type=F32).astype(BF16)  2.22 us
    unnamed x8, local copies, waits for them, and re-layouts  2.2 us
  transfers between devices with their start and end apart: 26, of which 13 were waited for; matrix products, arithmetic and copies ran while one was open for 6% of the time, Pallas kernels for 12%

profile of v1, /device:TPU:0, one launch (start us, length us, event | category | flops | bytes accessed | tf_op | source)
XLA Modules:
  0.0 98.5 jit_solution(6181972712362279514)
XLA Ops:
  0.0 0.5 collective-permute-start.20
  0.5 0.5 collective-permute-start.23
  1.0 0.8 select_reduce_fusion.1
  1.8 0.2 convert_reduce_fusion
  2.0 0.7 fusion.16
  2.7 2.2 %fusion.8 = bf16[1024,256]{1,0:T(8,128)(2,1)} fusion(bf16[384,256]{1,0:T(8,128)(2,1)} %bitcast.75, s32[384]{0:T(512)S(1)} %get-tuple-element.225), kind=kOutput, calls=%fused_computation.20 | convolution fusion | flops 201981952 | bytes 722432 | tf_op jit(solution)/shard_map/dot_general | solution.py:134
  4.9 7.0 %all-to-all-start.2 = ((bf16[32,32,256]{2,1,0:T(8,128)(2,1)}), bf16[32,32,256]{2,1,0:T(8,128)(2,1)S(1)}, u32[]{:S(2)}, u32[]{:S(2)}) async-start(bf16[32,32,256]{2,1,0:T(8,128)(2,1)} %bitcast.42), calls=%async_computation.2 | async-start | bytes 1048576 | tf_op jit(solution)/shard_map/all_to_all | solution.py:127
  11.9 0.2 select_reduce_fusion.2
  12.2 15.2 %all-to-all-done.2.rows_ref = bf16[32,32,256]{2,1,0:T(8,128)(2,1)S(1)} async-done(((bf16[32,32,256]{2,1,0:T(8,128)(2,1)}), bf16[32,32,256]{2,1,0:T(8,128)(2,1)S(1)}, u32[]{:S(2)}, u32[]{:S(2)}) %all-to-all-start.2) | async-done | bytes 524320 | tf_op jit(solution)/shard_map/all_to_all | solution.py:127
  27.5 6.4 %owner.6 = bf16[32,32,256]{2,1,0:T(8,128)(2,1)} custom-call(bf16[32,32,256]{2,1,0:T(8,128)(2,1)S(1)} %all-to-all-done.2.rows_ref, f32[32,256]{1,0:T(8,128)S(1)} %compare_convert_fusion.1.mask_ref, bf16[128,8192]{1,0:T(8,128)(2,1)} %bitcast.68, bf16[128,8192]{1,0:T(8,128)(2,1)} %collective-permute-done.22.s1_ref, bf16[128,8192]{1,0:T(8,128)(2,1)} %bitcast.71, ...), custom_call_target="tpu_custom_call" | custom-call | tf_op jit(solution)/shard_map/owner/pallas_call | solution.py:39
  33.9 3.3 %all-to-all-start.3 = ((bf16[32,32,256]{2,1,0:T(8,128)(2,1)}), bf16[32,32,256]{2,1,0:T(8,128)(2,1)}, u32[]{:S(2)}, u32[]{:S(2)}) async-start(bf16[32,32,256]{2,1,0:T(8,128)(2,1)} %owner.6), calls=%async_computation.3 | async-start | bytes 1048576 | tf_op jit(solution)/shard_map/all_to_all | solution.py:127
  37.2 0.1 collective-permute-start
  37.4 1.2 %collective-permute-done = bf16[192,256]{1,0:T(8,128)(2,1)S(1)} collective-permute-done((bf16[192,256]{1,0:T(8,128)(2,1)S(1)}, bf16[192,256]{1,0:T(8,128)(2,1)S(1)}, u32[]{:S(2)}, u32[]{:S(2)}) %collective-permute-start) | collective-permute-done | bytes 98336 | tf_op jit(solution)/shard_map/ppermute | solution.py:99
  38.6 1.6 %collective-permute-start.1 = (bf16[192,512]{1,0:T(8,128)(2,1)S(1)}, bf16[192,512]{1,0:T(8,128)(2,1)S(1)}, u32[]{:S(2)}, u32[]{:S(2)}) collective-permute-start(bf16[192,512]{1,0:T(8,128)(2,1)S(1)} %pad_maximum_fusion.refs_0_), channel_id=1, source_target_pairs={{0,2},{1,3},{2,0},{3,1},{4,6},{5,7},{6,4},{7,5},{8,10},{9,11},{10,... | collective-permute-start | bytes 589832 | tf_op jit(solution)/shard_map/ppermute | solution.py:96
  40.3 1.5 %collective-permute-start.5 = (bf16[192,512]{1,0:T(8,128)(2,1)S(1)}, bf16[192,512]{1,0:T(8,128)(2,1)S(1)}, u32[]{:S(2)}, u32[]{:S(2)}) collective-permute-start(bf16[192,512]{1,0:T(8,128)(2,1)S(1)} %pad_maximum_fusion.refs_0_), channel_id=1, source_target_pairs={{0,8},{1,9},{2,10},{3,11},{4,12},{5,13},{6,14},{7,15},{8,16},{9,17... | collective-permute-start | bytes 589832 | tf_op jit(solution)/shard_map/ppermute | solution.py:96
  41.8 1.5 %collective-permute-start.2 = (bf16[192,512]{1,0:T(8,128)(2,1)S(1)}, bf16[192,512]{1,0:T(8,128)(2,1)S(1)}, u32[]{:S(2)}, u32[]{:S(2)}) collective-permute-start(bf16[192,512]{1,0:T(8,128)(2,1)S(1)} %pad_maximum_fusion.refs_0_), channel_id=1, source_target_pairs={{0,4},{1,5},{2,6},{3,7},{4,0},{5,1},{6,2},{7,3},{8,12},{9,13},{10,... | collective-permute-start | bytes 589832 | tf_op jit(solution)/shard_map/ppermute | solution.py:96
  43.3 2.5 %collective-permute-start.10 = (bf16[192,512]{1,0:T(8,128)(2,1)S(1)}, bf16[192,512]{1,0:T(8,128)(2,1)S(1)}, u32[]{:S(2)}, u32[]{:S(2)}) collective-permute-start(bf16[192,512]{1,0:T(8,128)(2,1)S(1)} %pad_maximum_fusion.refs_0_), channel_id=1, source_target_pairs={{0,16},{1,17},{2,18},{3,19},{4,20},{5,21},{6,22},{7,23},{8,24},{9,... | collective-permute-start | bytes 589832 | tf_op jit(solution)/shard_map/ppermute | solution.py:96
  45.8 3.0 %collective-permute-done.1.refs_1_ = bf16[192,512]{1,0:T(8,128)(2,1)S(1)} collective-permute-done((bf16[192,512]{1,0:T(8,128)(2,1)S(1)}, bf16[192,512]{1,0:T(8,128)(2,1)S(1)}, u32[]{:S(2)}, u32[]{:S(2)}) %collective-permute-start.1) | collective-permute-done | bytes 196640 | tf_op jit(solution)/shard_map/ppermute | solution.py:96
  48.8 3.8 %collective-permute-start.15 = (bf16[192,512]{1,0:T(8,128)(2,1)S(1)}, bf16[192,512]{1,0:T(8,128)(2,1)S(1)}, u32[]{:S(2)}, u32[]{:S(2)}) collective-permute-start(bf16[192,512]{1,0:T(8,128)(2,1)S(1)} %pad_maximum_fusion.refs_0_), channel_id=1, source_target_pairs={{0,24},{1,25},{2,26},{3,27},{4,28},{5,29},{6,30},{7,31},{8,0},{9,1... | collective-permute-start | bytes 589832 | tf_op jit(solution)/shard_map/ppermute | solution.py:96
  52.6 2.3 %collective-permute-done.5.refs_5_ = bf16[192,512]{1,0:T(8,128)(2,1)S(1)} collective-permute-done((bf16[192,512]{1,0:T(8,128)(2,1)S(1)}, bf16[192,512]{1,0:T(8,128)(2,1)S(1)}, u32[]{:S(2)}, u32[]{:S(2)}) %collective-permute-start.5) | collective-permute-done | bytes 196640 | tf_op jit(solution)/shard_map/ppermute | solution.py:96
  54.9 1.5 %collective-permute-start.6 = (bf16[192,512]{1,0:T(8,128)(2,1)S(1)}, bf16[192,512]{1,0:T(8,128)(2,1)S(1)}, u32[]{:S(2)}, u32[]{:S(2)}) collective-permute-start(bf16[192,512]{1,0:T(8,128)(2,1)S(1)} %collective-permute-done.5.refs_5_), channel_id=1, source_target_pairs={{0,2},{1,3},{2,0},{3,1},{4,6},{5,7},{6,4},{7,5},{8,10},{9,11},{10,... | collective-permute-start | bytes 589832 | tf_op jit(solution)/shard_map/ppermute | solution.py:96
  56.4 1.5 %collective-permute-start.7 = (bf16[192,512]{1,0:T(8,128)(2,1)S(1)}, bf16[192,512]{1,0:T(8,128)(2,1)S(1)}, u32[]{:S(2)}, u32[]{:S(2)}) collective-permute-start(bf16[192,512]{1,0:T(8,128)(2,1)S(1)} %collective-permute-done.5.refs_5_), channel_id=1, source_target_pairs={{0,4},{1,5},{2,6},{3,7},{4,0},{5,1},{6,2},{7,3},{8,12},{9,13},{10,... | collective-permute-start | bytes 589832 | tf_op jit(solution)/shard_map/ppermute | solution.py:96
  57.9 7.3 %collective-permute-done.10.refs_10_ = bf16[192,512]{1,0:T(8,128)(2,1)S(1)} collective-permute-done((bf16[192,512]{1,0:T(8,128)(2,1)S(1)}, bf16[192,512]{1,0:T(8,128)(2,1)S(1)}, u32[]{:S(2)}, u32[]{:S(2)}) %collective-permute-start.10) | collective-permute-done | bytes 196640 | tf_op jit(solution)/shard_map/ppermute | solution.py:96
  65.2 1.5 %collective-permute-start.11 = (bf16[192,512]{1,0:T(8,128)(2,1)S(1)}, bf16[192,512]{1,0:T(8,128)(2,1)S(1)}, u32[]{:S(2)}, u32[]{:S(2)}) collective-permute-start(bf16[192,512]{1,0:T(8,128)(2,1)S(1)} %collective-permute-done.10.refs_10_), channel_id=1, source_target_pairs={{0,2},{1,3},{2,0},{3,1},{4,6},{5,7},{6,4},{7,5},{8,10},{9,11},{10,... | collective-permute-start | bytes 589832 | tf_op jit(solution)/shard_map/ppermute | solution.py:96
  66.6 1.5 %collective-permute-start.12 = (bf16[192,512]{1,0:T(8,128)(2,1)S(1)}, bf16[192,512]{1,0:T(8,128)(2,1)S(1)}, u32[]{:S(2)}, u32[]{:S(2)}) collective-permute-start(bf16[192,512]{1,0:T(8,128)(2,1)S(1)} %collective-permute-done.10.refs_10_), channel_id=1, source_target_pairs={{0,4},{1,5},{2,6},{3,7},{4,0},{5,1},{6,2},{7,3},{8,12},{9,13},{10,... | collective-permute-start | bytes 589832 | tf_op jit(solution)/shard_map/ppermute | solution.py:96
  68.1 0.5 collective-permute-start.16
  68.7 0.5 collective-permute-start.17
  69.3 3.6 %collective-permute-done.11.refs_11_ = bf16[192,512]{1,0:T(8,128)(2,1)S(1)} collective-permute-done((bf16[192,512]{1,0:T(8,128)(2,1)S(1)}, bf16[192,512]{1,0:T(8,128)(2,1)S(1)}, u32[]{:S(2)}, u32[]{:S(2)}) %collective-permute-start.11) | collective-permute-done | bytes 196640 | tf_op jit(solution)/shard_map/ppermute | solution.py:96
  72.9 1.6 %collective-permute-start.3 = (bf16[96,512]{1,0:T(8,128)(2,1)S(1)}, bf16[96,512]{1,0:T(8,128)(2,1)S(1)}, u32[]{:S(2)}, u32[]{:S(2)}) collective-permute-start(bf16[96,512]{1,0:T(8,128)(2,1)S(1)} %slice.32), channel_id=1, source_target_pairs={{0,4},{1,5},{2,6},{3,7},{4,0},{5,1},{6,2},{7,3},{8,12},{9,13},{10,... | collective-permute-start | bytes 294920 | tf_op jit(solution)/shard_map/ppermute | solution.py:96
  74.5 1.5 %collective-permute-start.4 = (bf16[96,512]{1,0:T(8,128)(2,1)S(1)}, bf16[96,512]{1,0:T(8,128)(2,1)S(1)}, u32[]{:S(2)}, u32[]{:S(2)}) collective-permute-start(bf16[96,512]{1,0:T(8,128)(2,1)S(1)} %slice.33), channel_id=1, source_target_pairs={{0,2},{1,3},{2,0},{3,1},{4,6},{5,7},{6,4},{7,5},{8,10},{9,11},{10,... | collective-permute-start | bytes 294920 | tf_op jit(solution)/shard_map/ppermute | solution.py:96
  76.0 0.4 collective-permute-done.16.refs_16_
  76.4 1.5 %collective-permute-start.8 = (bf16[96,512]{1,0:T(8,128)(2,1)S(1)}, bf16[96,512]{1,0:T(8,128)(2,1)S(1)}, u32[]{:S(2)}, u32[]{:S(2)}) collective-permute-start(bf16[96,512]{1,0:T(8,128)(2,1)S(1)} %slice.34), channel_id=1, source_target_pairs={{0,4},{1,5},{2,6},{3,7},{4,0},{5,1},{6,2},{7,3},{8,12},{9,13},{10,... | collective-permute-start | bytes 294920 | tf_op jit(solution)/shard_map/ppermute | solution.py:96
  77.9 0.8 collective-permute-done.17.refs_17_
  78.7 0.7 collective-permute-start.9
  79.4 0.7 collective-permute-done.3.refs_3_
  80.2 1.5 %collective-permute-start.13 = (bf16[96,512]{1,0:T(8,128)(2,1)S(1)}, bf16[96,512]{1,0:T(8,128)(2,1)S(1)}, u32[]{:S(2)}, u32[]{:S(2)}) collective-permute-start(bf16[96,512]{1,0:T(8,128)(2,1)S(1)} %slice.36), channel_id=1, source_target_pairs={{0,4},{1,5},{2,6},{3,7},{4,0},{5,1},{6,2},{7,3},{8,12},{9,13},{10,... | collective-permute-start | bytes 294920 | tf_op jit(solution)/shard_map/ppermute | solution.py:96
  81.6 0.7 collective-permute-start.14
  82.3 1.4 %collective-permute-start.18 = (bf16[96,512]{1,0:T(8,128)(2,1)S(1)}, bf16[96,512]{1,0:T(8,128)(2,1)S(1)}, u32[]{:S(2)}, u32[]{:S(2)}) collective-permute-start(bf16[96,512]{1,0:T(8,128)(2,1)S(1)} %slice.38), channel_id=1, source_target_pairs={{0,4},{1,5},{2,6},{3,7},{4,0},{5,1},{6,2},{7,3},{8,12},{9,13},{10,... | collective-permute-start | bytes 294920 | tf_op jit(solution)/shard_map/ppermute | solution.py:96
  83.7 0.3 collective-permute-done.9.refs_9_
  84.0 0.3 collective-permute-start.19
  85.0 0.1 stack.137.place_ref
  85.1 1.1 %collective-permute-done.14.refs_14_ = bf16[96,512]{1,0:T(8,128)(2,1)S(1)} collective-permute-done((bf16[96,512]{1,0:T(8,128)(2,1)S(1)}, bf16[96,512]{1,0:T(8,128)(2,1)S(1)}, u32[]{:S(2)}, u32[]{:S(2)}) %collective-permute-start.14) | collective-permute-done | bytes 98336 | tf_op jit(solution)/shard_map/ppermute | solution.py:96
  86.3 0.7 collective-permute-done.18.refs_18_
  86.9 1.7 %collective-permute-done.19.refs_19_ = bf16[96,512]{1,0:T(8,128)(2,1)S(1)} collective-permute-done((bf16[96,512]{1,0:T(8,128)(2,1)S(1)}, bf16[96,512]{1,0:T(8,128)(2,1)S(1)}, u32[]{:S(2)}, u32[]{:S(2)}) %collective-permute-start.19) | collective-permute-done | bytes 98336 | tf_op jit(solution)/shard_map/ppermute | solution.py:96
  88.6 2.2 %copy-done = bf16[256,8192]{1,0:T(8,128)(2,1)S(1)} copy-done((bf16[256,8192]{1,0:T(8,128)(2,1)S(1)}, bf16[256,8192]{1,0:T(8,128)(2,1)}, u32[]{:S(2)}) %copy-start) | copy-done | bytes 4194328
  90.8 5.1 %base.1 = (f32[192,256]{1,0:T(8,128)S(1)}, f32[192,256]{1,0:T(8,128)S(1)}) custom-call(s32[32]{0:T(128)S(1)} %stack.137.place_ref, bf16[192,512]{1,0:T(8,128)(2,1)S(1)} %pad_maximum_fusion.refs_0_, bf16[192,512]{1,0:T(8,128)(2,1)S(1)} %collective-permute-done.1.refs_1_, bf16[192,512]{1,0:T(8,128)(2,1)S(1)} %collective-permute-done.2.refs_2_, ...), custom_call_target="tpu_custom_call" | custom-call | tf_op jit(solution)/shard_map/base/pallas_call | solution.py:74
  96.0 1.7 %fusion.6 = f32[384,256]{1,0:T(8,128)S(1)} fusion(bf16[1024,256]{1,0:T(8,128)(2,1)} %bitcast.45, s32[384]{0:T(512)} %copy-done.3), kind=kOutput, calls=%fused_computation.18 | convolution fusion | flops 201719808 | bytes 919040 | tf_op jit(solution)/shard_map/dot_general | solution.py:140
  97.8 0.7 fusion.12
  (40 shorter events, 0.4 us)
Async XLA Ops:
  0.0 88.6 %collective-permute-start.20 = (bf16[256,8192]{1,0:T(8,128)(2,1)}, bf16[256,8192]{1,0:T(8,128)(2,1)}, u32[]{:S(2)}, u32[]{:S(2)}) collective-permute-start(bf16[256,8192]{1,0:T(8,128)(2,1)} %refs_20_.1), channel_id=1, source_target_pairs={{0,1},{1,0},{2,3},{3,2},{4,5},{5,4},{6,7},{7,6},{8,9},{9,8},{10,11... | collective-permute-start | bytes 12582920 | tf_op jit(solution)/shard_map/ppermute | solution.py:99
  0.5 27.0 %collective-permute-start.22 = (bf16[128,8192]{1,0:T(8,128)(2,1)}, bf16[128,8192]{1,0:T(8,128)(2,1)}, u32[]{:S(2)}, u32[]{:S(2)}) collective-permute-start(bf16[128,8192]{1,0:T(8,128)(2,1)} %bitcast.67), channel_id=1, source_target_pairs={{0,1},{1,0},{2,3},{3,2},{4,5},{5,4},{6,7},{7,6},{8,9},{9,8},{10,11... | collective-permute-start | bytes 6291464 | tf_op jit(solution)/shard_map/ppermute | solution.py:99
  0.5 26.9 %collective-permute-start.23 = (bf16[128,8192]{1,0:T(8,128)(2,1)}, bf16[128,8192]{1,0:T(8,128)(2,1)}, u32[]{:S(2)}, u32[]{:S(2)}) collective-permute-start(bf16[128,8192]{1,0:T(8,128)(2,1)} %bitcast.70), channel_id=1, source_target_pairs={{0,1},{1,0},{2,3},{3,2},{4,5},{5,4},{6,7},{7,6},{8,9},{9,8},{10,11... | collective-permute-start | bytes 6291464 | tf_op jit(solution)/shard_map/ppermute | solution.py:99
  2.7 31.1 %copy-start.3 = (s32[384]{0:T(512)}, s32[384]{0:T(512)S(1)}, u32[]{:S(2)}) copy-start(s32[384]{0:T(512)S(1)} %get-tuple-element.225) | copy-start | bytes 4612
  4.9 22.5 %all-to-all-start.2 = ((bf16[32,32,256]{2,1,0:T(8,128)(2,1)}), bf16[32,32,256]{2,1,0:T(8,128)(2,1)S(1)}, u32[]{:S(2)}, u32[]{:S(2)}) async-start(bf16[32,32,256]{2,1,0:T(8,128)(2,1)} %bitcast.42), calls=%async_computation.2 | async-start | bytes 1048576 | tf_op jit(solution)/shard_map/all_to_all | solution.py:127
  12.2 25.0 %copy-start.1 = (bf16[3,128,256]{2,1,0:T(8,128)(2,1)S(1)}, bf16[3,128,256]{2,1,0:T(8,128)(2,1)}, u32[]{:S(2)}) copy-start(bf16[3,128,256]{2,1,0:T(8,128)(2,1)} %param.8) | copy-start | bytes 589828
  33.9 62.1 %all-to-all-start.3 = ((bf16[32,32,256]{2,1,0:T(8,128)(2,1)}), bf16[32,32,256]{2,1,0:T(8,128)(2,1)}, u32[]{:S(2)}, u32[]{:S(2)}) async-start(bf16[32,32,256]{2,1,0:T(8,128)(2,1)} %owner.6), calls=%async_computation.3 | async-start | bytes 1048576 | tf_op jit(solution)/shard_map/all_to_all | solution.py:127
  37.2 1.4 %collective-permute-start = (bf16[192,256]{1,0:T(8,128)(2,1)S(1)}, bf16[192,256]{1,0:T(8,128)(2,1)S(1)}, u32[]{:S(2)}, u32[]{:S(2)}) collective-permute-start(bf16[192,256]{1,0:T(8,128)(2,1)S(1)} %bitcast.79), channel_id=1, source_target_pairs={{0,1},{1,0},{2,3},{3,2},{4,5},{5,4},{6,7},{7,6},{8,9},{9,8},{10,11... | collective-permute-start | bytes 294920 | tf_op jit(solution)/shard_map/ppermute | solution.py:99
  38.6 10.1 %collective-permute-start.1 = (bf16[192,512]{1,0:T(8,128)(2,1)S(1)}, bf16[192,512]{1,0:T(8,128)(2,1)S(1)}, u32[]{:S(2)}, u32[]{:S(2)}) collective-permute-start(bf16[192,512]{1,0:T(8,128)(2,1)S(1)} %pad_maximum_fusion.refs_0_), channel_id=1, source_target_pairs={{0,2},{1,3},{2,0},{3,1},{4,6},{5,7},{6,4},{7,5},{8,10},{9,11},{10,... | collective-permute-start | bytes 589832 | tf_op jit(solution)/shard_map/ppermute | solution.py:96
  40.3 14.6 %collective-permute-start.5 = (bf16[192,512]{1,0:T(8,128)(2,1)S(1)}, bf16[192,512]{1,0:T(8,128)(2,1)S(1)}, u32[]{:S(2)}, u32[]{:S(2)}) collective-permute-start(bf16[192,512]{1,0:T(8,128)(2,1)S(1)} %pad_maximum_fusion.refs_0_), channel_id=1, source_target_pairs={{0,8},{1,9},{2,10},{3,11},{4,12},{5,13},{6,14},{7,15},{8,16},{9,17... | collective-permute-start | bytes 589832 | tf_op jit(solution)/shard_map/ppermute | solution.py:96
  41.8 14.6 %collective-permute-start.2 = (bf16[192,512]{1,0:T(8,128)(2,1)S(1)}, bf16[192,512]{1,0:T(8,128)(2,1)S(1)}, u32[]{:S(2)}, u32[]{:S(2)}) collective-permute-start(bf16[192,512]{1,0:T(8,128)(2,1)S(1)} %pad_maximum_fusion.refs_0_), channel_id=1, source_target_pairs={{0,4},{1,5},{2,6},{3,7},{4,0},{5,1},{6,2},{7,3},{8,12},{9,13},{10,... | collective-permute-start | bytes 589832 | tf_op jit(solution)/shard_map/ppermute | solution.py:96
  43.3 21.9 %collective-permute-start.10 = (bf16[192,512]{1,0:T(8,128)(2,1)S(1)}, bf16[192,512]{1,0:T(8,128)(2,1)S(1)}, u32[]{:S(2)}, u32[]{:S(2)}) collective-permute-start(bf16[192,512]{1,0:T(8,128)(2,1)S(1)} %pad_maximum_fusion.refs_0_), channel_id=1, source_target_pairs={{0,16},{1,17},{2,18},{3,19},{4,20},{5,21},{6,22},{7,23},{8,24},{9,... | collective-permute-start | bytes 589832 | tf_op jit(solution)/shard_map/ppermute | solution.py:96
  48.8 17.9 %collective-permute-start.15 = (bf16[192,512]{1,0:T(8,128)(2,1)S(1)}, bf16[192,512]{1,0:T(8,128)(2,1)S(1)}, u32[]{:S(2)}, u32[]{:S(2)}) collective-permute-start(bf16[192,512]{1,0:T(8,128)(2,1)S(1)} %pad_maximum_fusion.refs_0_), channel_id=1, source_target_pairs={{0,24},{1,25},{2,26},{3,27},{4,28},{5,29},{6,30},{7,31},{8,0},{9,1... | collective-permute-start | bytes 589832 | tf_op jit(solution)/shard_map/ppermute | solution.py:96
  54.9 13.2 %collective-permute-start.6 = (bf16[192,512]{1,0:T(8,128)(2,1)S(1)}, bf16[192,512]{1,0:T(8,128)(2,1)S(1)}, u32[]{:S(2)}, u32[]{:S(2)}) collective-permute-start(bf16[192,512]{1,0:T(8,128)(2,1)S(1)} %collective-permute-done.5.refs_5_), channel_id=1, source_target_pairs={{0,2},{1,3},{2,0},{3,1},{4,6},{5,7},{6,4},{7,5},{8,10},{9,11},{10,... | collective-permute-start | bytes 589832 | tf_op jit(solution)/shard_map/ppermute | solution.py:96
  56.4 12.3 %collective-permute-start.7 = (bf16[192,512]{1,0:T(8,128)(2,1)S(1)}, bf16[192,512]{1,0:T(8,128)(2,1)S(1)}, u32[]{:S(2)}, u32[]{:S(2)}) collective-permute-start(bf16[192,512]{1,0:T(8,128)(2,1)S(1)} %collective-permute-done.5.refs_5_), channel_id=1, source_target_pairs={{0,4},{1,5},{2,6},{3,7},{4,0},{5,1},{6,2},{7,3},{8,12},{9,13},{10,... | collective-permute-start | bytes 589832 | tf_op jit(solution)/shard_map/ppermute | solution.py:96
  65.2 7.8 %collective-permute-start.11 = (bf16[192,512]{1,0:T(8,128)(2,1)S(1)}, bf16[192,512]{1,0:T(8,128)(2,1)S(1)}, u32[]{:S(2)}, u32[]{:S(2)}) collective-permute-start(bf16[192,512]{1,0:T(8,128)(2,1)S(1)} %collective-permute-done.10.refs_10_), channel_id=1, source_target_pairs={{0,2},{1,3},{2,0},{3,1},{4,6},{5,7},{6,4},{7,5},{8,10},{9,11},{10,... | collective-permute-start | bytes 589832 | tf_op jit(solution)/shard_map/ppermute | solution.py:96
  66.6 7.9 %collective-permute-start.12 = (bf16[192,512]{1,0:T(8,128)(2,1)S(1)}, bf16[192,512]{1,0:T(8,128)(2,1)S(1)}, u32[]{:S(2)}, u32[]{:S(2)}) collective-permute-start(bf16[192,512]{1,0:T(8,128)(2,1)S(1)} %collective-permute-done.10.refs_10_), channel_id=1, source_target_pairs={{0,4},{1,5},{2,6},{3,7},{4,0},{5,1},{6,2},{7,3},{8,12},{9,13},{10,... | collective-permute-start | bytes 589832 | tf_op jit(solution)/shard_map/ppermute | solution.py:96
  68.1 8.3 %collective-permute-start.16 = (bf16[192,512]{1,0:T(8,128)(2,1)S(1)}, bf16[192,512]{1,0:T(8,128)(2,1)S(1)}, u32[]{:S(2)}, u32[]{:S(2)}) collective-permute-start(bf16[192,512]{1,0:T(8,128)(2,1)S(1)} %collective-permute-done.15.refs_15_), channel_id=1, source_target_pairs={{0,2},{1,3},{2,0},{3,1},{4,6},{5,7},{6,4},{7,5},{8,10},{9,11},{10,... | collective-permute-start | bytes 589832 | tf_op jit(solution)/shard_map/ppermute | solution.py:96
  68.7 10.0 %collective-permute-start.17 = (bf16[192,512]{1,0:T(8,128)(2,1)S(1)}, bf16[192,512]{1,0:T(8,128)(2,1)S(1)}, u32[]{:S(2)}, u32[]{:S(2)}) collective-permute-start(bf16[192,512]{1,0:T(8,128)(2,1)S(1)} %collective-permute-done.15.refs_15_), channel_id=1, source_target_pairs={{0,4},{1,5},{2,6},{3,7},{4,0},{5,1},{6,2},{7,3},{8,12},{9,13},{10,... | collective-permute-start | bytes 589832 | tf_op jit(solution)/shard_map/ppermute | solution.py:96
  72.9 7.2 %collective-permute-start.3 = (bf16[96,512]{1,0:T(8,128)(2,1)S(1)}, bf16[96,512]{1,0:T(8,128)(2,1)S(1)}, u32[]{:S(2)}, u32[]{:S(2)}) collective-permute-start(bf16[96,512]{1,0:T(8,128)(2,1)S(1)} %slice.32), channel_id=1, source_target_pairs={{0,4},{1,5},{2,6},{3,7},{4,0},{5,1},{6,2},{7,3},{8,12},{9,13},{10,... | collective-permute-start | bytes 294920 | tf_op jit(solution)/shard_map/ppermute | solution.py:96
  74.5 7.1 %collective-permute-start.4 = (bf16[96,512]{1,0:T(8,128)(2,1)S(1)}, bf16[96,512]{1,0:T(8,128)(2,1)S(1)}, u32[]{:S(2)}, u32[]{:S(2)}) collective-permute-start(bf16[96,512]{1,0:T(8,128)(2,1)S(1)} %slice.33), channel_id=1, source_target_pairs={{0,2},{1,3},{2,0},{3,1},{4,6},{5,7},{6,4},{7,5},{8,10},{9,11},{10,... | collective-permute-start | bytes 294920 | tf_op jit(solution)/shard_map/ppermute | solution.py:96
  76.4 5.9 %collective-permute-start.8 = (bf16[96,512]{1,0:T(8,128)(2,1)S(1)}, bf16[96,512]{1,0:T(8,128)(2,1)S(1)}, u32[]{:S(2)}, u32[]{:S(2)}) collective-permute-start(bf16[96,512]{1,0:T(8,128)(2,1)S(1)} %slice.34), channel_id=1, source_target_pairs={{0,4},{1,5},{2,6},{3,7},{4,0},{5,1},{6,2},{7,3},{8,12},{9,13},{10,... | collective-permute-start | bytes 294920 | tf_op jit(solution)/shard_map/ppermute | solution.py:96
  78.7 5.3 %collective-permute-start.9 = (bf16[96,512]{1,0:T(8,128)(2,1)S(1)}, bf16[96,512]{1,0:T(8,128)(2,1)S(1)}, u32[]{:S(2)}, u32[]{:S(2)}) collective-permute-start(bf16[96,512]{1,0:T(8,128)(2,1)S(1)} %slice.35), channel_id=1, source_target_pairs={{0,2},{1,3},{2,0},{3,1},{4,6},{5,7},{6,4},{7,5},{8,10},{9,11},{10,... | collective-permute-start | bytes 294920 | tf_op jit(solution)/shard_map/ppermute | solution.py:96
  80.2 5.0 %collective-permute-start.13 = (bf16[96,512]{1,0:T(8,128)(2,1)S(1)}, bf16[96,512]{1,0:T(8,128)(2,1)S(1)}, u32[]{:S(2)}, u32[]{:S(2)}) collective-permute-start(bf16[96,512]{1,0:T(8,128)(2,1)S(1)} %slice.36), channel_id=1, source_target_pairs={{0,4},{1,5},{2,6},{3,7},{4,0},{5,1},{6,2},{7,3},{8,12},{9,13},{10,... | collective-permute-start | bytes 294920 | tf_op jit(solution)/shard_map/ppermute | solution.py:96
  81.6 4.6 %collective-permute-start.14 = (bf16[96,512]{1,0:T(8,128)(2,1)S(1)}, bf16[96,512]{1,0:T(8,128)(2,1)S(1)}, u32[]{:S(2)}, u32[]{:S(2)}) collective-permute-start(bf16[96,512]{1,0:T(8,128)(2,1)S(1)} %slice.37), channel_id=1, source_target_pairs={{0,2},{1,3},{2,0},{3,1},{4,6},{5,7},{6,4},{7,5},{8,10},{9,11},{10,... | collective-permute-start | bytes 294920 | tf_op jit(solution)/shard_map/ppermute | solution.py:96
  82.3 4.6 %collective-permute-start.18 = (bf16[96,512]{1,0:T(8,128)(2,1)S(1)}, bf16[96,512]{1,0:T(8,128)(2,1)S(1)}, u32[]{:S(2)}, u32[]{:S(2)}) collective-permute-start(bf16[96,512]{1,0:T(8,128)(2,1)S(1)} %slice.38), channel_id=1, source_target_pairs={{0,4},{1,5},{2,6},{3,7},{4,0},{5,1},{6,2},{7,3},{8,12},{9,13},{10,... | collective-permute-start | bytes 294920 | tf_op jit(solution)/shard_map/ppermute | solution.py:96
  84.0 4.6 %collective-permute-start.19 = (bf16[96,512]{1,0:T(8,128)(2,1)S(1)}, bf16[96,512]{1,0:T(8,128)(2,1)S(1)}, u32[]{:S(2)}, u32[]{:S(2)}) collective-permute-start(bf16[96,512]{1,0:T(8,128)(2,1)S(1)} %slice.39), channel_id=1, source_target_pairs={{0,2},{1,3},{2,0},{3,1},{4,6},{5,7},{6,4},{7,5},{8,10},{9,11},{10,... | collective-permute-start | bytes 294920 | tf_op jit(solution)/shard_map/ppermute | solution.py:96
  88.6 2.2 %copy-start = (bf16[256,8192]{1,0:T(8,128)(2,1)S(1)}, bf16[256,8192]{1,0:T(8,128)(2,1)}, u32[]{:S(2)}) copy-start(bf16[256,8192]{1,0:T(8,128)(2,1)} %refs_20_.1) | copy-start | bytes 12582916
  95.9 1.8 %copy-start.2 = (bf16[3,128,256]{2,1,0:T(8,128)(2,1)S(1)}, bf16[3,128,256]{2,1,0:T(8,128)(2,1)}, u32[]{:S(2)}) copy-start(bf16[3,128,256]{2,1,0:T(8,128)(2,1)} %param.8) | copy-start | bytes 589828
  95.9 1.8 %collective-permute-start.21 = (f32[192,256]{1,0:T(8,128)S(1)}, f32[192,256]{1,0:T(8,128)S(1)}, u32[]{:S(2)}, u32[]{:S(2)}) collective-permute-start(f32[192,256]{1,0:T(8,128)S(1)} %get-tuple-element.194), channel_id=1, source_target_pairs={{0,1},{1,0},{2,3},{3,2},{4,5},{5,4},{6,7},{7,6},{8,9},{9,8},{10,11... | collective-permute-start | bytes 589832 | tf_op jit(solution)/shard_map/ppermute | solution.py:99

commit v2 on v0

v2 whole, which is shorter than its diff:
```python
import functools

import jax
import jax.numpy as jnp
from jax import lax
from jax.experimental import pallas as pl
from jax.experimental.pallas import tpu as pltpu
from jax.sharding import PartitionSpec as P

SLOTS = 32
LIMIT = 40 << 20
NT = (((1,), (1,)), ((), ()))
F32 = jnp.float32
BF16 = jnp.bfloat16
HBM = pl.BlockSpec(memory_space=pl.ANY)
VMEM = pl.BlockSpec(memory_space=pltpu.VMEM)
SMEM = pl.BlockSpec(memory_space=pltpu.SMEM)


def take(place_ref, blocks, tables, totals, packed=None):
    rows = totals[0].shape[0]
    for part, block in enumerate(blocks):
        if packed is not None:
            packed[part * rows : (part + 1) * rows, :] = block
        width = block.shape[1]
        columns = pl.ds(pl.multiple_of(place_ref[part], width), width)
        totals = [
            total + lax.dot_general(block, table[:, columns], NT, preferred_element_type=F32)
            for total, table in zip(totals, tables)
        ]
    return totals


def parts_of(refs, whole, rows):
    parts = []
    for index in whole:
        part = refs[index][...]
        if part.shape[0] != rows:
            part = jnp.concatenate([part, refs[index + 1][...]], axis=0)
        parts.append(part)
    return parts


def first_kernel(whole, place_ref, *refs):
    *blocks, t0_ref, t1_ref, out0_ref, out1_ref, packed_ref = refs
    parts = parts_of(blocks, whole, out0_ref.shape[0])
    totals = [jnp.zeros(out0_ref.shape, F32), jnp.zeros(out1_ref.shape, F32)]
    out0_ref[...], out1_ref[...] = take(place_ref, parts, (t0_ref, t1_ref), totals, packed_ref)


def first(places, blocks, whole, tables):
    rows, width = blocks[0].shape
    shape = jax.ShapeDtypeStruct((rows, tables[0].shape[0]), F32)
    return pl.pallas_call(
        functools.partial(first_kernel, whole),
        out_shape=(shape, shape, jax.ShapeDtypeStruct((len(whole) * rows, width), BF16)),
        in_specs=[SMEM] + [VMEM] * (len(blocks) + 2),
        out_specs=(VMEM,) * 3,
        compiler_params=pltpu.CompilerParams(vmem_limit_bytes=LIMIT),
        name="first",
    )(places, *blocks, *tables)


def base_kernel(place_ref, *refs):
    *packs, table_ref, out_ref = refs
    rows = out_ref.shape[0]
    parts = [pack[start : start + rows, :] for pack in packs for start in range(0, pack.shape[0], rows)]
    (out_ref[...],) = take(place_ref, parts, (table_ref,), [jnp.zeros(out_ref.shape, F32)])


def base(places, packs, table, rows, name):
    return pl.pallas_call(
        base_kernel,
        out_shape=jax.ShapeDtypeStruct((rows, table.shape[0]), F32),
        in_specs=[SMEM] + [VMEM] * (len(packs) + 1),
        out_specs=VMEM,
        compiler_params=pltpu.CompilerParams(vmem_limit_bytes=LIMIT),
        name=name,
    )(places, *packs, table)


def expand_rows(pick, lows, tables, out_ref):
    lows = [jnp.dot(pick, low, preferred_element_type=F32).astype(BF16) for low in lows]
    width = out_ref.shape[2]
    for part in range(out_ref.shape[0]):
        columns = slice(part * width, (part + 1) * width)
        value = jnp.dot(lows[0], tables[0][:, columns], preferred_element_type=F32)
        value += jnp.dot(lows[1], tables[1][:, columns], preferred_element_type=F32)
        out_ref[part] = value.astype(BF16)


def owner_kernel(whole, place_ref, *refs):
    *blocks, a0_ref, a1_ref, mask_ref, pick_ref, s0_ref, s1_ref, e0_ref, e1_ref = refs[:-5]
    out_ref, low_ref, packed_ref, given, sem = refs[-5:]
    rows, half = a0_ref.shape
    parts = parts_of(blocks, whole, rows)
    totals = take(place_ref, parts, (s0_ref, s1_ref), [a0_ref[...], a1_ref[...]], packed_ref)
    lows = []
    for side, total in enumerate(totals):
        columns = slice(side * half, (side + 1) * half)
        lows.append((total * mask_ref[:, columns]).astype(BF16))
        low_ref[:, columns] = lows[side]
    expand_rows(pick_ref[...], lows, (e0_ref, e1_ref), given)
    copy = pltpu.make_async_copy(given, out_ref, sem)
    copy.start()
    copy.wait()


def owner(places, blocks, whole, before, mask, pick, tables, out_shape):
    rows, width = mask.shape[0], blocks[-1].shape[1]
    return pl.pallas_call(
        functools.partial(owner_kernel, whole),
        out_shape=(
            jax.ShapeDtypeStruct(out_shape, BF16),
            jax.ShapeDtypeStruct(mask.shape, BF16),
            jax.ShapeDtypeStruct((len(whole) * rows, width), BF16),
        ),
        in_specs=[SMEM] + [VMEM] * (len(blocks) + 8),
        out_specs=(HBM, VMEM, VMEM),
        scratch_shapes=[pltpu.VMEM(out_shape, BF16), pltpu.SemaphoreType.DMA],
        compiler_params=pltpu.CompilerParams(vmem_limit_bytes=LIMIT),
        name="owner",
    )(places, *blocks, *before, mask, pick, *tables)


def again_kernel(pick_ref, low_ref, e0_ref, e1_ref, out_ref):
    half = e0_ref.shape[0]
    lows = [low_ref[:, :half], low_ref[:, half:]]
    expand_rows(pick_ref[...], lows, (e0_ref, e1_ref), out_ref)


def again(pick, low, e0, e1, out_shape):
    return pl.pallas_call(
        again_kernel,
        out_shape=jax.ShapeDtypeStruct(out_shape, BF16),
        in_specs=[VMEM] * 4,
        out_specs=VMEM,
        compiler_params=pltpu.CompilerParams(vmem_limit_bytes=LIMIT),
        name="again",
    )(pick, low, e0, e1)


def body(groups, inputs, base_weight, shrink_table, expand_table, table_slot, adapter_ids):
    wide = lax.axis_size("wide")
    me = lax.axis_index("wide")
    core, chip = me % 2, me // 2
    chips = wide // 2
    steps, requests, width = inputs.shape
    count = steps * requests
    held, rank, _ = shrink_table.shape

    def move(value, target):
        pairs = [(2 * c + k, 2 * target(c) + k) for c in range(chips) for k in range(2)]
        return lax.ppermute(value, "wide", pairs)

    def swap(value):
        return lax.ppermute(value, "wide", [(i, i ^ 1) for i in range(wide)])

    def after(value, *done):
        return lax.optimization_barrier((value, *done))[0]

    def flip(bits):
        return lambda c: c ^ bits

    def shift(k):
        return lambda c: (c + 4 * k) % chips

    half = requests // 2
    rows = steps * half
    split = inputs.reshape(steps, 2, half, width)
    own_half = lax.dynamic_index_in_dim(split, core, 1, keepdims=False).reshape(rows, width)
    other_half = lax.dynamic_index_in_dim(split, 1 - core, 1, keepdims=False).reshape(rows, width)
    got_half = swap(other_half)
    block = jnp.where(
        core == 0,
        jnp.concatenate([own_half, got_half], axis=1),
        jnp.concatenate([got_half, own_half], axis=1),
    )

    shrink0 = shrink_table.reshape(held * rank, -1)
    expand0 = expand_table.reshape(held * rank, -1)
    shrink1, expand1 = swap(after(shrink0, block)), swap(after(expand0, block))

    depth = chips // 4
    shifts = [0] + sorted(range(1, depth), key=lambda k: min(k, depth - k))
    edge = rows // 2
    x, y, far, z = {}, {}, {}, {0: block}

    def gather(some):
        blocks, whole, sources = [], [], []
        for k, bits in some:
            parts = far[k] if bits == 3 else ((z, x, y)[bits][k],)
            whole.append(len(blocks))
            sources.append(((chip - 4 * k) % chips) ^ bits)
            blocks.extend(parts)
        return (jnp.stack(sources) * (2 * width)).astype(jnp.int32), blocks, tuple(whole)

    x[0], y[0] = move(block, flip(1)), move(block, flip(2))
    for k in sorted(shifts[1:]):
        if k == 1:
            source = block
        elif k == depth - 1:
            source = after(block, shrink1, expand1)
        else:
            source = z[k - 1]
        z[k] = move(source, shift(k if k == depth - 1 else 1))
    far[0] = (move(after(x[0], y[0]), flip(2)),)
    for number, k in enumerate(shifts[1:], 1):
        ready = z[k]
        if number == 1:
            ready = after(ready, x[0], y[0])
        if number == depth - 1:
            ready = after(ready, far[0][0], x[1])
        x[k], y[k] = move(ready, flip(1)), move(ready, flip(2))
        if number < depth - 1:
            far[k] = (move(x[k], flip(2)) if number % 2 == 0 else move(y[k], flip(1)),)
    last = shifts[-1]
    early = [(k, bits) for k in shifts[:-3] for bits in range(4)] + [(shifts[-3], bits) for bits in range(3)]
    *sums, packed0 = first(*gather(early), (shrink0, shrink1))
    far[last] = (
        move(x[last][:edge], flip(2)),
        move(y[last][edge:], flip(1)),
    )
    tail = [(shifts[-3], 3)] + [(k, bits) for k in shifts[-2:] for bits in range(4)]

    table = table_slot.shape[0]
    ids = adapter_ids.reshape(count)
    slot = jnp.sum((ids[:, None] == jnp.arange(table, dtype=jnp.int32)) * table_slot, axis=1)
    side = jnp.arange(count) % requests // half
    holder = slot // (2 * held) * 2 + side
    earlier = jnp.arange(count)[:, None] > jnp.arange(count)
    order = jnp.sum((holder[:, None] == holder) & earlier, axis=1)
    here = lax.dynamic_index_in_dim(
        jnp.stack([slot, holder, order]).reshape(3, steps, 2, half), core, 2, keepdims=False
    ).reshape(3, rows)
    local = (here[0] - core * held) % (2 * held)
    mask = (local[:, None] == jnp.arange(2 * held * rank) // rank).astype(F32)
    chosen = jnp.where(here[1] == me, here[2], -1)

    def pick_of(index):
        return (chosen == (index * SLOTS + jnp.arange(SLOTS))[:, None]).astype(BF16)

    def give_back(sent, index):
        value = lax.all_to_all(sent, "wide", split_axis=0, concat_axis=0, tiled=True)
        rest = order - index * SLOTS
        place = jnp.where((rest >= 0) & (rest < SLOTS), holder * SLOTS + rest, -1)
        spread = (place[:, None] == jnp.arange(wide * SLOTS)).astype(BF16)
        return jnp.dot(spread, value.reshape(wide * SLOTS, width), preferred_element_type=F32)

    out_shape = (wide, SLOTS, width)
    sent, low, packed1 = owner(
        *gather(tail), sums, mask, pick_of(0), (shrink0, shrink1, expand0, expand1), out_shape
    )
    adapter_out = give_back(sent, 0)
    weight1 = swap(after(base_weight, low))
    places = gather(early + tail)[0]
    out0 = base(places, (packed0, packed1), base_weight, rows, "base")
    out1 = base(places, (packed0, packed1), weight1, rows, "other")
    got = swap(out1)

    rounds = jnp.max(order) // SLOTS + 1
    if groups > 1:
        rounds = lax.pmax(rounds, "groups")
    _, adapter_out = lax.while_loop(
        lambda state: state[0] < rounds,
        lambda state: (
            state[0] + 1,
            state[1] + give_back(again(pick_of(state[0]), low, expand0, expand1, out_shape), state[0]),
        ),
        (jnp.int32(1), adapter_out),
    )

    shape = (steps, half, width)
    a, b = out0.reshape(shape), got.reshape(shape)
    base_out = jnp.where(core == 0, jnp.stack([a, b], 1), jnp.stack([b, a], 1))
    result = base_out.reshape(count, width) + 2.0 * adapter_out
    return result.astype(BF16).reshape(steps, requests, width)


def solution(mesh):
    return jax.shard_map(
        functools.partial(body, mesh.shape["groups"]),
        mesh=mesh,
        in_specs=(
            P(None, "groups", "wide"),
            P("wide", None),
            P("wide", None, None),
            P("wide", None, None),
            P(),
            P(None, "groups"),
        ),
        out_specs=P(None, "groups", "wide"),
        check_vma=False,
    )
```

time: 246 us -> 75.6 us (0.31)
  waiting for transfers between devices: 86.1 us -> 17.8 us
  local copies, waits for them, and re-layouts: 73.1 us -> 7.8 us
  blocking collectives: 39.3 us -> 0 us
  matrix products: 18.7 us -> 2.23 us
  starting transfers between devices: 11.7 us -> 26.9 us
  Pallas kernels: 0 us -> 13.8 us
  between operations: 13.3 us -> 2.83 us
  other arithmetic: 1.04 us -> 3.69 us
    all_to_all x2 -> x1, waiting for transfers between devices: 84.6 us -> 2.29 us  [give_back(): lax.all_to_all(sent, 'wide', split_axis=0, concat_axis=0, tiled=True)]
    unnamed x14 -> x20, local copies, waits for them, and re-layouts: 52.4 us -> 6.2 us
    psum x1 -> x0, blocking collectives: 39.3 us -> none  [body(): low_rank = lax.psum(partial_sum, 'wide').astype(jnp.bfloat16)]
    ppermute x0 -> x21, starting transfers between devices: none -> 23.1 us  [the longest x16 21.9 us: move(): return lax.ppermute(value, 'wide', pairs)]
    all_to_all x2 -> x0, local copies, waits for them, and re-layouts: 19.1 us -> none  [the longest x1 9.74 us: body(): lax.all_to_all(shrink_table, 'wide', split_axis=2, concat_axis=0, tiled=T...]
    dot_general x9 -> x1, matrix products: 18.7 us -> 2.23 us  [give_back(): jnp.dot(spread, value.reshape(wide * SLOTS, width), preferred_element_typ...]
    ppermute x0 -> x21, waiting for transfers between devices: none -> 15.5 us  [the longest x16 14.6 us: move(): return lax.ppermute(value, 'wide', pairs)]
    pallas_call x0 -> x4, Pallas kernels: none -> 13.8 us  [the longest x2 8.21 us: base(): pl.pallas_call(base_kernel, out_shape=jax.ShapeDtypeStruct((rows, table.s...]
  transfers between devices with their start and end apart: 5 -> 22, of which waited for: 2 -> 8; matrix products, arithmetic and copies ran while one was open for 35% -> 6% of each run, Pallas kernels for 0% -> 13%
where the time goes in v2:
time: 75.6 us; the launch traced here: 75 us
  starting transfers between devices  26.9 us (36%)
  waiting for transfers between devices  17.8 us (24%)
  Pallas kernels  13.8 us (18%)
  local copies, waits for them, and re-layouts  7.8 us (10%)
  other arithmetic  3.69 us (5%)
  between operations  2.83 us (4%)
  matrix products  2.23 us (3%)
    ppermute x16, starting transfers between devices, move(): return lax.ppermute(value, 'wide', pairs)  21.9 us
    ppermute x16, waiting for transfers between devices, move(): return lax.ppermute(value, 'wide', pairs)  14.6 us
    pallas_call x2, Pallas kernels, base(): pl.pallas_call(base_kernel, out_shape=jax.ShapeDtypeStruct((rows, table.s...  8.21 us
    unnamed x20, local copies, waits for them, and re-layouts  6.2 us
    pallas_call x1, Pallas kernels, owner(): pl.pallas_call(functools.partial(owner_kernel, whole), out_shape=(jax.Sha...  4.16 us
    all_to_all x1, starting transfers between devices, give_back(): lax.all_to_all(sent, 'wide', split_axis=0, concat_axis=0, tiled=True)  3.73 us
    all_to_all x1, waiting for transfers between devices, give_back(): lax.all_to_all(sent, 'wide', split_axis=0, concat_axis=0, tiled=True)  2.29 us
    dot_general x1, matrix products, give_back(): jnp.dot(spread, value.reshape(wide * SLOTS, width), preferred_element_typ...  2.23 us
  transfers between devices with their start and end apart: 22, of which 8 were waited for; matrix products, arithmetic and copies ran while one was open for 6% of the time, Pallas kernels for 13%

profile of v2, /device:TPU:0, one launch (start us, length us, event | category | flops | bytes accessed | tf_op | source)
XLA Modules:
  0.0 75.0 jit_solution(5726488736875309567)
XLA Ops:
  0.0 1.0 %constant_dynamic-slice_fusion.1 = (bf16[3,1,64,256]{3,2,1,0:T(8,128)(2,1)S(1)}, bf16[3,1,64,256]{3,2,1,0:T(8,128)(2,1)S(1)}) fusion(bf16[3,2,64,256]{3,2,1,0:T(8,128)(2,1)} %bitcast.50, s32[]{:T(128)S(6)} %select_n.243, s32[]{:T(128)S(6)} %select_n.244), kind=kLoop, calls=%fused_computation.75 | loop fusion | bytes 393224 | tf_op jit(solution)/shard_map/jit(dynamic_index_in_dim)/dynamic_slice | solution.py:171
  1.0 0.5 collective-permute-start
  1.5 0.9 %collective-permute-done = bf16[192,256]{1,0:T(8,128)(2,1)S(1)} collective-permute-done((bf16[192,256]{1,0:T(8,128)(2,1)S(1)}, bf16[192,256]{1,0:T(8,128)(2,1)S(1)}, u32[]{:S(2)}, u32[]{:S(2)}) %collective-permute-start) | collective-permute-done | bytes 98336 | tf_op jit(solution)/shard_map/ppermute | solution.py:157
  2.5 0.4 collective-permute-start.7
  2.9 0.2 collective-permute-start.9
  3.1 0.8 %select_reduce_fusion = s32[384]{0:T(512)S(1)} fusion(s32[64]{0:T(128)} %param.12, s32[384]{0:T(512)} %bitcast.53), kind=kLoop, calls=%fused_computation.18 | loop fusion | flops 73344 | bytes 3328 | tf_op jit(solution)/shard_map/reduce_sum | solution.py:228
  3.9 0.1 stack.108
  4.0 0.2 convert_reduce_fusion
  4.2 0.1 stack.109
  4.7 3.0 %collective-permute-start.4 = (bf16[192,512]{1,0:T(8,128)(2,1)S(1)}, bf16[192,512]{1,0:T(8,128)(2,1)S(1)}, u32[]{:S(2)}, u32[]{:S(2)}) collective-permute-start(bf16[192,512]{1,0:T(8,128)(2,1)S(1)} %maximum_select_fusion.1.refs_0_), channel_id=1, source_target_pairs={{0,8},{1,9},{2,10},{3,11},{4,12},{5,13},{6,14},{7,15},{8,16},{9,17... | collective-permute-start | bytes 589832 | tf_op jit(solution)/shard_map/ppermute | solution.py:154
  7.7 1.5 %collective-permute-start.2 = (bf16[192,512]{1,0:T(8,128)(2,1)S(1)}, bf16[192,512]{1,0:T(8,128)(2,1)S(1)}, u32[]{:S(2)}, u32[]{:S(2)}) collective-permute-start(bf16[192,512]{1,0:T(8,128)(2,1)S(1)} %maximum_select_fusion.1.refs_0_), channel_id=1, source_target_pairs={{0,4},{1,5},{2,6},{3,7},{4,0},{5,1},{6,2},{7,3},{8,12},{9,13},{10,... | collective-permute-start | bytes 589832 | tf_op jit(solution)/shard_map/ppermute | solution.py:154
  9.2 1.5 %collective-permute-start.1 = (bf16[192,512]{1,0:T(8,128)(2,1)S(1)}, bf16[192,512]{1,0:T(8,128)(2,1)S(1)}, u32[]{:S(2)}, u32[]{:S(2)}) collective-permute-start(bf16[192,512]{1,0:T(8,128)(2,1)S(1)} %maximum_select_fusion.1.refs_0_), channel_id=1, source_target_pairs={{0,2},{1,3},{2,0},{3,1},{4,6},{5,7},{6,4},{7,5},{8,10},{9,11},{10,... | collective-permute-start | bytes 589832 | tf_op jit(solution)/shard_map/ppermute | solution.py:154
  10.7 0.1 compare_convert_fusion.1.refs_12_
  10.8 4.1 %collective-permute-done.4.refs_4_ = bf16[192,512]{1,0:T(8,128)(2,1)S(1)} collective-permute-done((bf16[192,512]{1,0:T(8,128)(2,1)S(1)}, bf16[192,512]{1,0:T(8,128)(2,1)S(1)}, u32[]{:S(2)}, u32[]{:S(2)}) %collective-permute-start.4) | collective-permute-done | bytes 196640 | tf_op jit(solution)/shard_map/ppermute | solution.py:154
  15.0 0.7 collective-permute-done.1.refs_1_
  15.6 0.9 %collective-permute-start.3 = (bf16[192,512]{1,0:T(8,128)(2,1)S(1)}, bf16[192,512]{1,0:T(8,128)(2,1)S(1)}, u32[]{:S(2)}, u32[]{:S(2)}) collective-permute-start(bf16[192,512]{1,0:T(8,128)(2,1)S(1)} %collective-permute-done.1.refs_1_), channel_id=1, source_target_pairs={{0,4},{1,5},{2,6},{3,7},{4,0},{5,1},{6,2},{7,3},{8,12},{9,13},{10,... | collective-permute-start | bytes 589832 | tf_op jit(solution)/shard_map/ppermute | solution.py:154
  16.5 1.5 %collective-permute-start.5 = (bf16[192,512]{1,0:T(8,128)(2,1)S(1)}, bf16[192,512]{1,0:T(8,128)(2,1)S(1)}, u32[]{:S(2)}, u32[]{:S(2)}) collective-permute-start(bf16[192,512]{1,0:T(8,128)(2,1)S(1)} %collective-permute-done.4.refs_4_), channel_id=1, source_target_pairs={{0,2},{1,3},{2,0},{3,1},{4,6},{5,7},{6,4},{7,5},{8,10},{9,11},{10,... | collective-permute-start | bytes 589832 | tf_op jit(solution)/shard_map/ppermute | solution.py:154
  18.0 1.2 %collective-permute-start.14 = (bf16[192,512]{1,0:T(8,128)(2,1)S(1)}, bf16[192,512]{1,0:T(8,128)(2,1)S(1)}, u32[]{:S(2)}, u32[]{:S(2)}) collective-permute-start(bf16[192,512]{1,0:T(8,128)(2,1)S(1)} %collective-permute-done.4.refs_4_), channel_id=1, source_target_pairs={{0,8},{1,9},{2,10},{3,11},{4,12},{5,13},{6,14},{7,15},{8,16},{9,17... | collective-permute-start | bytes 589832 | tf_op jit(solution)/shard_map/ppermute | solution.py:154
  19.2 2.6 %collective-permute-start.10 = (bf16[192,512]{1,0:T(8,128)(2,1)S(1)}, bf16[192,512]{1,0:T(8,128)(2,1)S(1)}, u32[]{:S(2)}, u32[]{:S(2)}) collective-permute-start(bf16[192,512]{1,0:T(8,128)(2,1)S(1)} %maximum_select_fusion.1.refs_0_), channel_id=1, source_target_pairs={{0,24},{1,25},{2,26},{3,27},{4,28},{5,29},{6,30},{7,31},{8,0},{9,1... | collective-permute-start | bytes 589832 | tf_op jit(solution)/shard_map/ppermute | solution.py:154
  21.8 1.2 %collective-permute-start.6 = (bf16[192,512]{1,0:T(8,128)(2,1)S(1)}, bf16[192,512]{1,0:T(8,128)(2,1)S(1)}, u32[]{:S(2)}, u32[]{:S(2)}) collective-permute-start(bf16[192,512]{1,0:T(8,128)(2,1)S(1)} %collective-permute-done.4.refs_4_), channel_id=1, source_target_pairs={{0,4},{1,5},{2,6},{3,7},{4,0},{5,1},{6,2},{7,3},{8,12},{9,13},{10,... | collective-permute-start | bytes 589832 | tf_op jit(solution)/shard_map/ppermute | solution.py:154
  23.0 4.6 %collective-permute-done.14.refs_5_ = bf16[192,512]{1,0:T(8,128)(2,1)S(1)} collective-permute-done((bf16[192,512]{1,0:T(8,128)(2,1)S(1)}, bf16[192,512]{1,0:T(8,128)(2,1)S(1)}, u32[]{:S(2)}, u32[]{:S(2)}) %collective-permute-start.14) | collective-permute-done | bytes 196640 | tf_op jit(solution)/shard_map/ppermute | solution.py:154
  27.6 0.6 collective-permute-start.16
  28.2 0.7 collective-permute-start.15
  28.9 1.3 %collective-permute-start.11 = (bf16[192,512]{1,0:T(8,128)(2,1)S(1)}, bf16[192,512]{1,0:T(8,128)(2,1)S(1)}, u32[]{:S(2)}, u32[]{:S(2)}) collective-permute-start(bf16[192,512]{1,0:T(8,128)(2,1)S(1)} %collective-permute-done.10.refs_1_), channel_id=1, source_target_pairs={{0,2},{1,3},{2,0},{3,1},{4,6},{5,7},{6,4},{7,5},{8,10},{9,11},{10,... | collective-permute-start | bytes 589832 | tf_op jit(solution)/shard_map/ppermute | solution.py:154
  30.3 0.7 collective-permute-start.8
  31.0 3.1 %collective-permute-done.16.refs_7_ = bf16[192,512]{1,0:T(8,128)(2,1)S(1)} collective-permute-done((bf16[192,512]{1,0:T(8,128)(2,1)S(1)}, bf16[192,512]{1,0:T(8,128)(2,1)S(1)}, u32[]{:S(2)}, u32[]{:S(2)}) %collective-permute-start.16) | collective-permute-done | bytes 196640 | tf_op jit(solution)/shard_map/ppermute | solution.py:154
  34.1 1.5 %collective-permute-done.15.refs_6_ = bf16[192,512]{1,0:T(8,128)(2,1)S(1)} collective-permute-done((bf16[192,512]{1,0:T(8,128)(2,1)S(1)}, bf16[192,512]{1,0:T(8,128)(2,1)S(1)}, u32[]{:S(2)}, u32[]{:S(2)}) %collective-permute-start.15) | collective-permute-done | bytes 196640 | tf_op jit(solution)/shard_map/ppermute | solution.py:154
  35.6 1.9 %collective-permute-start.17 = (bf16[96,512]{1,0:T(8,128)(2,1)S(1)}, bf16[96,512]{1,0:T(8,128)(2,1)S(1)}, u32[]{:S(2)}, u32[]{:S(2)}) collective-permute-start(bf16[96,512]{1,0:T(8,128)(2,1)S(1)} %slice.23), channel_id=1, source_target_pairs={{0,4},{1,5},{2,6},{3,7},{4,0},{5,1},{6,2},{7,3},{8,12},{9,13},{10,... | collective-permute-start | bytes 294920 | tf_op jit(solution)/shard_map/ppermute | solution.py:154
  37.5 0.2 collective-permute-start.12
  37.7 3.0 %collective-permute-start.13 = (bf16[192,512]{1,0:T(8,128)(2,1)S(1)}, bf16[192,512]{1,0:T(8,128)(2,1)S(1)}, u32[]{:S(2)}, u32[]{:S(2)}) collective-permute-start(bf16[192,512]{1,0:T(8,128)(2,1)S(1)} %collective-permute-done.11.refs_2_), channel_id=1, source_target_pairs={{0,4},{1,5},{2,6},{3,7},{4,0},{5,1},{6,2},{7,3},{8,12},{9,13},{10,... | collective-permute-start | bytes 589832 | tf_op jit(solution)/shard_map/ppermute | solution.py:154
  40.7 1.6 %copy-done = bf16[2,64,8192]{2,1,0:T(8,128)(2,1)S(1)} copy-done((bf16[2,64,8192]{2,1,0:T(8,128)(2,1)S(1)}, bf16[2,64,8192]{2,1,0:T(8,128)(2,1)}, u32[]{:S(2)}) %copy-start) | copy-done | bytes 2097176
  42.3 0.9 %copy-done.5 = bf16[192,512]{1,0:T(8,128)(2,1)S(1)} copy-done((bf16[192,512]{1,0:T(8,128)(2,1)S(1)}, bf16[192,512]{1,0:T(8,128)(2,1)}, u32[]{:S(2)}) %copy-start.5) | copy-done | bytes 196632
  43.2 1.4 %first.1 = (f32[192,128]{1,0:T(8,128)S(1)}, f32[192,128]{1,0:T(8,128)S(1)}, bf16[1344,512]{1,0:T(8,128)(2,1)S(1)}) custom-call(s32[7]{0:T(128)S(1)} %broadcast_multiply_fusion.1.place_ref, bf16[192,512]{1,0:T(8,128)(2,1)S(1)} %copy-done.5, bf16[192,512]{1,0:T(8,128)(2,1)S(1)} %collective-permute-done.1.refs_1_, ...), custom_call_target="tpu_custom_call" | custom-call | tf_op jit(solution)/shard_map/first/pallas_call | solution.py:54
  44.7 0.6 collective-permute-done.13.refs_4_
  45.3 0.1 copy-done.7
  45.5 4.2 %owner.1 = (bf16[32,32,256]{2,1,0:T(8,128)(2,1)S(1)}, bf16[192,256]{1,0:T(8,128)(2,1)}, bf16[1728,512]{1,0:T(8,128)(2,1)S(1)}) custom-call(s32[9]{0:T(128)S(1)} %broadcast_multiply_fusion.place_ref, bf16[192,512]{1,0:T(8,128)(2,1)S(1)} %collective-permute-done.8.refs_0_, bf16[192,512]{1,0:T(8,128)(2,1)S(1)} %collective-permute-done.10.refs_1_, ...), custom_call_target="tpu_custom_call" | custom-call | tf_op jit(solution)/shard_map/owner/pallas_call | solution.py:111
  49.6 1.2 %copy-done.2 = bf16[1728,512]{1,0:T(8,128)(2,1)} copy-done((bf16[1728,512]{1,0:T(8,128)(2,1)}, bf16[1728,512]{1,0:T(8,128)(2,1)S(1)}, u32[]{:S(2)}) %copy-start.2) | copy-done | bytes 1769496
  50.9 0.8 %copy-done.6 = bf16[32,32,256]{2,1,0:T(8,128)(2,1)} copy-done((bf16[32,32,256]{2,1,0:T(8,128)(2,1)}, bf16[32,32,256]{2,1,0:T(8,128)(2,1)S(1)}, u32[]{:S(2)}) %copy-start.6) | copy-done | bytes 524312
  51.7 3.7 %all-to-all-start.1 = ((bf16[32,32,256]{2,1,0:T(8,128)(2,1)}), bf16[32,32,256]{2,1,0:T(8,128)(2,1)}, u32[]{:S(2)}, u32[]{:S(2)}) async-start(bf16[32,32,256]{2,1,0:T(8,128)(2,1)} %copy-done.6), calls=%async_computation.1 | async-start | bytes 1048576 | tf_op jit(solution)/shard_map/all_to_all | solution.py:244
  55.4 0.1 stack.105
  55.5 0.6 fusion.25
  58.8 1.5 %copy-done.3 = bf16[1728,512]{1,0:T(8,128)(2,1)S(1)} copy-done((bf16[1728,512]{1,0:T(8,128)(2,1)S(1)}, bf16[1728,512]{1,0:T(8,128)(2,1)}, u32[]{:S(2)}) %copy-start.3) | copy-done | bytes 1769496
  60.3 3.8 %base.1 = f32[192,256]{1,0:T(8,128)S(1)} custom-call(s32[16]{0:T(128)S(1)} %broadcast_multiply_fusion.2.place_ref, bf16[1344,512]{1,0:T(8,128)(2,1)S(1)} %get-tuple-element.69.refs_0_, bf16[1728,512]{1,0:T(8,128)(2,1)S(1)} %copy-done.3, bf16[256,8192]{1,0:T(8,128)(2,1)} %refs_2_.1), custom_call_target="tpu_custom_call" | custom-call | tf_op jit(solution)/shard_map/base/pallas_call | solution.py:72
  64.0 4.4 %other.1 = f32[192,256]{1,0:T(8,128)} custom-call(s32[16]{0:T(128)S(1)} %broadcast_multiply_fusion.2.place_ref, bf16[1344,512]{1,0:T(8,128)(2,1)S(1)} %get-tuple-element.69.refs_0_, bf16[1728,512]{1,0:T(8,128)(2,1)S(1)} %copy-done.3, bf16[256,8192]{1,0:T(8,128)(2,1)} %collective-permute-done.19.refs_2_), custom_call_target="tpu_custom_call" | custom-call | tf_op jit(solution)/shard_map/other/pallas_call | solution.py:72
  68.5 0.2 collective-permute-start.20
  68.7 2.3 %all-to-all-done.1 = bf16[32,32,256]{2,1,0:T(8,128)(2,1)} async-done(((bf16[32,32,256]{2,1,0:T(8,128)(2,1)}), bf16[32,32,256]{2,1,0:T(8,128)(2,1)}, u32[]{:S(2)}, u32[]{:S(2)}) %all-to-all-start.1) | async-done | bytes 524320 | tf_op jit(solution)/shard_map/all_to_all | solution.py:244
  71.0 2.2 %fusion.3 = f32[384,256]{1,0:T(8,128)} fusion(bf16[1024,256]{1,0:T(8,128)(2,1)} %bitcast.26, s32[384]{0:T(512)S(1)} %get-tuple-element.103), kind=kOutput, calls=%fused_computation.8 | convolution fusion | flops 201719808 | bytes 919040 | tf_op jit(solution)/shard_map/dot_general | solution.py:248
  73.3 1.7 %fusion.6 = bf16[384,256]{1,0:T(8,128)(2,1)} fusion(f32[3,2,64,256]{3,2,1,0:T(8,128)S(1)} %copy.12, f32[384,256]{1,0:T(8,128)} %get-tuple-element.79), kind=kLoop, calls=%fused_computation.15 | loop fusion | flops 294912 | bytes 983040 | tf_op jit(solution)/shard_map/convert_element_type | solution.py:277
  (50 shorter events, 0.7 us)
Async XLA Ops:
  1.0 1.5 %collective-permute-start = (bf16[192,256]{1,0:T(8,128)(2,1)S(1)}, bf16[192,256]{1,0:T(8,128)(2,1)S(1)}, u32[]{:S(2)}, u32[]{:S(2)}) collective-permute-start(bf16[192,256]{1,0:T(8,128)(2,1)S(1)} %bitcast.52), channel_id=1, source_target_pairs={{0,1},{1,0},{2,3},{3,2},{4,5},{5,4},{6,7},{7,6},{8,9},{9,8},{10,11... | collective-permute-start | bytes 294920 | tf_op jit(solution)/shard_map/ppermute | solution.py:157
  2.5 38.2 %copy-start.4 = (bf16[192,512]{1,0:T(8,128)(2,1)}, bf16[192,512]{1,0:T(8,128)(2,1)S(1)}, u32[]{:S(2)}) copy-start(bf16[192,512]{1,0:T(8,128)(2,1)S(1)} %maximum_select_fusion.1.refs_0_) | copy-start | bytes 589828
  2.5 16.7 %collective-permute-start.7 = (bf16[128,8192]{1,0:T(8,128)(2,1)}, bf16[128,8192]{1,0:T(8,128)(2,1)S(1)}, u32[]{:S(2)}, u32[]{:S(2)}) collective-permute-start(bf16[128,8192]{1,0:T(8,128)(2,1)} %bitcast.41), channel_id=1, source_target_pairs={{0,1},{1,0},{2,3},{3,2},{4,5},{5,4},{6,7},{7,6},{8,9},{9,8},{10,11... | collective-permute-start | bytes 6291464 | tf_op jit(solution)/shard_map/ppermute | solution.py:157
  2.9 16.3 %collective-permute-start.9 = (bf16[128,8192]{1,0:T(8,128)(2,1)}, bf16[128,8192]{1,0:T(8,128)(2,1)}, u32[]{:S(2)}, u32[]{:S(2)}) collective-permute-start(bf16[128,8192]{1,0:T(8,128)(2,1)} %bitcast.45), channel_id=1, source_target_pairs={{0,1},{1,0},{2,3},{3,2},{4,5},{5,4},{6,7},{7,6},{8,9},{9,8},{10,11... | collective-permute-start | bytes 6291464 | tf_op jit(solution)/shard_map/ppermute | solution.py:157
  4.7 10.2 %collective-permute-start.4 = (bf16[192,512]{1,0:T(8,128)(2,1)S(1)}, bf16[192,512]{1,0:T(8,128)(2,1)S(1)}, u32[]{:S(2)}, u32[]{:S(2)}) collective-permute-start(bf16[192,512]{1,0:T(8,128)(2,1)S(1)} %maximum_select_fusion.1.refs_0_), channel_id=1, source_target_pairs={{0,8},{1,9},{2,10},{3,11},{4,12},{5,13},{6,14},{7,15},{8,16},{9,17... | collective-permute-start | bytes 589832 | tf_op jit(solution)/shard_map/ppermute | solution.py:154
  7.7 7.2 %collective-permute-start.2 = (bf16[192,512]{1,0:T(8,128)(2,1)S(1)}, bf16[192,512]{1,0:T(8,128)(2,1)S(1)}, u32[]{:S(2)}, u32[]{:S(2)}) collective-permute-start(bf16[192,512]{1,0:T(8,128)(2,1)S(1)} %maximum_select_fusion.1.refs_0_), channel_id=1, source_target_pairs={{0,4},{1,5},{2,6},{3,7},{4,0},{5,1},{6,2},{7,3},{8,12},{9,13},{10,... | collective-permute-start | bytes 589832 | tf_op jit(solution)/shard_map/ppermute | solution.py:154
  9.2 6.4 %collective-permute-start.1 = (bf16[192,512]{1,0:T(8,128)(2,1)S(1)}, bf16[192,512]{1,0:T(8,128)(2,1)S(1)}, u32[]{:S(2)}, u32[]{:S(2)}) collective-permute-start(bf16[192,512]{1,0:T(8,128)(2,1)S(1)} %maximum_select_fusion.1.refs_0_), channel_id=1, source_target_pairs={{0,2},{1,3},{2,0},{3,1},{4,6},{5,7},{6,4},{7,5},{8,10},{9,11},{10,... | collective-permute-start | bytes 589832 | tf_op jit(solution)/shard_map/ppermute | solution.py:154
  15.6 11.9 %collective-permute-start.3 = (bf16[192,512]{1,0:T(8,128)(2,1)S(1)}, bf16[192,512]{1,0:T(8,128)(2,1)S(1)}, u32[]{:S(2)}, u32[]{:S(2)}) collective-permute-start(bf16[192,512]{1,0:T(8,128)(2,1)S(1)} %collective-permute-done.1.refs_1_), channel_id=1, source_target_pairs={{0,4},{1,5},{2,6},{3,7},{4,0},{5,1},{6,2},{7,3},{8,12},{9,13},{10,... | collective-permute-start | bytes 589832 | tf_op jit(solution)/shard_map/ppermute | solution.py:154
  16.5 11.1 %collective-permute-start.5 = (bf16[192,512]{1,0:T(8,128)(2,1)S(1)}, bf16[192,512]{1,0:T(8,128)(2,1)S(1)}, u32[]{:S(2)}, u32[]{:S(2)}) collective-permute-start(bf16[192,512]{1,0:T(8,128)(2,1)S(1)} %collective-permute-done.4.refs_4_), channel_id=1, source_target_pairs={{0,2},{1,3},{2,0},{3,1},{4,6},{5,7},{6,4},{7,5},{8,10},{9,11},{10,... | collective-permute-start | bytes 589832 | tf_op jit(solution)/shard_map/ppermute | solution.py:154
  18.0 9.6 %collective-permute-start.14 = (bf16[192,512]{1,0:T(8,128)(2,1)S(1)}, bf16[192,512]{1,0:T(8,128)(2,1)S(1)}, u32[]{:S(2)}, u32[]{:S(2)}) collective-permute-start(bf16[192,512]{1,0:T(8,128)(2,1)S(1)} %collective-permute-done.4.refs_4_), channel_id=1, source_target_pairs={{0,8},{1,9},{2,10},{3,11},{4,12},{5,13},{6,14},{7,15},{8,16},{9,17... | collective-permute-start | bytes 589832 | tf_op jit(solution)/shard_map/ppermute | solution.py:154
  19.2 9.7 %collective-permute-start.10 = (bf16[192,512]{1,0:T(8,128)(2,1)S(1)}, bf16[192,512]{1,0:T(8,128)(2,1)S(1)}, u32[]{:S(2)}, u32[]{:S(2)}) collective-permute-start(bf16[192,512]{1,0:T(8,128)(2,1)S(1)} %maximum_select_fusion.1.refs_0_), channel_id=1, source_target_pairs={{0,24},{1,25},{2,26},{3,27},{4,28},{5,29},{6,30},{7,31},{8,0},{9,1... | collective-permute-start | bytes 589832 | tf_op jit(solution)/shard_map/ppermute | solution.py:154
  21.8 8.4 %collective-permute-start.6 = (bf16[192,512]{1,0:T(8,128)(2,1)S(1)}, bf16[192,512]{1,0:T(8,128)(2,1)S(1)}, u32[]{:S(2)}, u32[]{:S(2)}) collective-permute-start(bf16[192,512]{1,0:T(8,128)(2,1)S(1)} %collective-permute-done.4.refs_4_), channel_id=1, source_target_pairs={{0,4},{1,5},{2,6},{3,7},{4,0},{5,1},{6,2},{7,3},{8,12},{9,13},{10,... | collective-permute-start | bytes 589832 | tf_op jit(solution)/shard_map/ppermute | solution.py:154
  27.6 6.5 %collective-permute-start.16 = (bf16[192,512]{1,0:T(8,128)(2,1)S(1)}, bf16[192,512]{1,0:T(8,128)(2,1)S(1)}, u32[]{:S(2)}, u32[]{:S(2)}) collective-permute-start(bf16[192,512]{1,0:T(8,128)(2,1)S(1)} %collective-permute-done.14.refs_5_), channel_id=1, source_target_pairs={{0,4},{1,5},{2,6},{3,7},{4,0},{5,1},{6,2},{7,3},{8,12},{9,13},{10,... | collective-permute-start | bytes 589832 | tf_op jit(solution)/shard_map/ppermute | solution.py:154
  28.2 7.4 %collective-permute-start.15 = (bf16[192,512]{1,0:T(8,128)(2,1)S(1)}, bf16[192,512]{1,0:T(8,128)(2,1)S(1)}, u32[]{:S(2)}, u32[]{:S(2)}) collective-permute-start(bf16[192,512]{1,0:T(8,128)(2,1)S(1)} %collective-permute-done.14.refs_5_), channel_id=1, source_target_pairs={{0,2},{1,3},{2,0},{3,1},{4,6},{5,7},{6,4},{7,5},{8,10},{9,11},{10,... | collective-permute-start | bytes 589832 | tf_op jit(solution)/shard_map/ppermute | solution.py:154
  28.9 8.8 %collective-permute-start.11 = (bf16[192,512]{1,0:T(8,128)(2,1)S(1)}, bf16[192,512]{1,0:T(8,128)(2,1)S(1)}, u32[]{:S(2)}, u32[]{:S(2)}) collective-permute-start(bf16[192,512]{1,0:T(8,128)(2,1)S(1)} %collective-permute-done.10.refs_1_), channel_id=1, source_target_pairs={{0,2},{1,3},{2,0},{3,1},{4,6},{5,7},{6,4},{7,5},{8,10},{9,11},{10,... | collective-permute-start | bytes 589832 | tf_op jit(solution)/shard_map/ppermute | solution.py:154
  30.3 14.4 %collective-permute-start.8 = (bf16[192,512]{1,0:T(8,128)(2,1)S(1)}, bf16[192,512]{1,0:T(8,128)(2,1)S(1)}, u32[]{:S(2)}, u32[]{:S(2)}) collective-permute-start(bf16[192,512]{1,0:T(8,128)(2,1)S(1)} %collective-permute-done.6.refs_6_), channel_id=1, source_target_pairs={{0,2},{1,3},{2,0},{3,1},{4,6},{5,7},{6,4},{7,5},{8,10},{9,11},{10,... | collective-permute-start | bytes 589832 | tf_op jit(solution)/shard_map/ppermute | solution.py:154
  34.1 10.6 %collective-permute-start.18 = (bf16[96,512]{1,0:T(8,128)(2,1)S(1)}, bf16[96,512]{1,0:T(8,128)(2,1)S(1)}, u32[]{:S(2)}, u32[]{:S(2)}) collective-permute-start(bf16[96,512]{1,0:T(8,128)(2,1)S(1)} %slice.24), channel_id=1, source_target_pairs={{0,2},{1,3},{2,0},{3,1},{4,6},{5,7},{6,4},{7,5},{8,10},{9,11},{10,... | collective-permute-start | bytes 294920 | tf_op jit(solution)/shard_map/ppermute | solution.py:154
  35.6 9.1 %collective-permute-start.17 = (bf16[96,512]{1,0:T(8,128)(2,1)S(1)}, bf16[96,512]{1,0:T(8,128)(2,1)S(1)}, u32[]{:S(2)}, u32[]{:S(2)}) collective-permute-start(bf16[96,512]{1,0:T(8,128)(2,1)S(1)} %slice.23), channel_id=1, source_target_pairs={{0,4},{1,5},{2,6},{3,7},{4,0},{5,1},{6,2},{7,3},{8,12},{9,13},{10,... | collective-permute-start | bytes 294920 | tf_op jit(solution)/shard_map/ppermute | solution.py:154
  37.5 7.2 %collective-permute-start.12 = (bf16[192,512]{1,0:T(8,128)(2,1)S(1)}, bf16[192,512]{1,0:T(8,128)(2,1)S(1)}, u32[]{:S(2)}, u32[]{:S(2)}) collective-permute-start(bf16[192,512]{1,0:T(8,128)(2,1)S(1)} %collective-permute-done.10.refs_1_), channel_id=1, source_target_pairs={{0,4},{1,5},{2,6},{3,7},{4,0},{5,1},{6,2},{7,3},{8,12},{9,13},{10,... | collective-permute-start | bytes 589832 | tf_op jit(solution)/shard_map/ppermute | solution.py:154
  37.7 7.6 %collective-permute-start.13 = (bf16[192,512]{1,0:T(8,128)(2,1)S(1)}, bf16[192,512]{1,0:T(8,128)(2,1)S(1)}, u32[]{:S(2)}, u32[]{:S(2)}) collective-permute-start(bf16[192,512]{1,0:T(8,128)(2,1)S(1)} %collective-permute-done.11.refs_2_), channel_id=1, source_target_pairs={{0,4},{1,5},{2,6},{3,7},{4,0},{5,1},{6,2},{7,3},{8,12},{9,13},{10,... | collective-permute-start | bytes 589832 | tf_op jit(solution)/shard_map/ppermute | solution.py:154
  40.7 1.6 %copy-start = (bf16[2,64,8192]{2,1,0:T(8,128)(2,1)S(1)}, bf16[2,64,8192]{2,1,0:T(8,128)(2,1)}, u32[]{:S(2)}) copy-start(bf16[2,64,8192]{2,1,0:T(8,128)(2,1)} %param.10) | copy-start | bytes 6291460
  42.3 0.9 %copy-start.5 = (bf16[192,512]{1,0:T(8,128)(2,1)S(1)}, bf16[192,512]{1,0:T(8,128)(2,1)}, u32[]{:S(2)}) copy-start(bf16[192,512]{1,0:T(8,128)(2,1)} %copy-done.4) | copy-start | bytes 589828
  43.2 2.1 %copy-start.1 = (bf16[2,64,8192]{2,1,0:T(8,128)(2,1)S(1)}, bf16[2,64,8192]{2,1,0:T(8,128)(2,1)}, u32[]{:S(2)}) copy-start(bf16[2,64,8192]{2,1,0:T(8,128)(2,1)} %param.10) | copy-start | bytes 6291460
  43.2 2.2 %copy-start.7 = (bf16[2,64,8192]{2,1,0:T(8,128)(2,1)S(1)}, bf16[2,64,8192]{2,1,0:T(8,128)(2,1)}, u32[]{:S(2)}) copy-start(bf16[2,64,8192]{2,1,0:T(8,128)(2,1)} %param.11) | copy-start | bytes 6291460
  49.6 1.2 %copy-start.2 = (bf16[1728,512]{1,0:T(8,128)(2,1)}, bf16[1728,512]{1,0:T(8,128)(2,1)S(1)}, u32[]{:S(2)}) copy-start(bf16[1728,512]{1,0:T(8,128)(2,1)S(1)} %get-tuple-element.75.refs_1_) | copy-start | bytes 5308420
  50.9 0.8 %copy-start.6 = (bf16[32,32,256]{2,1,0:T(8,128)(2,1)}, bf16[32,32,256]{2,1,0:T(8,128)(2,1)S(1)}, u32[]{:S(2)}) copy-start(bf16[32,32,256]{2,1,0:T(8,128)(2,1)S(1)} %get-tuple-element.78) | copy-start | bytes 1572868
  51.7 12.3 %collective-permute-start.19 = (bf16[256,8192]{1,0:T(8,128)(2,1)}, bf16[256,8192]{1,0:T(8,128)(2,1)}, u32[]{:S(2)}, u32[]{:S(2)}) collective-permute-start(bf16[256,8192]{1,0:T(8,128)(2,1)} %refs_2_.1), channel_id=1, source_target_pairs={{0,1},{1,0},{2,3},{3,2},{4,5},{5,4},{6,7},{7,6},{8,9},{9,8},{10,11... | collective-permute-start | bytes 12582920 | tf_op jit(solution)/shard_map/ppermute | solution.py:157
  51.7 19.3 %all-to-all-start.1 = ((bf16[32,32,256]{2,1,0:T(8,128)(2,1)}), bf16[32,32,256]{2,1,0:T(8,128)(2,1)}, u32[]{:S(2)}, u32[]{:S(2)}) async-start(bf16[32,32,256]{2,1,0:T(8,128)(2,1)} %copy-done.6), calls=%async_computation.1 | async-start | bytes 1048576 | tf_op jit(solution)/shard_map/all_to_all | solution.py:244
  58.8 1.5 %copy-start.3 = (bf16[1728,512]{1,0:T(8,128)(2,1)S(1)}, bf16[1728,512]{1,0:T(8,128)(2,1)}, u32[]{:S(2)}) copy-start(bf16[1728,512]{1,0:T(8,128)(2,1)} %copy-done.2) | copy-start | bytes 5308420
  68.5 4.8 %copy-start.8 = (bf16[2,64,8192]{2,1,0:T(8,128)(2,1)S(1)}, bf16[2,64,8192]{2,1,0:T(8,128)(2,1)}, u32[]{:S(2)}) copy-start(bf16[2,64,8192]{2,1,0:T(8,128)(2,1)} %param.11) | copy-start | bytes 6291460
  68.5 4.8 %copy-start.9 = (bf16[192,256]{1,0:T(8,128)(2,1)S(1)}, bf16[192,256]{1,0:T(8,128)(2,1)}, u32[]{:S(2)}) copy-start(bf16[192,256]{1,0:T(8,128)(2,1)} %get-tuple-element.166) | copy-start | bytes 294916
  68.5 4.7 %collective-permute-start.20 = (f32[192,256]{1,0:T(8,128)}, f32[192,256]{1,0:T(8,128)S(1)}, u32[]{:S(2)}, u32[]{:S(2)}) collective-permute-start(f32[192,256]{1,0:T(8,128)} %other.1), channel_id=1, source_target_pairs={{0,1},{1,0},{2,3},{3,2},{4,5},{5,4},{6,7},{7,6},{8,9},{9,8},{10,11... | collective-permute-start | bytes 589832 | tf_op jit(solution)/shard_map/ppermute | solution.py:157

commit v3 on v2

--- a/solution.py
+++ b/solution.py
@@ -12,7 +12,7 @@
 NT = (((1,), (1,)), ((), ()))
 F32 = jnp.float32
 BF16 = jnp.bfloat16
-HBM = pl.BlockSpec(memory_space=pl.ANY)
+HBM = pl.BlockSpec(memory_space=pltpu.HBM)
 VMEM = pl.BlockSpec(memory_space=pltpu.VMEM)
 SMEM = pl.BlockSpec(memory_space=pltpu.SMEM)
 
@@ -42,23 +42,39 @@
 
 
 def first_kernel(whole, place_ref, *refs):
-    *blocks, t0_ref, t1_ref, out0_ref, out1_ref, packed_ref = refs
+    *blocks, s0_ref, s1_ref, e1_ref = refs[:-6]
+    out0_ref, out1_ref, packed_ref, s1v_ref, e1v_ref, sems = refs[-6:]
+    copies = [
+        pltpu.make_async_copy(s1_ref, s1v_ref, sems.at[0]),
+        pltpu.make_async_copy(e1_ref, e1v_ref, sems.at[1]),
+    ]
+    for copy in copies:
+        copy.start()
     parts = parts_of(blocks, whole, out0_ref.shape[0])
-    totals = [jnp.zeros(out0_ref.shape, F32), jnp.zeros(out1_ref.shape, F32)]
-    out0_ref[...], out1_ref[...] = take(place_ref, parts, (t0_ref, t1_ref), totals, packed_ref)
-
-
-def first(places, blocks, whole, tables):
+    (out0_ref[...],) = take(place_ref, parts, (s0_ref,), [jnp.zeros(out0_ref.shape, F32)], packed_ref)
+    copies[0].wait()
+    (out1_ref[...],) = take(place_ref, parts, (s1v_ref,), [jnp.zeros(out1_ref.shape, F32)])
+    copies[1].wait()
+
+
+def first(places, blocks, whole, s0, s1, e1):
     rows, width = blocks[0].shape
-    shape = jax.ShapeDtypeStruct((rows, tables[0].shape[0]), F32)
+    shape = jax.ShapeDtypeStruct((rows, s0.shape[0]), F32)
     return pl.pallas_call(
         functools.partial(first_kernel, whole),
-        out_shape=(shape, shape, jax.ShapeDtypeStruct((len(whole) * rows, width), BF16)),
-        in_specs=[SMEM] + [VMEM] * (len(blocks) + 2),
-        out_specs=(VMEM,) * 3,
+        out_shape=(
+            shape,
+            shape,
+            jax.ShapeDtypeStruct((len(whole) * rows, width), BF16),
+            jax.ShapeDtypeStruct(s1.shape, BF16),
+            jax.ShapeDtypeStruct(e1.shape, BF16),
+        ),
+        in_specs=[SMEM] + [VMEM] * (len(blocks) + 1) + [HBM] * 2,
+        out_specs=(VMEM,) * 5,
+        scratch_shapes=[pltpu.SemaphoreType.DMA((2,))],
         compiler_params=pltpu.CompilerParams(vmem_limit_bytes=LIMIT),
         name="first",
-    )(places, *blocks, *tables)
+    )(places, *blocks, s0, s1, e1)
 
 
 def base_kernel(place_ref, *refs):
@@ -79,54 +95,41 @@
     )(places, *packs, table)
 
 
-def expand_rows(pick, lows, tables, out_ref):
-    lows = [jnp.dot(pick, low, preferred_element_type=F32).astype(BF16) for low in lows]
+def expand_rows(pick, low, table, out_ref):
+    low = jnp.dot(pick, low, preferred_element_type=F32).astype(BF16)
     width = out_ref.shape[2]
     for part in range(out_ref.shape[0]):
         columns = slice(part * width, (part + 1) * width)
-        value = jnp.dot(lows[0], tables[0][:, columns], preferred_element_type=F32)
-        value += jnp.dot(lows[1], tables[1][:, columns], preferred_element_type=F32)
-        out_ref[part] = value.astype(BF16)
+        out_ref[part] = jnp.dot(low, table[:, columns], preferred_element_type=F32).astype(BF16)
 
 
 def owner_kernel(whole, place_ref, *refs):
-    *blocks, a0_ref, a1_ref, mask_ref, pick_ref, s0_ref, s1_ref, e0_ref, e1_ref = refs[:-5]
-    out_ref, low_ref, packed_ref, given, sem = refs[-5:]
+    *blocks, a0_ref, a1_ref, mask_ref, s0_ref, s1_ref, low_ref, packed_ref = refs
     rows, half = a0_ref.shape
     parts = parts_of(blocks, whole, rows)
     totals = take(place_ref, parts, (s0_ref, s1_ref), [a0_ref[...], a1_ref[...]], packed_ref)
-    lows = []
     for side, total in enumerate(totals):
         columns = slice(side * half, (side + 1) * half)
-        lows.append((total * mask_ref[:, columns]).astype(BF16))
-        low_ref[:, columns] = lows[side]
-    expand_rows(pick_ref[...], lows, (e0_ref, e1_ref), given)
-    copy = pltpu.make_async_copy(given, out_ref, sem)
-    copy.start()
-    copy.wait()
-
-
-def owner(places, blocks, whole, before, mask, pick, tables, out_shape):
+        low_ref[:, columns] = (total * mask_ref[:, columns]).astype(BF16)
+
+
+def owner(places, blocks, whole, before, mask, s0, s1):
     rows, width = mask.shape[0], blocks[-1].shape[1]
     return pl.pallas_call(
         functools.partial(owner_kernel, whole),
         out_shape=(
-            jax.ShapeDtypeStruct(out_shape, BF16),
             jax.ShapeDtypeStruct(mask.shape, BF16),
             jax.ShapeDtypeStruct((len(whole) * rows, width), BF16),
         ),
-        in_specs=[SMEM] + [VMEM] * (len(blocks) + 8),
-        out_specs=(HBM, VMEM, VMEM),
-        scratch_shapes=[pltpu.VMEM(out_shape, BF16), pltpu.SemaphoreType.DMA],
+        in_specs=[SMEM] + [VMEM] * (len(blocks) + 5),
+        out_specs=(VMEM,) * 2,
         compiler_params=pltpu.CompilerParams(vmem_limit_bytes=LIMIT),
         name="owner",
-    )(places, *blocks, *before, mask, pick, *tables)
+    )(places, *blocks, *before, mask, s0, s1)
 
 
 def again_kernel(pick_ref, low_ref, e0_ref, e1_ref, out_ref):
-    half = e0_ref.shape[0]
-    lows = [low_ref[:, :half], low_ref[:, half:]]
-    expand_rows(pick_ref[...], lows, (e0_ref, e1_ref), out_ref)
+    expand_rows(pick_ref[...], low_ref[...], jnp.concatenate([e0_ref[...], e1_ref[...]], axis=0), out_ref)
 
 
 def again(pick, low, e0, e1, out_shape):
@@ -138,6 +141,35 @@
         compiler_params=pltpu.CompilerParams(vmem_limit_bytes=LIMIT),
         name="again",
     )(pick, low, e0, e1)
+
+
+def last_kernel(core_ref, place_ref, value_ref, own_ref, got_ref, extra_ref, out_ref):
+    count, (slots, width) = place_ref.shape[0], value_ref.shape
+    chunk = min(slots, 512)
+    total = extra_ref[...]
+    for start in range(0, slots, chunk):
+        number = lax.broadcasted_iota(jnp.int32, (count, chunk), 1) + start
+        spread = jnp.where(number == place_ref[...], 1.0, 0.0).astype(BF16)
+        total += jnp.dot(spread, value_ref[start : start + chunk, :], preferred_element_type=F32)
+    steps, _, half, _ = out_ref.shape
+    for step in range(steps):
+        own = own_ref[step * half : (step + 1) * half, :]
+        got = got_ref[step * half : (step + 1) * half, :]
+        for side in range(2):
+            row = (2 * step + side) * half
+            base_out = jnp.where(core_ref[0] == side, own, got)
+            out_ref[step, side] = (base_out + 2.0 * total[row : row + half, :]).astype(BF16)
+
+
+def finish(core, place, value, own, got, extra, shape):
+    return pl.pallas_call(
+        last_kernel,
+        out_shape=jax.ShapeDtypeStruct(shape, BF16),
+        in_specs=[SMEM] + [VMEM] * 5,
+        out_specs=VMEM,
+        compiler_params=pltpu.CompilerParams(vmem_limit_bytes=LIMIT),
+        name="finish",
+    )(core, place, value, own, got, extra)
 
 
 def body(groups, inputs, base_weight, shrink_table, expand_table, table_slot, adapter_ids):
@@ -216,7 +248,7 @@
             far[k] = (move(x[k], flip(2)) if number % 2 == 0 else move(y[k], flip(1)),)
     last = shifts[-1]
     early = [(k, bits) for k in shifts[:-3] for bits in range(4)] + [(shifts[-3], bits) for bits in range(3)]
-    *sums, packed0 = first(*gather(early), (shrink0, shrink1))
+    *sums, packed0, near_shrink, near_expand = first(*gather(early), shrink0, shrink1, expand1)
     far[last] = (
         move(x[last][:edge], flip(2)),
         move(y[last][edge:], flip(1)),
@@ -240,41 +272,42 @@
     def pick_of(index):
         return (chosen == (index * SLOTS + jnp.arange(SLOTS))[:, None]).astype(BF16)
 
-    def give_back(sent, index):
+    def give_back(sent):
         value = lax.all_to_all(sent, "wide", split_axis=0, concat_axis=0, tiled=True)
+        return value.reshape(wide * SLOTS, width)
+
+    def place_of(index):
         rest = order - index * SLOTS
-        place = jnp.where((rest >= 0) & (rest < SLOTS), holder * SLOTS + rest, -1)
-        spread = (place[:, None] == jnp.arange(wide * SLOTS)).astype(BF16)
-        return jnp.dot(spread, value.reshape(wide * SLOTS, width), preferred_element_type=F32)
+        return jnp.where((rest >= 0) & (rest < SLOTS), holder * SLOTS + rest, -1)[:, None]
 
     out_shape = (wide, SLOTS, width)
-    sent, low, packed1 = owner(
-        *gather(tail), sums, mask, pick_of(0), (shrink0, shrink1, expand0, expand1), out_shape
-    )
-    adapter_out = give_back(sent, 0)
-    weight1 = swap(after(base_weight, low))
+    low, packed1 = owner(*gather(tail), sums, mask, shrink0, near_shrink)
+    sent = again(pick_of(0), low, expand0, near_expand, out_shape)
+    value = give_back(sent)
+    weight1 = swap(after(base_weight, sent))
     places = gather(early + tail)[0]
-    out0 = base(places, (packed0, packed1), base_weight, rows, "base")
     out1 = base(places, (packed0, packed1), weight1, rows, "other")
+    out0 = base(after(places, out1), (packed0, packed1), base_weight, rows, "base")
     got = swap(out1)
 
     rounds = jnp.max(order) // SLOTS + 1
     if groups > 1:
         rounds = lax.pmax(rounds, "groups")
-    _, adapter_out = lax.while_loop(
-        lambda state: state[0] < rounds,
-        lambda state: (
-            state[0] + 1,
-            state[1] + give_back(again(pick_of(state[0]), low, expand0, expand1, out_shape), state[0]),
-        ),
-        (jnp.int32(1), adapter_out),
-    )
-
-    shape = (steps, half, width)
-    a, b = out0.reshape(shape), got.reshape(shape)
-    base_out = jnp.where(core == 0, jnp.stack([a, b], 1), jnp.stack([b, a], 1))
-    result = base_out.reshape(count, width) + 2.0 * adapter_out
-    return result.astype(BF16).reshape(steps, requests, width)
+
+    def more(state):
+        index, total = state
+        got_rows = give_back(again(pick_of(index), low, expand0, expand1, out_shape))
+        spread = (place_of(index) == jnp.arange(wide * SLOTS)).astype(BF16)
+        return index + 1, total + jnp.dot(spread, got_rows, preferred_element_type=F32)
+
+    _, extra = lax.while_loop(
+        lambda state: state[0] < rounds, more, (after(jnp.int32(1), value, got, out0), jnp.zeros((count, width), F32))
+    )
+
+    result = finish(
+        core.astype(jnp.int32)[None], place_of(0), value, out0, got, extra, (steps, 2, half, width)
+    )
+    return result.reshape(steps, requests, width)
 
 
 def solution(mesh):

time: 75.6 us -> 70.9 us (0.938)
  local copies, waits for them, and re-layouts: 7.8 us -> 4.94 us
  matrix products: 2.23 us -> 0 us
  Pallas kernels: 13.8 us -> 15.3 us
  other arithmetic: 3.69 us -> 2.21 us
  waiting for transfers between devices: 17.8 us -> 19.1 us
  starting transfers between devices: 26.9 us -> 26.1 us
    pallas_call x0 -> x2, Pallas kernels: none -> 3.18 us  [the longest x1 2.24 us: finish(): pl.pallas_call(last_kernel, out_shape=jax.ShapeDtypeStruct(shape, BF16),...]
    ppermute x5, waiting for transfers between devices: 0.95 us -> 4.04 us  [swap(): return lax.ppermute(value, 'wide', [(i, i ^ 1) for i in range(wide)])]
    unnamed x20 -> x14, local copies, waits for them, and re-layouts: 6.2 us -> 3.34 us
    pallas_call x1, Pallas kernels: 4.16 us -> 1.63 us  [owner(): pl.pallas_call(functools.partial(owner_kernel, whole), out_shape=(jax.Sha...]
    dot_general x1 -> x0, matrix products: 2.23 us -> none  [give_back(): jnp.dot(spread, value.reshape(wide * SLOTS, width), preferred_element_typ...]
    convert_element_type x1 -> x0, other arithmetic: 1.73 us -> none  [body(): return result.astype(BF16).reshape(steps, requests, width)]
    all_to_all x1, waiting for transfers between devices: 2.29 us -> 0.62 us  [give_back(): lax.all_to_all(sent, 'wide', split_axis=0, concat_axis=0, tiled=True)]
    ppermute x16, starting transfers between devices: 21.9 us -> 20.6 us  [move(): return lax.ppermute(value, 'wide', pairs)]
  transfers between devices with their start and end apart: 22 -> 22, of which waited for: 8 -> 10; matrix products, arithmetic and copies ran while one was open for 6% -> 4% of each run, Pallas kernels for 13% -> 15%
where the time goes in v3:
time: 70.9 us; the launch traced here: 70.4 us
  starting transfers between devices  26.1 us (37%)
  waiting for transfers between devices  19.1 us (27%)
  Pallas kernels  15.3 us (22%)
  local copies, waits for them, and re-layouts  4.94 us (7%)
  between operations  2.74 us (4%)
  other arithmetic  2.21 us (3%)
    ppermute x16, starting transfers between devices, move(): return lax.ppermute(value, 'wide', pairs)  20.6 us
    ppermute x16, waiting for transfers between devices, move(): return lax.ppermute(value, 'wide', pairs)  14.5 us
    pallas_call x2, Pallas kernels, base(): pl.pallas_call(base_kernel, out_shape=jax.ShapeDtypeStruct((rows, table.s...  8.1 us
    all_to_all x1, starting transfers between devices, give_back(): lax.all_to_all(sent, 'wide', split_axis=0, concat_axis=0, tiled=True)  4.29 us
    ppermute x5, waiting for transfers between devices, swap(): return lax.ppermute(value, 'wide', [(i, i ^ 1) for i in range(wide)])  4.04 us
    unnamed x14, local copies, waits for them, and re-layouts  3.34 us
    pallas_call x1, Pallas kernels, first(): pl.pallas_call(functools.partial(first_kernel, whole), out_shape=(shape,...  2.42 us
    pallas_call x1, Pallas kernels, finish(): pl.pallas_call(last_kernel, out_shape=jax.ShapeDtypeStruct(shape, BF16),...  2.24 us
  transfers between devices with their start and end apart: 22, of which 10 were waited for; matrix products, arithmetic and copies ran while one was open for 4% of the time, Pallas kernels for 15%

profile of v3, /device:TPU:0, one launch (start us, length us, event | category | flops | bytes accessed | tf_op | source)
XLA Modules:
  0.0 70.4 jit_solution(7196334511191679003)
XLA Ops:
  0.0 1.0 %constant_dynamic-slice_fusion.1 = (bf16[3,1,64,256]{3,2,1,0:T(8,128)(2,1)S(1)}, bf16[3,1,64,256]{3,2,1,0:T(8,128)(2,1)S(1)}) fusion(bf16[3,2,64,256]{3,2,1,0:T(8,128)(2,1)} %bitcast.43, s32[]{:T(128)S(6)} %select_n.252, s32[]{:T(128)S(6)} %select_n.260), kind=kLoop, calls=%fused_computation.101 | loop fusion | bytes 393224 | tf_op jit(solution)/shard_map/jit(dynamic_index_in_dim)/dynamic_slice | solution.py:203
  1.0 0.5 collective-permute-start
  1.5 0.9 %collective-permute-done = bf16[192,256]{1,0:T(8,128)(2,1)S(1)} collective-permute-done((bf16[192,256]{1,0:T(8,128)(2,1)S(1)}, bf16[192,256]{1,0:T(8,128)(2,1)S(1)}, u32[]{:S(2)}, u32[]{:S(2)}) %collective-permute-start) | collective-permute-done | bytes 98336 | tf_op jit(solution)/shard_map/ppermute | solution.py:189
  2.5 0.4 collective-permute-start.6
  2.9 0.2 collective-permute-start.7
  3.1 0.8 %select_reduce_fusion = s32[384]{0:T(512)S(1)} fusion(s32[64]{0:T(128)} %param.12, s32[384]{0:T(512)} %bitcast.45), kind=kLoop, calls=%fused_computation.45 | loop fusion | flops 73344 | bytes 3328 | tf_op jit(solution)/shard_map/reduce_sum | solution.py:260
  3.9 0.1 stack.83
  4.0 0.2 convert_reduce_fusion
  4.2 0.1 stack.84
  4.7 2.9 %collective-permute-start.2 = (bf16[192,512]{1,0:T(8,128)(2,1)S(1)}, bf16[192,512]{1,0:T(8,128)(2,1)S(1)}, u32[]{:S(2)}, u32[]{:S(2)}) collective-permute-start(bf16[192,512]{1,0:T(8,128)(2,1)S(1)} %maximum_select_fusion.refs_0_), channel_id=1, source_target_pairs={{0,2},{1,3},{2,0},{3,1},{4,6},{5,7},{6,4},{7,5},{8,10},{9,11},{10,... | collective-permute-start | bytes 589832 | tf_op jit(solution)/shard_map/ppermute | solution.py:186
  7.6 1.5 %collective-permute-start.3 = (bf16[192,512]{1,0:T(8,128)(2,1)S(1)}, bf16[192,512]{1,0:T(8,128)(2,1)S(1)}, u32[]{:S(2)}, u32[]{:S(2)}) collective-permute-start(bf16[192,512]{1,0:T(8,128)(2,1)S(1)} %maximum_select_fusion.refs_0_), channel_id=1, source_target_pairs={{0,4},{1,5},{2,6},{3,7},{4,0},{5,1},{6,2},{7,3},{8,12},{9,13},{10,... | collective-permute-start | bytes 589832 | tf_op jit(solution)/shard_map/ppermute | solution.py:186
  9.2 1.6 %collective-permute-start.1 = (bf16[192,512]{1,0:T(8,128)(2,1)S(1)}, bf16[192,512]{1,0:T(8,128)(2,1)S(1)}, u32[]{:S(2)}, u32[]{:S(2)}) collective-permute-start(bf16[192,512]{1,0:T(8,128)(2,1)S(1)} %maximum_select_fusion.refs_0_), channel_id=1, source_target_pairs={{0,8},{1,9},{2,10},{3,11},{4,12},{5,13},{6,14},{7,15},{8,16},{9,17... | collective-permute-start | bytes 589832 | tf_op jit(solution)/shard_map/ppermute | solution.py:186
  10.7 0.1 compare_convert_fusion.1.refs_12_
  10.8 2.0 %collective-permute-done.2.refs_1_ = bf16[192,512]{1,0:T(8,128)(2,1)S(1)} collective-permute-done((bf16[192,512]{1,0:T(8,128)(2,1)S(1)}, bf16[192,512]{1,0:T(8,128)(2,1)S(1)}, u32[]{:S(2)}, u32[]{:S(2)}) %collective-permute-start.2) | collective-permute-done | bytes 196640 | tf_op jit(solution)/shard_map/ppermute | solution.py:186
  12.9 1.5 %collective-permute-done.3.refs_2_ = bf16[192,512]{1,0:T(8,128)(2,1)S(1)} collective-permute-done((bf16[192,512]{1,0:T(8,128)(2,1)S(1)}, bf16[192,512]{1,0:T(8,128)(2,1)S(1)}, u32[]{:S(2)}, u32[]{:S(2)}) %collective-permute-start.3) | collective-permute-done | bytes 196640 | tf_op jit(solution)/shard_map/ppermute | solution.py:186
  14.3 1.5 %collective-permute-start.13 = (bf16[192,512]{1,0:T(8,128)(2,1)S(1)}, bf16[192,512]{1,0:T(8,128)(2,1)S(1)}, u32[]{:S(2)}, u32[]{:S(2)}) collective-permute-start(bf16[192,512]{1,0:T(8,128)(2,1)S(1)} %collective-permute-done.2.refs_1_), channel_id=1, source_target_pairs={{0,4},{1,5},{2,6},{3,7},{4,0},{5,1},{6,2},{7,3},{8,12},{9,13},{10,... | collective-permute-start | bytes 589832 | tf_op jit(solution)/shard_map/ppermute | solution.py:186
  15.8 1.6 %collective-permute-done.1.refs_4_ = bf16[192,512]{1,0:T(8,128)(2,1)S(1)} collective-permute-done((bf16[192,512]{1,0:T(8,128)(2,1)S(1)}, bf16[192,512]{1,0:T(8,128)(2,1)S(1)}, u32[]{:S(2)}, u32[]{:S(2)}) %collective-permute-start.1) | collective-permute-done | bytes 196640 | tf_op jit(solution)/shard_map/ppermute | solution.py:186
  17.4 0.5 collective-permute-start.14
  18.0 3.8 %collective-permute-start.8 = (bf16[192,512]{1,0:T(8,128)(2,1)S(1)}, bf16[192,512]{1,0:T(8,128)(2,1)S(1)}, u32[]{:S(2)}, u32[]{:S(2)}) collective-permute-start(bf16[192,512]{1,0:T(8,128)(2,1)S(1)} %maximum_select_fusion.refs_0_), channel_id=1, source_target_pairs={{0,24},{1,25},{2,26},{3,27},{4,28},{5,29},{6,30},{7,31},{8,0},{9,1... | collective-permute-start | bytes 589832 | tf_op jit(solution)/shard_map/ppermute | solution.py:186
  21.8 0.5 collective-permute-start.4
  22.3 0.8 %collective-permute-done.14.refs_5_ = bf16[192,512]{1,0:T(8,128)(2,1)S(1)} collective-permute-done((bf16[192,512]{1,0:T(8,128)(2,1)S(1)}, bf16[192,512]{1,0:T(8,128)(2,1)S(1)}, u32[]{:S(2)}, u32[]{:S(2)}) %collective-permute-start.14) | collective-permute-done | bytes 196640 | tf_op jit(solution)/shard_map/ppermute | solution.py:186
  23.1 4.1 %collective-permute-done.12.refs_5_ = bf16[192,512]{1,0:T(8,128)(2,1)S(1)} collective-permute-done((bf16[192,512]{1,0:T(8,128)(2,1)S(1)}, bf16[192,512]{1,0:T(8,128)(2,1)S(1)}, u32[]{:S(2)}, u32[]{:S(2)}) %collective-permute-start.12) | collective-permute-done | bytes 196640 | tf_op jit(solution)/shard_map/ppermute | solution.py:186
  27.2 1.5 %collective-permute-start.15 = (bf16[192,512]{1,0:T(8,128)(2,1)S(1)}, bf16[192,512]{1,0:T(8,128)(2,1)S(1)}, u32[]{:S(2)}, u32[]{:S(2)}) collective-permute-start(bf16[192,512]{1,0:T(8,128)(2,1)S(1)} %collective-permute-done.12.refs_5_), channel_id=1, source_target_pairs={{0,2},{1,3},{2,0},{3,1},{4,6},{5,7},{6,4},{7,5},{8,10},{9,11},{10,... | collective-permute-start | bytes 589832 | tf_op jit(solution)/shard_map/ppermute | solution.py:186
  28.7 0.5 collective-permute-start.16
  29.2 0.8 %collective-permute-start.9 = (bf16[192,512]{1,0:T(8,128)(2,1)S(1)}, bf16[192,512]{1,0:T(8,128)(2,1)S(1)}, u32[]{:S(2)}, u32[]{:S(2)}) collective-permute-start(bf16[192,512]{1,0:T(8,128)(2,1)S(1)} %collective-permute-done.8.refs_1_), channel_id=1, source_target_pairs={{0,2},{1,3},{2,0},{3,1},{4,6},{5,7},{6,4},{7,5},{8,10},{9,11},{10,... | collective-permute-start | bytes 589832 | tf_op jit(solution)/shard_map/ppermute | solution.py:186
  30.0 1.3 %collective-permute-start.5 = (bf16[192,512]{1,0:T(8,128)(2,1)S(1)}, bf16[192,512]{1,0:T(8,128)(2,1)S(1)}, u32[]{:S(2)}, u32[]{:S(2)}) collective-permute-start(bf16[192,512]{1,0:T(8,128)(2,1)S(1)} %collective-permute-done.4.refs_6_), channel_id=1, source_target_pairs={{0,2},{1,3},{2,0},{3,1},{4,6},{5,7},{6,4},{7,5},{8,10},{9,11},{10,... | collective-permute-start | bytes 589832 | tf_op jit(solution)/shard_map/ppermute | solution.py:186
  31.3 3.7 %collective-permute-done.15.refs_6_ = bf16[192,512]{1,0:T(8,128)(2,1)S(1)} collective-permute-done((bf16[192,512]{1,0:T(8,128)(2,1)S(1)}, bf16[192,512]{1,0:T(8,128)(2,1)S(1)}, u32[]{:S(2)}, u32[]{:S(2)}) %collective-permute-start.15) | collective-permute-done | bytes 196640 | tf_op jit(solution)/shard_map/ppermute | solution.py:186
  35.0 0.9 %collective-permute-start.17 = (bf16[96,512]{1,0:T(8,128)(2,1)S(1)}, bf16[96,512]{1,0:T(8,128)(2,1)S(1)}, u32[]{:S(2)}, u32[]{:S(2)}) collective-permute-start(bf16[96,512]{1,0:T(8,128)(2,1)S(1)} %slice.25), channel_id=1, source_target_pairs={{0,4},{1,5},{2,6},{3,7},{4,0},{5,1},{6,2},{7,3},{8,12},{9,13},{10,... | collective-permute-start | bytes 294920 | tf_op jit(solution)/shard_map/ppermute | solution.py:186
  35.9 1.2 %collective-permute-start.18 = (bf16[96,512]{1,0:T(8,128)(2,1)S(1)}, bf16[96,512]{1,0:T(8,128)(2,1)S(1)}, u32[]{:S(2)}, u32[]{:S(2)}) collective-permute-start(bf16[96,512]{1,0:T(8,128)(2,1)S(1)} %slice.26), channel_id=1, source_target_pairs={{0,2},{1,3},{2,0},{3,1},{4,6},{5,7},{6,4},{7,5},{8,10},{9,11},{10,... | collective-permute-start | bytes 294920 | tf_op jit(solution)/shard_map/ppermute | solution.py:186
  37.1 1.5 %collective-permute-start.10 = (bf16[192,512]{1,0:T(8,128)(2,1)S(1)}, bf16[192,512]{1,0:T(8,128)(2,1)S(1)}, u32[]{:S(2)}, u32[]{:S(2)}) collective-permute-start(bf16[192,512]{1,0:T(8,128)(2,1)S(1)} %collective-permute-done.8.refs_1_), channel_id=1, source_target_pairs={{0,4},{1,5},{2,6},{3,7},{4,0},{5,1},{6,2},{7,3},{8,12},{9,13},{10,... | collective-permute-start | bytes 589832 | tf_op jit(solution)/shard_map/ppermute | solution.py:186
  38.7 0.5 collective-permute-start.11
  39.2 1.6 %copy-done = bf16[2,64,8192]{2,1,0:T(8,128)(2,1)S(1)} copy-done((bf16[2,64,8192]{2,1,0:T(8,128)(2,1)S(1)}, bf16[2,64,8192]{2,1,0:T(8,128)(2,1)}, u32[]{:S(2)}) %copy-start) | copy-done | bytes 2097176
  40.8 0.9 %copy-done.4 = bf16[192,512]{1,0:T(8,128)(2,1)S(1)} copy-done((bf16[192,512]{1,0:T(8,128)(2,1)S(1)}, bf16[192,512]{1,0:T(8,128)(2,1)}, u32[]{:S(2)}) %copy-start.4) | copy-done | bytes 196632
  41.7 2.4 %first.1 = (f32[192,128]{1,0:T(8,128)S(1)}, f32[192,128]{1,0:T(8,128)S(1)}, bf16[1344,512]{1,0:T(8,128)(2,1)S(1)}, bf16[128,8192]{1,0:T(8,128)(2,1)S(1)}, bf16[128,8192]{1,0:T(8,128)(2,1)S(1)}) custom-call(s32[7]{0:T(128)S(1)} %broadcast_multiply_fusion.1.place_ref, bf16[192,512]{1,0:T(8,128)(2,1)S(1)} %copy-done.4, ...), custom_call_target="tpu_custom_call" | custom-call | tf_op jit(solution)/shard_map/first/pallas_call | solution.py:63
  44.2 0.7 %collective-permute-done.11.refs_4_ = bf16[192,512]{1,0:T(8,128)(2,1)S(1)} collective-permute-done((bf16[192,512]{1,0:T(8,128)(2,1)S(1)}, bf16[192,512]{1,0:T(8,128)(2,1)S(1)}, u32[]{:S(2)}, u32[]{:S(2)}) %collective-permute-start.11) | collective-permute-done | bytes 196640 | tf_op jit(solution)/shard_map/ppermute | solution.py:186
  44.9 1.6 %owner.1 = (bf16[192,256]{1,0:T(8,128)(2,1)S(1)}, bf16[1728,512]{1,0:T(8,128)(2,1)S(1)}) custom-call(s32[9]{0:T(128)S(1)} %broadcast_multiply_fusion.2.place_ref, bf16[192,512]{1,0:T(8,128)(2,1)S(1)} %collective-permute-done.5.refs_0_, bf16[192,512]{1,0:T(8,128)(2,1)S(1)} %collective-permute-done.8.refs_1_, ...), custom_call_target="tpu_custom_call" | custom-call | tf_op jit(solution)/shard_map/owner/pallas_call | solution.py:118
  46.6 0.9 %again.2 = bf16[32,32,256]{2,1,0:T(8,128)(2,1)S(1)} custom-call(bf16[32,192]{1,0:T(8,128)(2,1)S(1)} %fusion.22.pick_ref, bf16[192,256]{1,0:T(8,128)(2,1)S(1)} %get-tuple-element.170.low_ref, bf16[128,8192]{1,0:T(8,128)(2,1)S(1)} %bitcast.40, bf16[128,8192]{1,0:T(8,128)(2,1)S(1)} %get-tuple-element.79.e1_ref), custom_call_target="tpu_custom_call" | custom-call | tf_op jit(solution)/shard_map/again/pallas_call | solution.py:136
  47.5 0.8 %copy-done.2 = bf16[32,32,256]{2,1,0:T(8,128)(2,1)} copy-done((bf16[32,32,256]{2,1,0:T(8,128)(2,1)}, bf16[32,32,256]{2,1,0:T(8,128)(2,1)S(1)}, u32[]{:S(2)}) %copy-start.2) | copy-done | bytes 524312
  48.3 4.3 %all-to-all-start.1 = ((bf16[32,32,256]{2,1,0:T(8,128)(2,1)}), bf16[32,32,256]{2,1,0:T(8,128)(2,1)}, u32[]{:S(2)}, u32[]{:S(2)}) async-start(bf16[32,32,256]{2,1,0:T(8,128)(2,1)} %copy-done.2), calls=%async_computation.1 | async-start | bytes 1048576 | tf_op jit(solution)/shard_map/all_to_all | solution.py:276
  52.6 0.1 stack.104
  52.7 3.1 %collective-permute-done.19.refs_2_ = bf16[256,8192]{1,0:T(8,128)(2,1)} collective-permute-done((bf16[256,8192]{1,0:T(8,128)(2,1)}, bf16[256,8192]{1,0:T(8,128)(2,1)}, u32[]{:S(2)}, u32[]{:S(2)}) %collective-permute-start.19) | collective-permute-done | bytes 4194336 | tf_op jit(solution)/shard_map/ppermute | solution.py:189
  55.8 4.4 %other.1 = f32[192,256]{1,0:T(8,128)} custom-call(s32[16]{0:T(128)S(1)} %broadcast_multiply_fusion.place_ref, bf16[1344,512]{1,0:T(8,128)(2,1)S(1)} %get-tuple-element.80.refs_0_, bf16[1728,512]{1,0:T(8,128)(2,1)S(1)} %get-tuple-element.81.refs_1_, bf16[256,8192]{1,0:T(8,128)(2,1)} %collective-permute-done.19.refs_2_), custom_call_target="tpu_custom_call" | custom-call | tf_op jit(solution)/shard_map/other/pallas_call | solution.py:88
  60.2 0.1 collective-permute-start.20
  60.4 0.7 reduce_max.9
  63.6 0.2 fusion.13.place_ref
  63.8 3.7 %base.1.own_ref = f32[192,256]{1,0:T(8,128)S(1)} custom-call(s32[16]{0:T(128)S(1)} %broadcast_multiply_fusion.place_ref, bf16[1344,512]{1,0:T(8,128)(2,1)S(1)} %get-tuple-element.80.refs_0_, bf16[1728,512]{1,0:T(8,128)(2,1)S(1)} %get-tuple-element.81.refs_1_, bf16[256,8192]{1,0:T(8,128)(2,1)} %refs_2_.1), custom_call_target="tpu_custom_call" | custom-call | tf_op jit(solution)/shard_map/base/pallas_call | solution.py:88
  67.5 0.6 all-to-all-done.1
  68.2 2.2 %finish.1 = bf16[3,2,64,256]{3,2,1,0:T(8,128)(2,1)} custom-call(s32[1]{0:T(128)} %bitcast.1.core_ref, s32[384,1]{1,0:T(8,128)S(1)} %fusion.13.place_ref, bf16[1024,256]{1,0:T(8,128)(2,1)} %bitcast.24.value_ref, f32[192,256]{1,0:T(8,128)S(1)} %base.1.own_ref, f32[192,256]{1,0:T(8,128)} %collective-permute-done.20.got_ref, ...), custom_call_target="tpu_custom_call" | custom-call | tf_op jit(solution)/shard_map/finish/pallas_call | solution.py:165
  (44 shorter events, 0.7 us)
Async XLA Ops:
  1.0 1.5 %collective-permute-start = (bf16[192,256]{1,0:T(8,128)(2,1)S(1)}, bf16[192,256]{1,0:T(8,128)(2,1)S(1)}, u32[]{:S(2)}, u32[]{:S(2)}) collective-permute-start(bf16[192,256]{1,0:T(8,128)(2,1)S(1)} %bitcast.44), channel_id=1, source_target_pairs={{0,1},{1,0},{2,3},{3,2},{4,5},{5,4},{6,7},{7,6},{8,9},{9,8},{10,11... | collective-permute-start | bytes 294920 | tf_op jit(solution)/shard_map/ppermute | solution.py:189
  2.5 36.7 %copy-start.3 = (bf16[192,512]{1,0:T(8,128)(2,1)}, bf16[192,512]{1,0:T(8,128)(2,1)S(1)}, u32[]{:S(2)}) copy-start(bf16[192,512]{1,0:T(8,128)(2,1)S(1)} %maximum_select_fusion.refs_0_) | copy-start | bytes 589828
  2.5 15.5 %collective-permute-start.6 = (bf16[128,8192]{1,0:T(8,128)(2,1)}, bf16[128,8192]{1,0:T(8,128)(2,1)S(1)}, u32[]{:S(2)}, u32[]{:S(2)}) collective-permute-start(bf16[128,8192]{1,0:T(8,128)(2,1)} %bitcast.35), channel_id=1, source_target_pairs={{0,1},{1,0},{2,3},{3,2},{4,5},{5,4},{6,7},{7,6},{8,9},{9,8},{10,11... | collective-permute-start | bytes 6291464 | tf_op jit(solution)/shard_map/ppermute | solution.py:189
  2.9 15.0 %collective-permute-start.7 = (bf16[128,8192]{1,0:T(8,128)(2,1)}, bf16[128,8192]{1,0:T(8,128)(2,1)}, u32[]{:S(2)}, u32[]{:S(2)}) collective-permute-start(bf16[128,8192]{1,0:T(8,128)(2,1)} %bitcast.38), channel_id=1, source_target_pairs={{0,1},{1,0},{2,3},{3,2},{4,5},{5,4},{6,7},{7,6},{8,9},{9,8},{10,11... | collective-permute-start | bytes 6291464 | tf_op jit(solution)/shard_map/ppermute | solution.py:189
  4.7 8.1 %collective-permute-start.2 = (bf16[192,512]{1,0:T(8,128)(2,1)S(1)}, bf16[192,512]{1,0:T(8,128)(2,1)S(1)}, u32[]{:S(2)}, u32[]{:S(2)}) collective-permute-start(bf16[192,512]{1,0:T(8,128)(2,1)S(1)} %maximum_select_fusion.refs_0_), channel_id=1, source_target_pairs={{0,2},{1,3},{2,0},{3,1},{4,6},{5,7},{6,4},{7,5},{8,10},{9,11},{10,... | collective-permute-start | bytes 589832 | tf_op jit(solution)/shard_map/ppermute | solution.py:186
  7.6 6.7 %collective-permute-start.3 = (bf16[192,512]{1,0:T(8,128)(2,1)S(1)}, bf16[192,512]{1,0:T(8,128)(2,1)S(1)}, u32[]{:S(2)}, u32[]{:S(2)}) collective-permute-start(bf16[192,512]{1,0:T(8,128)(2,1)S(1)} %maximum_select_fusion.refs_0_), channel_id=1, source_target_pairs={{0,4},{1,5},{2,6},{3,7},{4,0},{5,1},{6,2},{7,3},{8,12},{9,13},{10,... | collective-permute-start | bytes 589832 | tf_op jit(solution)/shard_map/ppermute | solution.py:186
  9.2 8.3 %collective-permute-start.1 = (bf16[192,512]{1,0:T(8,128)(2,1)S(1)}, bf16[192,512]{1,0:T(8,128)(2,1)S(1)}, u32[]{:S(2)}, u32[]{:S(2)}) collective-permute-start(bf16[192,512]{1,0:T(8,128)(2,1)S(1)} %maximum_select_fusion.refs_0_), channel_id=1, source_target_pairs={{0,8},{1,9},{2,10},{3,11},{4,12},{5,13},{6,14},{7,15},{8,16},{9,17... | collective-permute-start | bytes 589832 | tf_op jit(solution)/shard_map/ppermute | solution.py:186
  14.3 8.0 %collective-permute-start.13 = (bf16[192,512]{1,0:T(8,128)(2,1)S(1)}, bf16[192,512]{1,0:T(8,128)(2,1)S(1)}, u32[]{:S(2)}, u32[]{:S(2)}) collective-permute-start(bf16[192,512]{1,0:T(8,128)(2,1)S(1)} %collective-permute-done.2.refs_1_), channel_id=1, source_target_pairs={{0,4},{1,5},{2,6},{3,7},{4,0},{5,1},{6,2},{7,3},{8,12},{9,13},{10,... | collective-permute-start | bytes 589832 | tf_op jit(solution)/shard_map/ppermute | solution.py:186
  17.4 5.7 %collective-permute-start.14 = (bf16[192,512]{1,0:T(8,128)(2,1)S(1)}, bf16[192,512]{1,0:T(8,128)(2,1)S(1)}, u32[]{:S(2)}, u32[]{:S(2)}) collective-permute-start(bf16[192,512]{1,0:T(8,128)(2,1)S(1)} %collective-permute-done.1.refs_4_), channel_id=1, source_target_pairs={{0,2},{1,3},{2,0},{3,1},{4,6},{5,7},{6,4},{7,5},{8,10},{9,11},{10,... | collective-permute-start | bytes 589832 | tf_op jit(solution)/shard_map/ppermute | solution.py:186
  18.0 9.3 %collective-permute-start.12 = (bf16[192,512]{1,0:T(8,128)(2,1)S(1)}, bf16[192,512]{1,0:T(8,128)(2,1)S(1)}, u32[]{:S(2)}, u32[]{:S(2)}) collective-permute-start(bf16[192,512]{1,0:T(8,128)(2,1)S(1)} %collective-permute-done.1.refs_4_), channel_id=1, source_target_pairs={{0,8},{1,9},{2,10},{3,11},{4,12},{5,13},{6,14},{7,15},{8,16},{9,17... | collective-permute-start | bytes 589832 | tf_op jit(solution)/shard_map/ppermute | solution.py:186
  18.0 11.3 %collective-permute-start.8 = (bf16[192,512]{1,0:T(8,128)(2,1)S(1)}, bf16[192,512]{1,0:T(8,128)(2,1)S(1)}, u32[]{:S(2)}, u32[]{:S(2)}) collective-permute-start(bf16[192,512]{1,0:T(8,128)(2,1)S(1)} %maximum_select_fusion.refs_0_), channel_id=1, source_target_pairs={{0,24},{1,25},{2,26},{3,27},{4,28},{5,29},{6,30},{7,31},{8,0},{9,1... | collective-permute-start | bytes 589832 | tf_op jit(solution)/shard_map/ppermute | solution.py:186
  21.8 8.2 %collective-permute-start.4 = (bf16[192,512]{1,0:T(8,128)(2,1)S(1)}, bf16[192,512]{1,0:T(8,128)(2,1)S(1)}, u32[]{:S(2)}, u32[]{:S(2)}) collective-permute-start(bf16[192,512]{1,0:T(8,128)(2,1)S(1)} %collective-permute-done.1.refs_4_), channel_id=1, source_target_pairs={{0,4},{1,5},{2,6},{3,7},{4,0},{5,1},{6,2},{7,3},{8,12},{9,13},{10,... | collective-permute-start | bytes 589832 | tf_op jit(solution)/shard_map/ppermute | solution.py:186
  27.2 7.7 %collective-permute-start.15 = (bf16[192,512]{1,0:T(8,128)(2,1)S(1)}, bf16[192,512]{1,0:T(8,128)(2,1)S(1)}, u32[]{:S(2)}, u32[]{:S(2)}) collective-permute-start(bf16[192,512]{1,0:T(8,128)(2,1)S(1)} %collective-permute-done.12.refs_5_), channel_id=1, source_target_pairs={{0,2},{1,3},{2,0},{3,1},{4,6},{5,7},{6,4},{7,5},{8,10},{9,11},{10,... | collective-permute-start | bytes 589832 | tf_op jit(solution)/shard_map/ppermute | solution.py:186
  28.7 7.2 %collective-permute-start.16 = (bf16[192,512]{1,0:T(8,128)(2,1)S(1)}, bf16[192,512]{1,0:T(8,128)(2,1)S(1)}, u32[]{:S(2)}, u32[]{:S(2)}) collective-permute-start(bf16[192,512]{1,0:T(8,128)(2,1)S(1)} %collective-permute-done.12.refs_5_), channel_id=1, source_target_pairs={{0,4},{1,5},{2,6},{3,7},{4,0},{5,1},{6,2},{7,3},{8,12},{9,13},{10,... | collective-permute-start | bytes 589832 | tf_op jit(solution)/shard_map/ppermute | solution.py:186
  29.2 9.4 %collective-permute-start.9 = (bf16[192,512]{1,0:T(8,128)(2,1)S(1)}, bf16[192,512]{1,0:T(8,128)(2,1)S(1)}, u32[]{:S(2)}, u32[]{:S(2)}) collective-permute-start(bf16[192,512]{1,0:T(8,128)(2,1)S(1)} %collective-permute-done.8.refs_1_), channel_id=1, source_target_pairs={{0,2},{1,3},{2,0},{3,1},{4,6},{5,7},{6,4},{7,5},{8,10},{9,11},{10,... | collective-permute-start | bytes 589832 | tf_op jit(solution)/shard_map/ppermute | solution.py:186
  30.0 14.1 %collective-permute-start.5 = (bf16[192,512]{1,0:T(8,128)(2,1)S(1)}, bf16[192,512]{1,0:T(8,128)(2,1)S(1)}, u32[]{:S(2)}, u32[]{:S(2)}) collective-permute-start(bf16[192,512]{1,0:T(8,128)(2,1)S(1)} %collective-permute-done.4.refs_6_), channel_id=1, source_target_pairs={{0,2},{1,3},{2,0},{3,1},{4,6},{5,7},{6,4},{7,5},{8,10},{9,11},{10,... | collective-permute-start | bytes 589832 | tf_op jit(solution)/shard_map/ppermute | solution.py:186
  35.0 9.1 %collective-permute-start.17 = (bf16[96,512]{1,0:T(8,128)(2,1)S(1)}, bf16[96,512]{1,0:T(8,128)(2,1)S(1)}, u32[]{:S(2)}, u32[]{:S(2)}) collective-permute-start(bf16[96,512]{1,0:T(8,128)(2,1)S(1)} %slice.25), channel_id=1, source_target_pairs={{0,4},{1,5},{2,6},{3,7},{4,0},{5,1},{6,2},{7,3},{8,12},{9,13},{10,... | collective-permute-start | bytes 294920 | tf_op jit(solution)/shard_map/ppermute | solution.py:186
  35.9 8.2 %collective-permute-start.18 = (bf16[96,512]{1,0:T(8,128)(2,1)S(1)}, bf16[96,512]{1,0:T(8,128)(2,1)S(1)}, u32[]{:S(2)}, u32[]{:S(2)}) collective-permute-start(bf16[96,512]{1,0:T(8,128)(2,1)S(1)} %slice.26), channel_id=1, source_target_pairs={{0,2},{1,3},{2,0},{3,1},{4,6},{5,7},{6,4},{7,5},{8,10},{9,11},{10,... | collective-permute-start | bytes 294920 | tf_op jit(solution)/shard_map/ppermute | solution.py:186
  37.1 7.0 %collective-permute-start.10 = (bf16[192,512]{1,0:T(8,128)(2,1)S(1)}, bf16[192,512]{1,0:T(8,128)(2,1)S(1)}, u32[]{:S(2)}, u32[]{:S(2)}) collective-permute-start(bf16[192,512]{1,0:T(8,128)(2,1)S(1)} %collective-permute-done.8.refs_1_), channel_id=1, source_target_pairs={{0,4},{1,5},{2,6},{3,7},{4,0},{5,1},{6,2},{7,3},{8,12},{9,13},{10,... | collective-permute-start | bytes 589832 | tf_op jit(solution)/shard_map/ppermute | solution.py:186
  38.7 6.3 %collective-permute-start.11 = (bf16[192,512]{1,0:T(8,128)(2,1)S(1)}, bf16[192,512]{1,0:T(8,128)(2,1)S(1)}, u32[]{:S(2)}, u32[]{:S(2)}) collective-permute-start(bf16[192,512]{1,0:T(8,128)(2,1)S(1)} %collective-permute-done.9.refs_2_), channel_id=1, source_target_pairs={{0,4},{1,5},{2,6},{3,7},{4,0},{5,1},{6,2},{7,3},{8,12},{9,13},{10,... | collective-permute-start | bytes 589832 | tf_op jit(solution)/shard_map/ppermute | solution.py:186
  39.2 1.6 %copy-start = (bf16[2,64,8192]{2,1,0:T(8,128)(2,1)S(1)}, bf16[2,64,8192]{2,1,0:T(8,128)(2,1)}, u32[]{:S(2)}) copy-start(bf16[2,64,8192]{2,1,0:T(8,128)(2,1)} %param.10) | copy-start | bytes 6291460
  40.8 0.9 %copy-start.4 = (bf16[192,512]{1,0:T(8,128)(2,1)S(1)}, bf16[192,512]{1,0:T(8,128)(2,1)}, u32[]{:S(2)}) copy-start(bf16[192,512]{1,0:T(8,128)(2,1)} %copy-done.3) | copy-start | bytes 589828
  41.7 3.2 %copy-start.1 = (bf16[2,64,8192]{2,1,0:T(8,128)(2,1)S(1)}, bf16[2,64,8192]{2,1,0:T(8,128)(2,1)}, u32[]{:S(2)}) copy-start(bf16[2,64,8192]{2,1,0:T(8,128)(2,1)} %param.10) | copy-start | bytes 6291460
  44.9 1.6 %copy-start.5 = (bf16[2,64,8192]{2,1,0:T(8,128)(2,1)S(1)}, bf16[2,64,8192]{2,1,0:T(8,128)(2,1)}, u32[]{:S(2)}) copy-start(bf16[2,64,8192]{2,1,0:T(8,128)(2,1)} %param.11) | copy-start | bytes 6291460
  46.5 1.0 %copy-start.6 = (bf16[192,256]{1,0:T(8,128)(2,1)}, bf16[192,256]{1,0:T(8,128)(2,1)S(1)}, u32[]{:S(2)}) copy-start(bf16[192,256]{1,0:T(8,128)(2,1)S(1)} %get-tuple-element.170.low_ref) | copy-start | bytes 294916
  47.5 0.8 %copy-start.2 = (bf16[32,32,256]{2,1,0:T(8,128)(2,1)}, bf16[32,32,256]{2,1,0:T(8,128)(2,1)S(1)}, u32[]{:S(2)}) copy-start(bf16[32,32,256]{2,1,0:T(8,128)(2,1)S(1)} %again.2) | copy-start | bytes 1572868
  48.3 7.5 %collective-permute-start.19 = (bf16[256,8192]{1,0:T(8,128)(2,1)}, bf16[256,8192]{1,0:T(8,128)(2,1)}, u32[]{:S(2)}, u32[]{:S(2)}) collective-permute-start(bf16[256,8192]{1,0:T(8,128)(2,1)} %refs_2_.1), channel_id=1, source_target_pairs={{0,1},{1,0},{2,3},{3,2},{4,5},{5,4},{6,7},{7,6},{8,9},{9,8},{10,11... | collective-permute-start | bytes 12582920 | tf_op jit(solution)/shard_map/ppermute | solution.py:189
  48.3 19.8 %all-to-all-start.1 = ((bf16[32,32,256]{2,1,0:T(8,128)(2,1)}), bf16[32,32,256]{2,1,0:T(8,128)(2,1)}, u32[]{:S(2)}, u32[]{:S(2)}) async-start(bf16[32,32,256]{2,1,0:T(8,128)(2,1)} %copy-done.2), calls=%async_computation.1 | async-start | bytes 1048576 | tf_op jit(solution)/shard_map/all_to_all | solution.py:276
  60.2 7.9 %collective-permute-start.20 = (f32[192,256]{1,0:T(8,128)}, f32[192,256]{1,0:T(8,128)}, u32[]{:S(2)}, u32[]{:S(2)}) collective-permute-start(f32[192,256]{1,0:T(8,128)} %other.1), channel_id=1, source_target_pairs={{0,1},{1,0},{2,3},{3,2},{4,5},{5,4},{6,7},{7,6},{8,9},{9,8},{10,11... | collective-permute-start | bytes 589832 | tf_op jit(solution)/shard_map/ppermute | solution.py:189

commit v4 on v3

--- a/solution.py
+++ b/solution.py
@@ -232,11 +232,11 @@
         if k == 1:
             source = block
         elif k == depth - 1:
-            source = after(block, shrink1, expand1)
+            source = after(block, x[0], shrink1)
         else:
             source = z[k - 1]
         z[k] = move(source, shift(k if k == depth - 1 else 1))
-    far[0] = (move(after(x[0], y[0]), flip(2)),)
+    far[0] = (move(after(x[0], y[0], expand1), flip(2)),)
     for number, k in enumerate(shifts[1:], 1):
         ready = z[k]
         if number == 1:

time: 70.9 us -> 70.3 us (level)
  waiting for transfers between devices: 19.1 us -> 18.1 us
    ppermute x16, waiting for transfers between devices: 14.5 us -> 13.1 us  [move(): return lax.ppermute(value, 'wide', pairs)]
    ppermute x16, starting transfers between devices: 20.6 us -> 21.9 us  [move(): return lax.ppermute(value, 'wide', pairs)]
    all_to_all x1, starting transfers between devices: 4.29 us -> 3.33 us  [give_back(): lax.all_to_all(sent, 'wide', split_axis=0, concat_axis=0, tiled=True)]
    ppermute x5, waiting for transfers between devices: 4.04 us -> 5 us  [swap(): return lax.ppermute(value, 'wide', [(i, i ^ 1) for i in range(wide)])]
  transfers between devices with their start and end apart: 22 -> 22, of which waited for: 10 -> 9; matrix products, arithmetic and copies ran while one was open for 4% -> 4% of each run, Pallas kernels for 15% -> 15%
where the time goes in v4:
time: 70.3 us; the launch traced here: 69.9 us
  starting transfers between devices  26.5 us (38%)
  waiting for transfers between devices  18.1 us (26%)
  Pallas kernels  15.3 us (22%)
  local copies, waits for them, and re-layouts  4.94 us (7%)
  between operations  2.77 us (4%)
  other arithmetic  2.21 us (3%)
    ppermute x16, starting transfers between devices, move(): return lax.ppermute(value, 'wide', pairs)  21.9 us
    ppermute x16, waiting for transfers between devices, move(): return lax.ppermute(value, 'wide', pairs)  13.1 us
    pallas_call x2, Pallas kernels, base(): pl.pallas_call(base_kernel, out_shape=jax.ShapeDtypeStruct((rows, table.s...  8.1 us
    ppermute x5, waiting for transfers between devices, swap(): return lax.ppermute(value, 'wide', [(i, i ^ 1) for i in range(wide)])  5 us
    unnamed x14, local copies, waits for them, and re-layouts  3.35 us
    all_to_all x1, starting transfers between devices, give_back(): lax.all_to_all(sent, 'wide', split_axis=0, concat_axis=0, tiled=True)  3.33 us
    pallas_call x1, Pallas kernels, first(): pl.pallas_call(functools.partial(first_kernel, whole), out_shape=(shape,...  2.42 us
    pallas_call x1, Pallas kernels, finish(): pl.pallas_call(last_kernel, out_shape=jax.ShapeDtypeStruct(shape, BF16),...  2.24 us
  transfers between devices with their start and end apart: 22, of which 9 were waited for; matrix products, arithmetic and copies ran while one was open for 4% of the time, Pallas kernels for 15%

profile of v4, /device:TPU:0, one launch (start us, length us, event | category | flops | bytes accessed | tf_op | source)
XLA Modules:
  0.0 69.9 jit_solution(12335895867816500068)
XLA Ops:
  0.0 1.0 %constant_dynamic-slice_fusion.1 = (bf16[3,1,64,256]{3,2,1,0:T(8,128)(2,1)S(1)}, bf16[3,1,64,256]{3,2,1,0:T(8,128)(2,1)S(1)}) fusion(bf16[3,2,64,256]{3,2,1,0:T(8,128)(2,1)} %bitcast.43, s32[]{:T(128)S(6)} %select_n.252, s32[]{:T(128)S(6)} %select_n.260), kind=kLoop, calls=%fused_computation.101 | loop fusion | bytes 393224 | tf_op jit(solution)/shard_map/jit(dynamic_index_in_dim)/dynamic_slice | solution.py:203
  1.0 0.5 collective-permute-start
  1.5 0.9 %collective-permute-done = bf16[192,256]{1,0:T(8,128)(2,1)S(1)} collective-permute-done((bf16[192,256]{1,0:T(8,128)(2,1)S(1)}, bf16[192,256]{1,0:T(8,128)(2,1)S(1)}, u32[]{:S(2)}, u32[]{:S(2)}) %collective-permute-start) | collective-permute-done | bytes 98336 | tf_op jit(solution)/shard_map/ppermute | solution.py:189
  2.5 0.4 collective-permute-start.12
  2.9 0.2 collective-permute-start.6
  3.1 0.8 %select_reduce_fusion = s32[384]{0:T(512)S(1)} fusion(s32[64]{0:T(128)} %param.12, s32[384]{0:T(512)} %bitcast.45), kind=kLoop, calls=%fused_computation.45 | loop fusion | flops 73344 | bytes 3328 | tf_op jit(solution)/shard_map/reduce_sum | solution.py:260
  3.9 0.1 stack.83
  4.0 0.2 convert_reduce_fusion
  4.2 0.1 stack.84
  4.6 0.1 stack.95
  4.7 2.9 %collective-permute-start.2 = (bf16[192,512]{1,0:T(8,128)(2,1)S(1)}, bf16[192,512]{1,0:T(8,128)(2,1)S(1)}, u32[]{:S(2)}, u32[]{:S(2)}) collective-permute-start(bf16[192,512]{1,0:T(8,128)(2,1)S(1)} %maximum_select_fusion.refs_0_), channel_id=1, source_target_pairs={{0,2},{1,3},{2,0},{3,1},{4,6},{5,7},{6,4},{7,5},{8,10},{9,11},{10,... | collective-permute-start | bytes 589832 | tf_op jit(solution)/shard_map/ppermute | solution.py:186
  7.6 1.5 %collective-permute-start.3 = (bf16[192,512]{1,0:T(8,128)(2,1)S(1)}, bf16[192,512]{1,0:T(8,128)(2,1)S(1)}, u32[]{:S(2)}, u32[]{:S(2)}) collective-permute-start(bf16[192,512]{1,0:T(8,128)(2,1)S(1)} %maximum_select_fusion.refs_0_), channel_id=1, source_target_pairs={{0,4},{1,5},{2,6},{3,7},{4,0},{5,1},{6,2},{7,3},{8,12},{9,13},{10,... | collective-permute-start | bytes 589832 | tf_op jit(solution)/shard_map/ppermute | solution.py:186
  9.2 1.6 %collective-permute-start.1 = (bf16[192,512]{1,0:T(8,128)(2,1)S(1)}, bf16[192,512]{1,0:T(8,128)(2,1)S(1)}, u32[]{:S(2)}, u32[]{:S(2)}) collective-permute-start(bf16[192,512]{1,0:T(8,128)(2,1)S(1)} %maximum_select_fusion.refs_0_), channel_id=1, source_target_pairs={{0,8},{1,9},{2,10},{3,11},{4,12},{5,13},{6,14},{7,15},{8,16},{9,17... | collective-permute-start | bytes 589832 | tf_op jit(solution)/shard_map/ppermute | solution.py:186
  10.7 0.1 compare_convert_fusion.1.refs_12_
  10.8 2.0 %collective-permute-done.2.refs_1_ = bf16[192,512]{1,0:T(8,128)(2,1)S(1)} collective-permute-done((bf16[192,512]{1,0:T(8,128)(2,1)S(1)}, bf16[192,512]{1,0:T(8,128)(2,1)S(1)}, u32[]{:S(2)}, u32[]{:S(2)}) %collective-permute-start.2) | collective-permute-done | bytes 196640 | tf_op jit(solution)/shard_map/ppermute | solution.py:186
  12.9 1.5 %collective-permute-done.3.refs_2_ = bf16[192,512]{1,0:T(8,128)(2,1)S(1)} collective-permute-done((bf16[192,512]{1,0:T(8,128)(2,1)S(1)}, bf16[192,512]{1,0:T(8,128)(2,1)S(1)}, u32[]{:S(2)}, u32[]{:S(2)}) %collective-permute-start.3) | collective-permute-done | bytes 196640 | tf_op jit(solution)/shard_map/ppermute | solution.py:186
  14.3 3.1 %collective-permute-done.1.refs_4_ = bf16[192,512]{1,0:T(8,128)(2,1)S(1)} collective-permute-done((bf16[192,512]{1,0:T(8,128)(2,1)S(1)}, bf16[192,512]{1,0:T(8,128)(2,1)S(1)}, u32[]{:S(2)}, u32[]{:S(2)}) %collective-permute-start.1) | collective-permute-done | bytes 196640 | tf_op jit(solution)/shard_map/ppermute | solution.py:186
  17.4 0.5 collective-permute-start.14
  18.0 0.5 collective-permute-start.13
  18.5 3.8 %collective-permute-start.7 = (bf16[192,512]{1,0:T(8,128)(2,1)S(1)}, bf16[192,512]{1,0:T(8,128)(2,1)S(1)}, u32[]{:S(2)}, u32[]{:S(2)}) collective-permute-start(bf16[192,512]{1,0:T(8,128)(2,1)S(1)} %maximum_select_fusion.refs_0_), channel_id=1, source_target_pairs={{0,24},{1,25},{2,26},{3,27},{4,28},{5,29},{6,30},{7,31},{8,0},{9,1... | collective-permute-start | bytes 589832 | tf_op jit(solution)/shard_map/ppermute | solution.py:186
  22.3 1.5 %collective-permute-start.4 = (bf16[192,512]{1,0:T(8,128)(2,1)S(1)}, bf16[192,512]{1,0:T(8,128)(2,1)S(1)}, u32[]{:S(2)}, u32[]{:S(2)}) collective-permute-start(bf16[192,512]{1,0:T(8,128)(2,1)S(1)} %collective-permute-done.1.refs_4_), channel_id=1, source_target_pairs={{0,4},{1,5},{2,6},{3,7},{4,0},{5,1},{6,2},{7,3},{8,12},{9,13},{10,... | collective-permute-start | bytes 589832 | tf_op jit(solution)/shard_map/ppermute | solution.py:186
  23.8 3.4 %collective-permute-done.11.refs_5_ = bf16[192,512]{1,0:T(8,128)(2,1)S(1)} collective-permute-done((bf16[192,512]{1,0:T(8,128)(2,1)S(1)}, bf16[192,512]{1,0:T(8,128)(2,1)S(1)}, u32[]{:S(2)}, u32[]{:S(2)}) %collective-permute-start.11) | collective-permute-done | bytes 196640 | tf_op jit(solution)/shard_map/ppermute | solution.py:186
  27.2 1.5 %collective-permute-start.15 = (bf16[192,512]{1,0:T(8,128)(2,1)S(1)}, bf16[192,512]{1,0:T(8,128)(2,1)S(1)}, u32[]{:S(2)}, u32[]{:S(2)}) collective-permute-start(bf16[192,512]{1,0:T(8,128)(2,1)S(1)} %collective-permute-done.11.refs_5_), channel_id=1, source_target_pairs={{0,2},{1,3},{2,0},{3,1},{4,6},{5,7},{6,4},{7,5},{8,10},{9,11},{10,... | collective-permute-start | bytes 589832 | tf_op jit(solution)/shard_map/ppermute | solution.py:186
  28.7 0.5 collective-permute-start.16
  29.2 0.8 %collective-permute-start.8 = (bf16[192,512]{1,0:T(8,128)(2,1)S(1)}, bf16[192,512]{1,0:T(8,128)(2,1)S(1)}, u32[]{:S(2)}, u32[]{:S(2)}) collective-permute-start(bf16[192,512]{1,0:T(8,128)(2,1)S(1)} %collective-permute-done.7.refs_1_), channel_id=1, source_target_pairs={{0,2},{1,3},{2,0},{3,1},{4,6},{5,7},{6,4},{7,5},{8,10},{9,11},{10,... | collective-permute-start | bytes 589832 | tf_op jit(solution)/shard_map/ppermute | solution.py:186
  30.0 1.5 %collective-permute-start.5 = (bf16[192,512]{1,0:T(8,128)(2,1)S(1)}, bf16[192,512]{1,0:T(8,128)(2,1)S(1)}, u32[]{:S(2)}, u32[]{:S(2)}) collective-permute-start(bf16[192,512]{1,0:T(8,128)(2,1)S(1)} %collective-permute-done.4.refs_6_), channel_id=1, source_target_pairs={{0,2},{1,3},{2,0},{3,1},{4,6},{5,7},{6,4},{7,5},{8,10},{9,11},{10,... | collective-permute-start | bytes 589832 | tf_op jit(solution)/shard_map/ppermute | solution.py:186
  31.5 1.3 %collective-permute-start.9 = (bf16[192,512]{1,0:T(8,128)(2,1)S(1)}, bf16[192,512]{1,0:T(8,128)(2,1)S(1)}, u32[]{:S(2)}, u32[]{:S(2)}) collective-permute-start(bf16[192,512]{1,0:T(8,128)(2,1)S(1)} %collective-permute-done.7.refs_1_), channel_id=1, source_target_pairs={{0,4},{1,5},{2,6},{3,7},{4,0},{5,1},{6,2},{7,3},{8,12},{9,13},{10,... | collective-permute-start | bytes 589832 | tf_op jit(solution)/shard_map/ppermute | solution.py:186
  32.8 2.3 %collective-permute-done.15.refs_6_ = bf16[192,512]{1,0:T(8,128)(2,1)S(1)} collective-permute-done((bf16[192,512]{1,0:T(8,128)(2,1)S(1)}, bf16[192,512]{1,0:T(8,128)(2,1)S(1)}, u32[]{:S(2)}, u32[]{:S(2)}) %collective-permute-start.15) | collective-permute-done | bytes 196640 | tf_op jit(solution)/shard_map/ppermute | solution.py:186
  35.1 0.7 collective-permute-start.17
  35.8 0.6 collective-permute-done.16.refs_7_
  36.4 0.8 %collective-permute-start.18 = (bf16[96,512]{1,0:T(8,128)(2,1)S(1)}, bf16[96,512]{1,0:T(8,128)(2,1)S(1)}, u32[]{:S(2)}, u32[]{:S(2)}) collective-permute-start(bf16[96,512]{1,0:T(8,128)(2,1)S(1)} %slice.26), channel_id=1, source_target_pairs={{0,2},{1,3},{2,0},{3,1},{4,6},{5,7},{6,4},{7,5},{8,10},{9,11},{10,... | collective-permute-start | bytes 294920 | tf_op jit(solution)/shard_map/ppermute | solution.py:186
  37.2 0.2 collective-permute-done.8.refs_2_
  37.4 2.5 %collective-permute-start.10 = (bf16[192,512]{1,0:T(8,128)(2,1)S(1)}, bf16[192,512]{1,0:T(8,128)(2,1)S(1)}, u32[]{:S(2)}, u32[]{:S(2)}) collective-permute-start(bf16[192,512]{1,0:T(8,128)(2,1)S(1)} %collective-permute-done.8.refs_2_), channel_id=1, source_target_pairs={{0,4},{1,5},{2,6},{3,7},{4,0},{5,1},{6,2},{7,3},{8,12},{9,13},{10,... | collective-permute-start | bytes 589832 | tf_op jit(solution)/shard_map/ppermute | solution.py:186
  39.9 1.6 %copy-done = bf16[2,64,8192]{2,1,0:T(8,128)(2,1)S(1)} copy-done((bf16[2,64,8192]{2,1,0:T(8,128)(2,1)S(1)}, bf16[2,64,8192]{2,1,0:T(8,128)(2,1)}, u32[]{:S(2)}) %copy-start) | copy-done | bytes 2097176
  41.5 0.9 %copy-done.4 = bf16[192,512]{1,0:T(8,128)(2,1)S(1)} copy-done((bf16[192,512]{1,0:T(8,128)(2,1)S(1)}, bf16[192,512]{1,0:T(8,128)(2,1)}, u32[]{:S(2)}) %copy-start.4) | copy-done | bytes 196632
  42.4 2.4 %first.1 = (f32[192,128]{1,0:T(8,128)S(1)}, f32[192,128]{1,0:T(8,128)S(1)}, bf16[1344,512]{1,0:T(8,128)(2,1)S(1)}, bf16[128,8192]{1,0:T(8,128)(2,1)S(1)}, bf16[128,8192]{1,0:T(8,128)(2,1)S(1)}) custom-call(s32[7]{0:T(128)S(1)} %broadcast_multiply_fusion.1.place_ref, bf16[192,512]{1,0:T(8,128)(2,1)S(1)} %copy-done.4, ...), custom_call_target="tpu_custom_call" | custom-call | tf_op jit(solution)/shard_map/first/pallas_call | solution.py:63
  44.9 1.6 %owner.1 = (bf16[192,256]{1,0:T(8,128)(2,1)S(1)}, bf16[1728,512]{1,0:T(8,128)(2,1)S(1)}) custom-call(s32[9]{0:T(128)S(1)} %broadcast_multiply_fusion.2.place_ref, bf16[192,512]{1,0:T(8,128)(2,1)S(1)} %collective-permute-done.5.refs_0_, bf16[192,512]{1,0:T(8,128)(2,1)S(1)} %collective-permute-done.7.refs_1_, ...), custom_call_target="tpu_custom_call" | custom-call | tf_op jit(solution)/shard_map/owner/pallas_call | solution.py:118
  46.6 0.9 %again.2 = bf16[32,32,256]{2,1,0:T(8,128)(2,1)S(1)} custom-call(bf16[32,192]{1,0:T(8,128)(2,1)S(1)} %fusion.22.pick_ref, bf16[192,256]{1,0:T(8,128)(2,1)S(1)} %get-tuple-element.170.low_ref, bf16[128,8192]{1,0:T(8,128)(2,1)S(1)} %bitcast.40, bf16[128,8192]{1,0:T(8,128)(2,1)S(1)} %get-tuple-element.79.e1_ref), custom_call_target="tpu_custom_call" | custom-call | tf_op jit(solution)/shard_map/again/pallas_call | solution.py:136
  47.6 0.8 %copy-done.2 = bf16[32,32,256]{2,1,0:T(8,128)(2,1)} copy-done((bf16[32,32,256]{2,1,0:T(8,128)(2,1)}, bf16[32,32,256]{2,1,0:T(8,128)(2,1)S(1)}, u32[]{:S(2)}) %copy-start.2) | copy-done | bytes 524312
  48.4 3.3 %all-to-all-start.1 = ((bf16[32,32,256]{2,1,0:T(8,128)(2,1)}), bf16[32,32,256]{2,1,0:T(8,128)(2,1)}, u32[]{:S(2)}, u32[]{:S(2)}) async-start(bf16[32,32,256]{2,1,0:T(8,128)(2,1)} %copy-done.2), calls=%async_computation.1 | async-start | bytes 1048576 | tf_op jit(solution)/shard_map/all_to_all | solution.py:276
  51.7 0.1 stack.104
  51.8 4.0 %collective-permute-done.19.refs_2_ = bf16[256,8192]{1,0:T(8,128)(2,1)} collective-permute-done((bf16[256,8192]{1,0:T(8,128)(2,1)}, bf16[256,8192]{1,0:T(8,128)(2,1)}, u32[]{:S(2)}, u32[]{:S(2)}) %collective-permute-start.19) | collective-permute-done | bytes 4194336 | tf_op jit(solution)/shard_map/ppermute | solution.py:189
  55.9 4.4 %other.1 = f32[192,256]{1,0:T(8,128)} custom-call(s32[16]{0:T(128)S(1)} %broadcast_multiply_fusion.place_ref, bf16[1344,512]{1,0:T(8,128)(2,1)S(1)} %get-tuple-element.80.refs_0_, bf16[1728,512]{1,0:T(8,128)(2,1)S(1)} %get-tuple-element.81.refs_1_, bf16[256,8192]{1,0:T(8,128)(2,1)} %collective-permute-done.19.refs_2_), custom_call_target="tpu_custom_call" | custom-call | tf_op jit(solution)/shard_map/other/pallas_call | solution.py:88
  60.3 0.1 collective-permute-start.20
  60.4 0.7 reduce_max.9
  63.6 0.2 fusion.13.place_ref
  63.8 3.7 %base.1.own_ref = f32[192,256]{1,0:T(8,128)S(1)} custom-call(s32[16]{0:T(128)S(1)} %broadcast_multiply_fusion.place_ref, bf16[1344,512]{1,0:T(8,128)(2,1)S(1)} %get-tuple-element.80.refs_0_, bf16[1728,512]{1,0:T(8,128)(2,1)S(1)} %get-tuple-element.81.refs_1_, bf16[256,8192]{1,0:T(8,128)(2,1)} %refs_2_.1), custom_call_target="tpu_custom_call" | custom-call | tf_op jit(solution)/shard_map/base/pallas_call | solution.py:88
  67.6 2.2 %finish.1 = bf16[3,2,64,256]{3,2,1,0:T(8,128)(2,1)} custom-call(s32[1]{0:T(128)} %bitcast.1.core_ref, s32[384,1]{1,0:T(8,128)S(1)} %fusion.13.place_ref, bf16[1024,256]{1,0:T(8,128)(2,1)} %bitcast.24.value_ref, f32[192,256]{1,0:T(8,128)S(1)} %base.1.own_ref, f32[192,256]{1,0:T(8,128)} %collective-permute-done.20.got_ref, ...), custom_call_target="tpu_custom_call" | custom-call | tf_op jit(solution)/shard_map/finish/pallas_call | solution.py:165
  (44 shorter events, 0.6 us)
Async XLA Ops:
  1.0 1.5 %collective-permute-start = (bf16[192,256]{1,0:T(8,128)(2,1)S(1)}, bf16[192,256]{1,0:T(8,128)(2,1)S(1)}, u32[]{:S(2)}, u32[]{:S(2)}) collective-permute-start(bf16[192,256]{1,0:T(8,128)(2,1)S(1)} %bitcast.44), channel_id=1, source_target_pairs={{0,1},{1,0},{2,3},{3,2},{4,5},{5,4},{6,7},{7,6},{8,9},{9,8},{10,11... | collective-permute-start | bytes 294920 | tf_op jit(solution)/shard_map/ppermute | solution.py:189
  2.5 37.4 %copy-start.3 = (bf16[192,512]{1,0:T(8,128)(2,1)}, bf16[192,512]{1,0:T(8,128)(2,1)S(1)}, u32[]{:S(2)}) copy-start(bf16[192,512]{1,0:T(8,128)(2,1)S(1)} %maximum_select_fusion.refs_0_) | copy-start | bytes 589828
  2.5 15.5 %collective-permute-start.12 = (bf16[128,8192]{1,0:T(8,128)(2,1)}, bf16[128,8192]{1,0:T(8,128)(2,1)}, u32[]{:S(2)}, u32[]{:S(2)}) collective-permute-start(bf16[128,8192]{1,0:T(8,128)(2,1)} %bitcast.38), channel_id=1, source_target_pairs={{0,1},{1,0},{2,3},{3,2},{4,5},{5,4},{6,7},{7,6},{8,9},{9,8},{10,11... | collective-permute-start | bytes 6291464 | tf_op jit(solution)/shard_map/ppermute | solution.py:189
  2.9 15.5 %collective-permute-start.6 = (bf16[128,8192]{1,0:T(8,128)(2,1)}, bf16[128,8192]{1,0:T(8,128)(2,1)S(1)}, u32[]{:S(2)}, u32[]{:S(2)}) collective-permute-start(bf16[128,8192]{1,0:T(8,128)(2,1)} %bitcast.35), channel_id=1, source_target_pairs={{0,1},{1,0},{2,3},{3,2},{4,5},{5,4},{6,7},{7,6},{8,9},{9,8},{10,11... | collective-permute-start | bytes 6291464 | tf_op jit(solution)/shard_map/ppermute | solution.py:189
  4.7 8.1 %collective-permute-start.2 = (bf16[192,512]{1,0:T(8,128)(2,1)S(1)}, bf16[192,512]{1,0:T(8,128)(2,1)S(1)}, u32[]{:S(2)}, u32[]{:S(2)}) collective-permute-start(bf16[192,512]{1,0:T(8,128)(2,1)S(1)} %maximum_select_fusion.refs_0_), channel_id=1, source_target_pairs={{0,2},{1,3},{2,0},{3,1},{4,6},{5,7},{6,4},{7,5},{8,10},{9,11},{10,... | collective-permute-start | bytes 589832 | tf_op jit(solution)/shard_map/ppermute | solution.py:186
  7.6 6.7 %collective-permute-start.3 = (bf16[192,512]{1,0:T(8,128)(2,1)S(1)}, bf16[192,512]{1,0:T(8,128)(2,1)S(1)}, u32[]{:S(2)}, u32[]{:S(2)}) collective-permute-start(bf16[192,512]{1,0:T(8,128)(2,1)S(1)} %maximum_select_fusion.refs_0_), channel_id=1, source_target_pairs={{0,4},{1,5},{2,6},{3,7},{4,0},{5,1},{6,2},{7,3},{8,12},{9,13},{10,... | collective-permute-start | bytes 589832 | tf_op jit(solution)/shard_map/ppermute | solution.py:186
  9.2 8.3 %collective-permute-start.1 = (bf16[192,512]{1,0:T(8,128)(2,1)S(1)}, bf16[192,512]{1,0:T(8,128)(2,1)S(1)}, u32[]{:S(2)}, u32[]{:S(2)}) collective-permute-start(bf16[192,512]{1,0:T(8,128)(2,1)S(1)} %maximum_select_fusion.refs_0_), channel_id=1, source_target_pairs={{0,8},{1,9},{2,10},{3,11},{4,12},{5,13},{6,14},{7,15},{8,16},{9,17... | collective-permute-start | bytes 589832 | tf_op jit(solution)/shard_map/ppermute | solution.py:186
  17.4 6.4 %collective-permute-start.14 = (bf16[192,512]{1,0:T(8,128)(2,1)S(1)}, bf16[192,512]{1,0:T(8,128)(2,1)S(1)}, u32[]{:S(2)}, u32[]{:S(2)}) collective-permute-start(bf16[192,512]{1,0:T(8,128)(2,1)S(1)} %collective-permute-done.1.refs_4_), channel_id=1, source_target_pairs={{0,2},{1,3},{2,0},{3,1},{4,6},{5,7},{6,4},{7,5},{8,10},{9,11},{10,... | collective-permute-start | bytes 589832 | tf_op jit(solution)/shard_map/ppermute | solution.py:186
  18.0 9.3 %collective-permute-start.11 = (bf16[192,512]{1,0:T(8,128)(2,1)S(1)}, bf16[192,512]{1,0:T(8,128)(2,1)S(1)}, u32[]{:S(2)}, u32[]{:S(2)}) collective-permute-start(bf16[192,512]{1,0:T(8,128)(2,1)S(1)} %collective-permute-done.1.refs_4_), channel_id=1, source_target_pairs={{0,8},{1,9},{2,10},{3,11},{4,12},{5,13},{6,14},{7,15},{8,16},{9,17... | collective-permute-start | bytes 589832 | tf_op jit(solution)/shard_map/ppermute | solution.py:186
  18.0 9.3 %collective-permute-start.13 = (bf16[192,512]{1,0:T(8,128)(2,1)S(1)}, bf16[192,512]{1,0:T(8,128)(2,1)S(1)}, u32[]{:S(2)}, u32[]{:S(2)}) collective-permute-start(bf16[192,512]{1,0:T(8,128)(2,1)S(1)} %collective-permute-done.2.refs_1_), channel_id=1, source_target_pairs={{0,4},{1,5},{2,6},{3,7},{4,0},{5,1},{6,2},{7,3},{8,12},{9,13},{10,... | collective-permute-start | bytes 589832 | tf_op jit(solution)/shard_map/ppermute | solution.py:186
  18.5 10.8 %collective-permute-start.7 = (bf16[192,512]{1,0:T(8,128)(2,1)S(1)}, bf16[192,512]{1,0:T(8,128)(2,1)S(1)}, u32[]{:S(2)}, u32[]{:S(2)}) collective-permute-start(bf16[192,512]{1,0:T(8,128)(2,1)S(1)} %maximum_select_fusion.refs_0_), channel_id=1, source_target_pairs={{0,24},{1,25},{2,26},{3,27},{4,28},{5,29},{6,30},{7,31},{8,0},{9,1... | collective-permute-start | bytes 589832 | tf_op jit(solution)/shard_map/ppermute | solution.py:186
  22.3 7.7 %collective-permute-start.4 = (bf16[192,512]{1,0:T(8,128)(2,1)S(1)}, bf16[192,512]{1,0:T(8,128)(2,1)S(1)}, u32[]{:S(2)}, u32[]{:S(2)}) collective-permute-start(bf16[192,512]{1,0:T(8,128)(2,1)S(1)} %collective-permute-done.1.refs_4_), channel_id=1, source_target_pairs={{0,4},{1,5},{2,6},{3,7},{4,0},{5,1},{6,2},{7,3},{8,12},{9,13},{10,... | collective-permute-start | bytes 589832 | tf_op jit(solution)/shard_map/ppermute | solution.py:186
  27.2 7.8 %collective-permute-start.15 = (bf16[192,512]{1,0:T(8,128)(2,1)S(1)}, bf16[192,512]{1,0:T(8,128)(2,1)S(1)}, u32[]{:S(2)}, u32[]{:S(2)}) collective-permute-start(bf16[192,512]{1,0:T(8,128)(2,1)S(1)} %collective-permute-done.11.refs_5_), channel_id=1, source_target_pairs={{0,2},{1,3},{2,0},{3,1},{4,6},{5,7},{6,4},{7,5},{8,10},{9,11},{10,... | collective-permute-start | bytes 589832 | tf_op jit(solution)/shard_map/ppermute | solution.py:186
  28.7 7.6 %collective-permute-start.16 = (bf16[192,512]{1,0:T(8,128)(2,1)S(1)}, bf16[192,512]{1,0:T(8,128)(2,1)S(1)}, u32[]{:S(2)}, u32[]{:S(2)}) collective-permute-start(bf16[192,512]{1,0:T(8,128)(2,1)S(1)} %collective-permute-done.11.refs_5_), channel_id=1, source_target_pairs={{0,4},{1,5},{2,6},{3,7},{4,0},{5,1},{6,2},{7,3},{8,12},{9,13},{10,... | collective-permute-start | bytes 589832 | tf_op jit(solution)/shard_map/ppermute | solution.py:186
  29.2 8.2 %collective-permute-start.8 = (bf16[192,512]{1,0:T(8,128)(2,1)S(1)}, bf16[192,512]{1,0:T(8,128)(2,1)S(1)}, u32[]{:S(2)}, u32[]{:S(2)}) collective-permute-start(bf16[192,512]{1,0:T(8,128)(2,1)S(1)} %collective-permute-done.7.refs_1_), channel_id=1, source_target_pairs={{0,2},{1,3},{2,0},{3,1},{4,6},{5,7},{6,4},{7,5},{8,10},{9,11},{10,... | collective-permute-start | bytes 589832 | tf_op jit(solution)/shard_map/ppermute | solution.py:186
  30.0 14.9 %collective-permute-start.5 = (bf16[192,512]{1,0:T(8,128)(2,1)S(1)}, bf16[192,512]{1,0:T(8,128)(2,1)S(1)}, u32[]{:S(2)}, u32[]{:S(2)}) collective-permute-start(bf16[192,512]{1,0:T(8,128)(2,1)S(1)} %collective-permute-done.4.refs_6_), channel_id=1, source_target_pairs={{0,2},{1,3},{2,0},{3,1},{4,6},{5,7},{6,4},{7,5},{8,10},{9,11},{10,... | collective-permute-start | bytes 589832 | tf_op jit(solution)/shard_map/ppermute | solution.py:186
  31.5 13.4 %collective-permute-start.9 = (bf16[192,512]{1,0:T(8,128)(2,1)S(1)}, bf16[192,512]{1,0:T(8,128)(2,1)S(1)}, u32[]{:S(2)}, u32[]{:S(2)}) collective-permute-start(bf16[192,512]{1,0:T(8,128)(2,1)S(1)} %collective-permute-done.7.refs_1_), channel_id=1, source_target_pairs={{0,4},{1,5},{2,6},{3,7},{4,0},{5,1},{6,2},{7,3},{8,12},{9,13},{10,... | collective-permute-start | bytes 589832 | tf_op jit(solution)/shard_map/ppermute | solution.py:186
  35.1 9.8 %collective-permute-start.17 = (bf16[96,512]{1,0:T(8,128)(2,1)S(1)}, bf16[96,512]{1,0:T(8,128)(2,1)S(1)}, u32[]{:S(2)}, u32[]{:S(2)}) collective-permute-start(bf16[96,512]{1,0:T(8,128)(2,1)S(1)} %slice.25), channel_id=1, source_target_pairs={{0,4},{1,5},{2,6},{3,7},{4,0},{5,1},{6,2},{7,3},{8,12},{9,13},{10,... | collective-permute-start | bytes 294920 | tf_op jit(solution)/shard_map/ppermute | solution.py:186
  36.4 8.5 %collective-permute-start.18 = (bf16[96,512]{1,0:T(8,128)(2,1)S(1)}, bf16[96,512]{1,0:T(8,128)(2,1)S(1)}, u32[]{:S(2)}, u32[]{:S(2)}) collective-permute-start(bf16[96,512]{1,0:T(8,128)(2,1)S(1)} %slice.26), channel_id=1, source_target_pairs={{0,2},{1,3},{2,0},{3,1},{4,6},{5,7},{6,4},{7,5},{8,10},{9,11},{10,... | collective-permute-start | bytes 294920 | tf_op jit(solution)/shard_map/ppermute | solution.py:186
  37.4 7.5 %collective-permute-start.10 = (bf16[192,512]{1,0:T(8,128)(2,1)S(1)}, bf16[192,512]{1,0:T(8,128)(2,1)S(1)}, u32[]{:S(2)}, u32[]{:S(2)}) collective-permute-start(bf16[192,512]{1,0:T(8,128)(2,1)S(1)} %collective-permute-done.8.refs_2_), channel_id=1, source_target_pairs={{0,4},{1,5},{2,6},{3,7},{4,0},{5,1},{6,2},{7,3},{8,12},{9,13},{10,... | collective-permute-start | bytes 589832 | tf_op jit(solution)/shard_map/ppermute | solution.py:186
  39.9 1.6 %copy-start = (bf16[2,64,8192]{2,1,0:T(8,128)(2,1)S(1)}, bf16[2,64,8192]{2,1,0:T(8,128)(2,1)}, u32[]{:S(2)}) copy-start(bf16[2,64,8192]{2,1,0:T(8,128)(2,1)} %param.10) | copy-start | bytes 6291460
  41.5 0.9 %copy-start.4 = (bf16[192,512]{1,0:T(8,128)(2,1)S(1)}, bf16[192,512]{1,0:T(8,128)(2,1)}, u32[]{:S(2)}) copy-start(bf16[192,512]{1,0:T(8,128)(2,1)} %copy-done.3) | copy-start | bytes 589828
  42.4 2.5 %copy-start.1 = (bf16[2,64,8192]{2,1,0:T(8,128)(2,1)S(1)}, bf16[2,64,8192]{2,1,0:T(8,128)(2,1)}, u32[]{:S(2)}) copy-start(bf16[2,64,8192]{2,1,0:T(8,128)(2,1)} %param.10) | copy-start | bytes 6291460
  44.9 1.7 %copy-start.5 = (bf16[2,64,8192]{2,1,0:T(8,128)(2,1)S(1)}, bf16[2,64,8192]{2,1,0:T(8,128)(2,1)}, u32[]{:S(2)}) copy-start(bf16[2,64,8192]{2,1,0:T(8,128)(2,1)} %param.11) | copy-start | bytes 6291460
  46.6 1.0 %copy-start.6 = (bf16[192,256]{1,0:T(8,128)(2,1)}, bf16[192,256]{1,0:T(8,128)(2,1)S(1)}, u32[]{:S(2)}) copy-start(bf16[192,256]{1,0:T(8,128)(2,1)S(1)} %get-tuple-element.170.low_ref) | copy-start | bytes 294916
  47.5 0.8 %copy-start.2 = (bf16[32,32,256]{2,1,0:T(8,128)(2,1)}, bf16[32,32,256]{2,1,0:T(8,128)(2,1)S(1)}, u32[]{:S(2)}) copy-start(bf16[32,32,256]{2,1,0:T(8,128)(2,1)S(1)} %again.2) | copy-start | bytes 1572868
  48.4 7.5 %collective-permute-start.19 = (bf16[256,8192]{1,0:T(8,128)(2,1)}, bf16[256,8192]{1,0:T(8,128)(2,1)}, u32[]{:S(2)}, u32[]{:S(2)}) collective-permute-start(bf16[256,8192]{1,0:T(8,128)(2,1)} %refs_2_.1), channel_id=1, source_target_pairs={{0,1},{1,0},{2,3},{3,2},{4,5},{5,4},{6,7},{7,6},{8,9},{9,8},{10,11... | collective-permute-start | bytes 12582920 | tf_op jit(solution)/shard_map/ppermute | solution.py:189
  48.4 19.2 %all-to-all-start.1 = ((bf16[32,32,256]{2,1,0:T(8,128)(2,1)}), bf16[32,32,256]{2,1,0:T(8,128)(2,1)}, u32[]{:S(2)}, u32[]{:S(2)}) async-start(bf16[32,32,256]{2,1,0:T(8,128)(2,1)} %copy-done.2), calls=%async_computation.1 | async-start | bytes 1048576 | tf_op jit(solution)/shard_map/all_to_all | solution.py:276
  60.3 7.3 %collective-permute-start.20 = (f32[192,256]{1,0:T(8,128)}, f32[192,256]{1,0:T(8,128)}, u32[]{:S(2)}, u32[]{:S(2)}) collective-permute-start(f32[192,256]{1,0:T(8,128)} %other.1), channel_id=1, source_target_pairs={{0,1},{1,0},{2,3},{3,2},{4,5},{5,4},{6,7},{7,6},{8,9},{9,8},{10,11... | collective-permute-start | bytes 589832 | tf_op jit(solution)/shard_map/ppermute | solution.py:189

commit v5 on v4

--- a/solution.py
+++ b/solution.py
@@ -242,7 +242,7 @@
         if number == 1:
             ready = after(ready, x[0], y[0])
         if number == depth - 1:
-            ready = after(ready, far[0][0], x[1])
+            ready = after(ready, far[0][0])
         x[k], y[k] = move(ready, flip(1)), move(ready, flip(2))
         if number < depth - 1:
             far[k] = (move(x[k], flip(2)) if number % 2 == 0 else move(y[k], flip(1)),)

time: 70.3 us -> 70 us (level)
  starting transfers between devices: 26.5 us -> 24.2 us
  waiting for transfers between devices: 18.1 us -> 20.1 us
    ppermute x16, starting transfers between devices: 21.9 us -> 19.6 us  [move(): return lax.ppermute(value, 'wide', pairs)]
    ppermute x16, waiting for transfers between devices: 13.1 us -> 15.1 us  [move(): return lax.ppermute(value, 'wide', pairs)]
  transfers between devices with their start and end apart: 22 -> 22, of which waited for: 9 -> 8; matrix products, arithmetic and copies ran while one was open for 4% -> 4% of each run, Pallas kernels for 15% -> 15%
where the time goes in v5:
time: 70 us; the launch traced here: 69.6 us
  starting transfers between devices  24.2 us (35%)
  waiting for transfers between devices  20.1 us (29%)
  Pallas kernels  15.3 us (22%)
  local copies, waits for them, and re-layouts  4.94 us (7%)
  between operations  2.76 us (4%)
  other arithmetic  2.21 us (3%)
    ppermute x16, starting transfers between devices, move(): return lax.ppermute(value, 'wide', pairs)  19.6 us
    ppermute x16, waiting for transfers between devices, move(): return lax.ppermute(value, 'wide', pairs)  15.1 us
    pallas_call x2, Pallas kernels, base(): pl.pallas_call(base_kernel, out_shape=jax.ShapeDtypeStruct((rows, table.s...  8.1 us
    ppermute x5, waiting for transfers between devices, swap(): return lax.ppermute(value, 'wide', [(i, i ^ 1) for i in range(wide)])  5 us
    unnamed x14, local copies, waits for them, and re-layouts  3.34 us
    all_to_all x1, starting transfers between devices, give_back(): lax.all_to_all(sent, 'wide', split_axis=0, concat_axis=0, tiled=True)  3.33 us
    pallas_call x1, Pallas kernels, first(): pl.pallas_call(functools.partial(first_kernel, whole), out_shape=(shape,...  2.42 us
    pallas_call x1, Pallas kernels, finish(): pl.pallas_call(last_kernel, out_shape=jax.ShapeDtypeStruct(shape, BF16),...  2.24 us
  transfers between devices with their start and end apart: 22, of which 8 were waited for; matrix products, arithmetic and copies ran while one was open for 4% of the time, Pallas kernels for 15%

profile of v5, /device:TPU:0, one launch (start us, length us, event | category | flops | bytes accessed | tf_op | source)
XLA Modules:
  0.0 69.6 jit_solution(7666040611369563252)
XLA Ops:
  0.0 1.0 %constant_dynamic-slice_fusion.1 = (bf16[3,1,64,256]{3,2,1,0:T(8,128)(2,1)S(1)}, bf16[3,1,64,256]{3,2,1,0:T(8,128)(2,1)S(1)}) fusion(bf16[3,2,64,256]{3,2,1,0:T(8,128)(2,1)} %bitcast.43, s32[]{:T(128)S(6)} %select_n.252, s32[]{:T(128)S(6)} %select_n.260), kind=kLoop, calls=%fused_computation.101 | loop fusion | bytes 393224 | tf_op jit(solution)/shard_map/jit(dynamic_index_in_dim)/dynamic_slice | solution.py:203
  1.0 0.5 collective-permute-start
  1.5 0.9 %collective-permute-done = bf16[192,256]{1,0:T(8,128)(2,1)S(1)} collective-permute-done((bf16[192,256]{1,0:T(8,128)(2,1)S(1)}, bf16[192,256]{1,0:T(8,128)(2,1)S(1)}, u32[]{:S(2)}, u32[]{:S(2)}) %collective-permute-start) | collective-permute-done | bytes 98336 | tf_op jit(solution)/shard_map/ppermute | solution.py:189
  2.5 0.4 collective-permute-start.12
  2.9 0.2 collective-permute-start.6
  3.1 0.8 %select_reduce_fusion = s32[384]{0:T(512)S(1)} fusion(s32[64]{0:T(128)} %param.12, s32[384]{0:T(512)} %bitcast.45), kind=kLoop, calls=%fused_computation.45 | loop fusion | flops 73344 | bytes 3328 | tf_op jit(solution)/shard_map/reduce_sum | solution.py:260
  3.9 0.1 stack.83
  4.0 0.2 convert_reduce_fusion
  4.2 0.1 stack.84
  4.5 0.1 stack.103
  4.6 0.1 stack.95
  4.7 2.9 %collective-permute-start.2 = (bf16[192,512]{1,0:T(8,128)(2,1)S(1)}, bf16[192,512]{1,0:T(8,128)(2,1)S(1)}, u32[]{:S(2)}, u32[]{:S(2)}) collective-permute-start(bf16[192,512]{1,0:T(8,128)(2,1)S(1)} %maximum_select_fusion.refs_0_), channel_id=1, source_target_pairs={{0,2},{1,3},{2,0},{3,1},{4,6},{5,7},{6,4},{7,5},{8,10},{9,11},{10,... | collective-permute-start | bytes 589832 | tf_op jit(solution)/shard_map/ppermute | solution.py:186
  7.6 1.5 %collective-permute-start.3 = (bf16[192,512]{1,0:T(8,128)(2,1)S(1)}, bf16[192,512]{1,0:T(8,128)(2,1)S(1)}, u32[]{:S(2)}, u32[]{:S(2)}) collective-permute-start(bf16[192,512]{1,0:T(8,128)(2,1)S(1)} %maximum_select_fusion.refs_0_), channel_id=1, source_target_pairs={{0,4},{1,5},{2,6},{3,7},{4,0},{5,1},{6,2},{7,3},{8,12},{9,13},{10,... | collective-permute-start | bytes 589832 | tf_op jit(solution)/shard_map/ppermute | solution.py:186
  9.2 1.6 %collective-permute-start.1 = (bf16[192,512]{1,0:T(8,128)(2,1)S(1)}, bf16[192,512]{1,0:T(8,128)(2,1)S(1)}, u32[]{:S(2)}, u32[]{:S(2)}) collective-permute-start(bf16[192,512]{1,0:T(8,128)(2,1)S(1)} %maximum_select_fusion.refs_0_), channel_id=1, source_target_pairs={{0,8},{1,9},{2,10},{3,11},{4,12},{5,13},{6,14},{7,15},{8,16},{9,17... | collective-permute-start | bytes 589832 | tf_op jit(solution)/shard_map/ppermute | solution.py:186
  10.7 0.1 compare_convert_fusion.1.refs_12_
  10.8 6.6 %collective-permute-done.1.refs_4_ = bf16[192,512]{1,0:T(8,128)(2,1)S(1)} collective-permute-done((bf16[192,512]{1,0:T(8,128)(2,1)S(1)}, bf16[192,512]{1,0:T(8,128)(2,1)S(1)}, u32[]{:S(2)}, u32[]{:S(2)}) %collective-permute-start.1) | collective-permute-done | bytes 196640 | tf_op jit(solution)/shard_map/ppermute | solution.py:186
  17.4 0.6 collective-permute-start.13
  18.0 3.8 %collective-permute-start.7 = (bf16[192,512]{1,0:T(8,128)(2,1)S(1)}, bf16[192,512]{1,0:T(8,128)(2,1)S(1)}, u32[]{:S(2)}, u32[]{:S(2)}) collective-permute-start(bf16[192,512]{1,0:T(8,128)(2,1)S(1)} %maximum_select_fusion.refs_0_), channel_id=1, source_target_pairs={{0,24},{1,25},{2,26},{3,27},{4,28},{5,29},{6,30},{7,31},{8,0},{9,1... | collective-permute-start | bytes 589832 | tf_op jit(solution)/shard_map/ppermute | solution.py:186
  21.8 0.5 collective-permute-start.18
  22.4 1.5 %collective-permute-start.4 = (bf16[192,512]{1,0:T(8,128)(2,1)S(1)}, bf16[192,512]{1,0:T(8,128)(2,1)S(1)}, u32[]{:S(2)}, u32[]{:S(2)}) collective-permute-start(bf16[192,512]{1,0:T(8,128)(2,1)S(1)} %collective-permute-done.1.refs_4_), channel_id=1, source_target_pairs={{0,4},{1,5},{2,6},{3,7},{4,0},{5,1},{6,2},{7,3},{8,12},{9,13},{10,... | collective-permute-start | bytes 589832 | tf_op jit(solution)/shard_map/ppermute | solution.py:186
  23.9 3.0 %collective-permute-done.11.refs_5_ = bf16[192,512]{1,0:T(8,128)(2,1)S(1)} collective-permute-done((bf16[192,512]{1,0:T(8,128)(2,1)S(1)}, bf16[192,512]{1,0:T(8,128)(2,1)S(1)}, u32[]{:S(2)}, u32[]{:S(2)}) %collective-permute-start.11) | collective-permute-done | bytes 196640 | tf_op jit(solution)/shard_map/ppermute | solution.py:186
  26.9 0.5 collective-permute-start.14
  27.5 0.6 collective-permute-start.15
  28.1 1.4 %collective-permute-start.8 = (bf16[192,512]{1,0:T(8,128)(2,1)S(1)}, bf16[192,512]{1,0:T(8,128)(2,1)S(1)}, u32[]{:S(2)}, u32[]{:S(2)}) collective-permute-start(bf16[192,512]{1,0:T(8,128)(2,1)S(1)} %collective-permute-done.7.refs_1_), channel_id=1, source_target_pairs={{0,2},{1,3},{2,0},{3,1},{4,6},{5,7},{6,4},{7,5},{8,10},{9,11},{10,... | collective-permute-start | bytes 589832 | tf_op jit(solution)/shard_map/ppermute | solution.py:186
  29.5 0.2 collective-permute-done.4.refs_6_
  29.7 1.5 %collective-permute-start.5 = (bf16[192,512]{1,0:T(8,128)(2,1)S(1)}, bf16[192,512]{1,0:T(8,128)(2,1)S(1)}, u32[]{:S(2)}, u32[]{:S(2)}) collective-permute-start(bf16[192,512]{1,0:T(8,128)(2,1)S(1)} %collective-permute-done.4.refs_6_), channel_id=1, source_target_pairs={{0,2},{1,3},{2,0},{3,1},{4,6},{5,7},{6,4},{7,5},{8,10},{9,11},{10,... | collective-permute-start | bytes 589832 | tf_op jit(solution)/shard_map/ppermute | solution.py:186
  31.2 3.6 %collective-permute-done.14.refs_6_ = bf16[192,512]{1,0:T(8,128)(2,1)S(1)} collective-permute-done((bf16[192,512]{1,0:T(8,128)(2,1)S(1)}, bf16[192,512]{1,0:T(8,128)(2,1)S(1)}, u32[]{:S(2)}, u32[]{:S(2)}) %collective-permute-start.14) | collective-permute-done | bytes 196640 | tf_op jit(solution)/shard_map/ppermute | solution.py:186
  34.8 0.4 collective-permute-start.9
  35.2 1.7 %collective-permute-start.16 = (bf16[96,512]{1,0:T(8,128)(2,1)S(1)}, bf16[96,512]{1,0:T(8,128)(2,1)S(1)}, u32[]{:S(2)}, u32[]{:S(2)}) collective-permute-start(bf16[96,512]{1,0:T(8,128)(2,1)S(1)} %slice.25), channel_id=1, source_target_pairs={{0,4},{1,5},{2,6},{3,7},{4,0},{5,1},{6,2},{7,3},{8,12},{9,13},{10,... | collective-permute-start | bytes 294920 | tf_op jit(solution)/shard_map/ppermute | solution.py:186
  36.9 0.6 collective-permute-start.17
  37.5 1.4 %collective-permute-done.8.refs_2_ = bf16[192,512]{1,0:T(8,128)(2,1)S(1)} collective-permute-done((bf16[192,512]{1,0:T(8,128)(2,1)S(1)}, bf16[192,512]{1,0:T(8,128)(2,1)S(1)}, u32[]{:S(2)}, u32[]{:S(2)}) %collective-permute-start.8) | collective-permute-done | bytes 196640 | tf_op jit(solution)/shard_map/ppermute | solution.py:186
  38.9 0.5 collective-permute-start.10
  39.4 1.6 %copy-done = bf16[2,64,8192]{2,1,0:T(8,128)(2,1)S(1)} copy-done((bf16[2,64,8192]{2,1,0:T(8,128)(2,1)S(1)}, bf16[2,64,8192]{2,1,0:T(8,128)(2,1)}, u32[]{:S(2)}) %copy-start) | copy-done | bytes 2097176
  41.0 0.9 %copy-done.4 = bf16[192,512]{1,0:T(8,128)(2,1)S(1)} copy-done((bf16[192,512]{1,0:T(8,128)(2,1)S(1)}, bf16[192,512]{1,0:T(8,128)(2,1)}, u32[]{:S(2)}) %copy-start.4) | copy-done | bytes 196632
  41.9 2.4 %first.1 = (f32[192,128]{1,0:T(8,128)S(1)}, f32[192,128]{1,0:T(8,128)S(1)}, bf16[1344,512]{1,0:T(8,128)(2,1)S(1)}, bf16[128,8192]{1,0:T(8,128)(2,1)S(1)}, bf16[128,8192]{1,0:T(8,128)(2,1)S(1)}) custom-call(s32[7]{0:T(128)S(1)} %broadcast_multiply_fusion.1.place_ref, bf16[192,512]{1,0:T(8,128)(2,1)S(1)} %copy-done.4, ...), custom_call_target="tpu_custom_call" | custom-call | tf_op jit(solution)/shard_map/first/pallas_call | solution.py:63
  44.4 0.2 collective-permute-done.10.refs_4_
  44.6 1.6 %owner.1 = (bf16[192,256]{1,0:T(8,128)(2,1)S(1)}, bf16[1728,512]{1,0:T(8,128)(2,1)S(1)}) custom-call(s32[9]{0:T(128)S(1)} %broadcast_multiply_fusion.2.place_ref, bf16[192,512]{1,0:T(8,128)(2,1)S(1)} %collective-permute-done.5.refs_0_, bf16[192,512]{1,0:T(8,128)(2,1)S(1)} %collective-permute-done.7.refs_1_, ...), custom_call_target="tpu_custom_call" | custom-call | tf_op jit(solution)/shard_map/owner/pallas_call | solution.py:118
  46.3 0.9 %again.2 = bf16[32,32,256]{2,1,0:T(8,128)(2,1)S(1)} custom-call(bf16[32,192]{1,0:T(8,128)(2,1)S(1)} %fusion.22.pick_ref, bf16[192,256]{1,0:T(8,128)(2,1)S(1)} %get-tuple-element.170.low_ref, bf16[128,8192]{1,0:T(8,128)(2,1)S(1)} %bitcast.40, bf16[128,8192]{1,0:T(8,128)(2,1)S(1)} %get-tuple-element.79.e1_ref), custom_call_target="tpu_custom_call" | custom-call | tf_op jit(solution)/shard_map/again/pallas_call | solution.py:136
  47.2 0.8 %copy-done.2 = bf16[32,32,256]{2,1,0:T(8,128)(2,1)} copy-done((bf16[32,32,256]{2,1,0:T(8,128)(2,1)}, bf16[32,32,256]{2,1,0:T(8,128)(2,1)S(1)}, u32[]{:S(2)}) %copy-start.2) | copy-done | bytes 524312
  48.0 3.3 %all-to-all-start.1 = ((bf16[32,32,256]{2,1,0:T(8,128)(2,1)}), bf16[32,32,256]{2,1,0:T(8,128)(2,1)}, u32[]{:S(2)}, u32[]{:S(2)}) async-start(bf16[32,32,256]{2,1,0:T(8,128)(2,1)} %copy-done.2), calls=%async_computation.1 | async-start | bytes 1048576 | tf_op jit(solution)/shard_map/all_to_all | solution.py:276
  51.4 0.1 stack.104
  51.5 4.0 %collective-permute-done.19.refs_2_ = bf16[256,8192]{1,0:T(8,128)(2,1)} collective-permute-done((bf16[256,8192]{1,0:T(8,128)(2,1)}, bf16[256,8192]{1,0:T(8,128)(2,1)}, u32[]{:S(2)}, u32[]{:S(2)}) %collective-permute-start.19) | collective-permute-done | bytes 4194336 | tf_op jit(solution)/shard_map/ppermute | solution.py:189
  55.5 4.4 %other.1 = f32[192,256]{1,0:T(8,128)} custom-call(s32[16]{0:T(128)S(1)} %broadcast_multiply_fusion.place_ref, bf16[1344,512]{1,0:T(8,128)(2,1)S(1)} %get-tuple-element.80.refs_0_, bf16[1728,512]{1,0:T(8,128)(2,1)S(1)} %get-tuple-element.81.refs_1_, bf16[256,8192]{1,0:T(8,128)(2,1)} %collective-permute-done.19.refs_2_), custom_call_target="tpu_custom_call" | custom-call | tf_op jit(solution)/shard_map/other/pallas_call | solution.py:88
  59.9 0.1 collective-permute-start.20
  60.1 0.7 reduce_max.9
  63.3 0.2 fusion.13.place_ref
  63.5 3.7 %base.1.own_ref = f32[192,256]{1,0:T(8,128)S(1)} custom-call(s32[16]{0:T(128)S(1)} %broadcast_multiply_fusion.place_ref, bf16[1344,512]{1,0:T(8,128)(2,1)S(1)} %get-tuple-element.80.refs_0_, bf16[1728,512]{1,0:T(8,128)(2,1)S(1)} %get-tuple-element.81.refs_1_, bf16[256,8192]{1,0:T(8,128)(2,1)} %refs_2_.1), custom_call_target="tpu_custom_call" | custom-call | tf_op jit(solution)/shard_map/base/pallas_call | solution.py:88
  67.3 2.2 %finish.1 = bf16[3,2,64,256]{3,2,1,0:T(8,128)(2,1)} custom-call(s32[1]{0:T(128)} %bitcast.1.core_ref, s32[384,1]{1,0:T(8,128)S(1)} %fusion.13.place_ref, bf16[1024,256]{1,0:T(8,128)(2,1)} %bitcast.24.value_ref, f32[192,256]{1,0:T(8,128)S(1)} %base.1.own_ref, f32[192,256]{1,0:T(8,128)} %collective-permute-done.20.got_ref, ...), custom_call_target="tpu_custom_call" | custom-call | tf_op jit(solution)/shard_map/finish/pallas_call | solution.py:165
  (44 shorter events, 0.5 us)
Async XLA Ops:
  1.0 1.5 %collective-permute-start = (bf16[192,256]{1,0:T(8,128)(2,1)S(1)}, bf16[192,256]{1,0:T(8,128)(2,1)S(1)}, u32[]{:S(2)}, u32[]{:S(2)}) collective-permute-start(bf16[192,256]{1,0:T(8,128)(2,1)S(1)} %bitcast.44), channel_id=1, source_target_pairs={{0,1},{1,0},{2,3},{3,2},{4,5},{5,4},{6,7},{7,6},{8,9},{9,8},{10,11... | collective-permute-start | bytes 294920 | tf_op jit(solution)/shard_map/ppermute | solution.py:189
  2.5 36.9 %copy-start.3 = (bf16[192,512]{1,0:T(8,128)(2,1)}, bf16[192,512]{1,0:T(8,128)(2,1)S(1)}, u32[]{:S(2)}) copy-start(bf16[192,512]{1,0:T(8,128)(2,1)S(1)} %maximum_select_fusion.refs_0_) | copy-start | bytes 589828
  2.5 14.9 %collective-permute-start.12 = (bf16[128,8192]{1,0:T(8,128)(2,1)}, bf16[128,8192]{1,0:T(8,128)(2,1)}, u32[]{:S(2)}, u32[]{:S(2)}) collective-permute-start(bf16[128,8192]{1,0:T(8,128)(2,1)} %bitcast.38), channel_id=1, source_target_pairs={{0,1},{1,0},{2,3},{3,2},{4,5},{5,4},{6,7},{7,6},{8,9},{9,8},{10,11... | collective-permute-start | bytes 6291464 | tf_op jit(solution)/shard_map/ppermute | solution.py:189
  2.9 15.1 %collective-permute-start.6 = (bf16[128,8192]{1,0:T(8,128)(2,1)}, bf16[128,8192]{1,0:T(8,128)(2,1)S(1)}, u32[]{:S(2)}, u32[]{:S(2)}) collective-permute-start(bf16[128,8192]{1,0:T(8,128)(2,1)} %bitcast.35), channel_id=1, source_target_pairs={{0,1},{1,0},{2,3},{3,2},{4,5},{5,4},{6,7},{7,6},{8,9},{9,8},{10,11... | collective-permute-start | bytes 6291464 | tf_op jit(solution)/shard_map/ppermute | solution.py:189
  4.7 12.7 %collective-permute-start.2 = (bf16[192,512]{1,0:T(8,128)(2,1)S(1)}, bf16[192,512]{1,0:T(8,128)(2,1)S(1)}, u32[]{:S(2)}, u32[]{:S(2)}) collective-permute-start(bf16[192,512]{1,0:T(8,128)(2,1)S(1)} %maximum_select_fusion.refs_0_), channel_id=1, source_target_pairs={{0,2},{1,3},{2,0},{3,1},{4,6},{5,7},{6,4},{7,5},{8,10},{9,11},{10,... | collective-permute-start | bytes 589832 | tf_op jit(solution)/shard_map/ppermute | solution.py:186
  7.6 9.8 %collective-permute-start.3 = (bf16[192,512]{1,0:T(8,128)(2,1)S(1)}, bf16[192,512]{1,0:T(8,128)(2,1)S(1)}, u32[]{:S(2)}, u32[]{:S(2)}) collective-permute-start(bf16[192,512]{1,0:T(8,128)(2,1)S(1)} %maximum_select_fusion.refs_0_), channel_id=1, source_target_pairs={{0,4},{1,5},{2,6},{3,7},{4,0},{5,1},{6,2},{7,3},{8,12},{9,13},{10,... | collective-permute-start | bytes 589832 | tf_op jit(solution)/shard_map/ppermute | solution.py:186
  9.2 8.3 %collective-permute-start.1 = (bf16[192,512]{1,0:T(8,128)(2,1)S(1)}, bf16[192,512]{1,0:T(8,128)(2,1)S(1)}, u32[]{:S(2)}, u32[]{:S(2)}) collective-permute-start(bf16[192,512]{1,0:T(8,128)(2,1)S(1)} %maximum_select_fusion.refs_0_), channel_id=1, source_target_pairs={{0,8},{1,9},{2,10},{3,11},{4,12},{5,13},{6,14},{7,15},{8,16},{9,17... | collective-permute-start | bytes 589832 | tf_op jit(solution)/shard_map/ppermute | solution.py:186
  17.4 9.5 %collective-permute-start.11 = (bf16[192,512]{1,0:T(8,128)(2,1)S(1)}, bf16[192,512]{1,0:T(8,128)(2,1)S(1)}, u32[]{:S(2)}, u32[]{:S(2)}) collective-permute-start(bf16[192,512]{1,0:T(8,128)(2,1)S(1)} %collective-permute-done.1.refs_4_), channel_id=1, source_target_pairs={{0,8},{1,9},{2,10},{3,11},{4,12},{5,13},{6,14},{7,15},{8,16},{9,17... | collective-permute-start | bytes 589832 | tf_op jit(solution)/shard_map/ppermute | solution.py:186
  17.4 9.5 %collective-permute-start.13 = (bf16[192,512]{1,0:T(8,128)(2,1)S(1)}, bf16[192,512]{1,0:T(8,128)(2,1)S(1)}, u32[]{:S(2)}, u32[]{:S(2)}) collective-permute-start(bf16[192,512]{1,0:T(8,128)(2,1)S(1)} %collective-permute-done.2.refs_1_), channel_id=1, source_target_pairs={{0,4},{1,5},{2,6},{3,7},{4,0},{5,1},{6,2},{7,3},{8,12},{9,13},{10,... | collective-permute-start | bytes 589832 | tf_op jit(solution)/shard_map/ppermute | solution.py:186
  18.0 10.1 %collective-permute-start.7 = (bf16[192,512]{1,0:T(8,128)(2,1)S(1)}, bf16[192,512]{1,0:T(8,128)(2,1)S(1)}, u32[]{:S(2)}, u32[]{:S(2)}) collective-permute-start(bf16[192,512]{1,0:T(8,128)(2,1)S(1)} %maximum_select_fusion.refs_0_), channel_id=1, source_target_pairs={{0,24},{1,25},{2,26},{3,27},{4,28},{5,29},{6,30},{7,31},{8,0},{9,1... | collective-permute-start | bytes 589832 | tf_op jit(solution)/shard_map/ppermute | solution.py:186
  21.8 15.1 %collective-permute-start.18 = (bf16[192,512]{1,0:T(8,128)(2,1)S(1)}, bf16[192,512]{1,0:T(8,128)(2,1)S(1)}, u32[]{:S(2)}, u32[]{:S(2)}) collective-permute-start(bf16[192,512]{1,0:T(8,128)(2,1)S(1)} %collective-permute-done.1.refs_4_), channel_id=1, source_target_pairs={{0,2},{1,3},{2,0},{3,1},{4,6},{5,7},{6,4},{7,5},{8,10},{9,11},{10,... | collective-permute-start | bytes 589832 | tf_op jit(solution)/shard_map/ppermute | solution.py:186
  22.4 7.3 %collective-permute-start.4 = (bf16[192,512]{1,0:T(8,128)(2,1)S(1)}, bf16[192,512]{1,0:T(8,128)(2,1)S(1)}, u32[]{:S(2)}, u32[]{:S(2)}) collective-permute-start(bf16[192,512]{1,0:T(8,128)(2,1)S(1)} %collective-permute-done.1.refs_4_), channel_id=1, source_target_pairs={{0,4},{1,5},{2,6},{3,7},{4,0},{5,1},{6,2},{7,3},{8,12},{9,13},{10,... | collective-permute-start | bytes 589832 | tf_op jit(solution)/shard_map/ppermute | solution.py:186
  26.9 7.8 %collective-permute-start.14 = (bf16[192,512]{1,0:T(8,128)(2,1)S(1)}, bf16[192,512]{1,0:T(8,128)(2,1)S(1)}, u32[]{:S(2)}, u32[]{:S(2)}) collective-permute-start(bf16[192,512]{1,0:T(8,128)(2,1)S(1)} %collective-permute-done.11.refs_5_), channel_id=1, source_target_pairs={{0,2},{1,3},{2,0},{3,1},{4,6},{5,7},{6,4},{7,5},{8,10},{9,11},{10,... | collective-permute-start | bytes 589832 | tf_op jit(solution)/shard_map/ppermute | solution.py:186
  27.5 7.7 %collective-permute-start.15 = (bf16[192,512]{1,0:T(8,128)(2,1)S(1)}, bf16[192,512]{1,0:T(8,128)(2,1)S(1)}, u32[]{:S(2)}, u32[]{:S(2)}) collective-permute-start(bf16[192,512]{1,0:T(8,128)(2,1)S(1)} %collective-permute-done.11.refs_5_), channel_id=1, source_target_pairs={{0,4},{1,5},{2,6},{3,7},{4,0},{5,1},{6,2},{7,3},{8,12},{9,13},{10,... | collective-permute-start | bytes 589832 | tf_op jit(solution)/shard_map/ppermute | solution.py:186
  28.1 10.8 %collective-permute-start.8 = (bf16[192,512]{1,0:T(8,128)(2,1)S(1)}, bf16[192,512]{1,0:T(8,128)(2,1)S(1)}, u32[]{:S(2)}, u32[]{:S(2)}) collective-permute-start(bf16[192,512]{1,0:T(8,128)(2,1)S(1)} %collective-permute-done.7.refs_1_), channel_id=1, source_target_pairs={{0,2},{1,3},{2,0},{3,1},{4,6},{5,7},{6,4},{7,5},{8,10},{9,11},{10,... | collective-permute-start | bytes 589832 | tf_op jit(solution)/shard_map/ppermute | solution.py:186
  29.7 14.6 %collective-permute-start.5 = (bf16[192,512]{1,0:T(8,128)(2,1)S(1)}, bf16[192,512]{1,0:T(8,128)(2,1)S(1)}, u32[]{:S(2)}, u32[]{:S(2)}) collective-permute-start(bf16[192,512]{1,0:T(8,128)(2,1)S(1)} %collective-permute-done.4.refs_6_), channel_id=1, source_target_pairs={{0,2},{1,3},{2,0},{3,1},{4,6},{5,7},{6,4},{7,5},{8,10},{9,11},{10,... | collective-permute-start | bytes 589832 | tf_op jit(solution)/shard_map/ppermute | solution.py:186
  34.8 9.6 %collective-permute-start.9 = (bf16[192,512]{1,0:T(8,128)(2,1)S(1)}, bf16[192,512]{1,0:T(8,128)(2,1)S(1)}, u32[]{:S(2)}, u32[]{:S(2)}) collective-permute-start(bf16[192,512]{1,0:T(8,128)(2,1)S(1)} %collective-permute-done.7.refs_1_), channel_id=1, source_target_pairs={{0,4},{1,5},{2,6},{3,7},{4,0},{5,1},{6,2},{7,3},{8,12},{9,13},{10,... | collective-permute-start | bytes 589832 | tf_op jit(solution)/shard_map/ppermute | solution.py:186
  35.2 9.2 %collective-permute-start.16 = (bf16[96,512]{1,0:T(8,128)(2,1)S(1)}, bf16[96,512]{1,0:T(8,128)(2,1)S(1)}, u32[]{:S(2)}, u32[]{:S(2)}) collective-permute-start(bf16[96,512]{1,0:T(8,128)(2,1)S(1)} %slice.25), channel_id=1, source_target_pairs={{0,4},{1,5},{2,6},{3,7},{4,0},{5,1},{6,2},{7,3},{8,12},{9,13},{10,... | collective-permute-start | bytes 294920 | tf_op jit(solution)/shard_map/ppermute | solution.py:186
  36.9 7.5 %collective-permute-start.17 = (bf16[96,512]{1,0:T(8,128)(2,1)S(1)}, bf16[96,512]{1,0:T(8,128)(2,1)S(1)}, u32[]{:S(2)}, u32[]{:S(2)}) collective-permute-start(bf16[96,512]{1,0:T(8,128)(2,1)S(1)} %slice.26), channel_id=1, source_target_pairs={{0,2},{1,3},{2,0},{3,1},{4,6},{5,7},{6,4},{7,5},{8,10},{9,11},{10,... | collective-permute-start | bytes 294920 | tf_op jit(solution)/shard_map/ppermute | solution.py:186
  38.9 5.7 %collective-permute-start.10 = (bf16[192,512]{1,0:T(8,128)(2,1)S(1)}, bf16[192,512]{1,0:T(8,128)(2,1)S(1)}, u32[]{:S(2)}, u32[]{:S(2)}) collective-permute-start(bf16[192,512]{1,0:T(8,128)(2,1)S(1)} %collective-permute-done.8.refs_2_), channel_id=1, source_target_pairs={{0,4},{1,5},{2,6},{3,7},{4,0},{5,1},{6,2},{7,3},{8,12},{9,13},{10,... | collective-permute-start | bytes 589832 | tf_op jit(solution)/shard_map/ppermute | solution.py:186
  39.4 1.6 %copy-start = (bf16[2,64,8192]{2,1,0:T(8,128)(2,1)S(1)}, bf16[2,64,8192]{2,1,0:T(8,128)(2,1)}, u32[]{:S(2)}) copy-start(bf16[2,64,8192]{2,1,0:T(8,128)(2,1)} %param.10) | copy-start | bytes 6291460
  41.0 0.9 %copy-start.4 = (bf16[192,512]{1,0:T(8,128)(2,1)S(1)}, bf16[192,512]{1,0:T(8,128)(2,1)}, u32[]{:S(2)}) copy-start(bf16[192,512]{1,0:T(8,128)(2,1)} %copy-done.3) | copy-start | bytes 589828
  41.9 2.7 %copy-start.1 = (bf16[2,64,8192]{2,1,0:T(8,128)(2,1)S(1)}, bf16[2,64,8192]{2,1,0:T(8,128)(2,1)}, u32[]{:S(2)}) copy-start(bf16[2,64,8192]{2,1,0:T(8,128)(2,1)} %param.10) | copy-start | bytes 6291460
  44.6 1.6 %copy-start.5 = (bf16[2,64,8192]{2,1,0:T(8,128)(2,1)S(1)}, bf16[2,64,8192]{2,1,0:T(8,128)(2,1)}, u32[]{:S(2)}) copy-start(bf16[2,64,8192]{2,1,0:T(8,128)(2,1)} %param.11) | copy-start | bytes 6291460
  46.3 1.0 %copy-start.6 = (bf16[192,256]{1,0:T(8,128)(2,1)}, bf16[192,256]{1,0:T(8,128)(2,1)S(1)}, u32[]{:S(2)}) copy-start(bf16[192,256]{1,0:T(8,128)(2,1)S(1)} %get-tuple-element.170.low_ref) | copy-start | bytes 294916
  47.2 0.8 %copy-start.2 = (bf16[32,32,256]{2,1,0:T(8,128)(2,1)}, bf16[32,32,256]{2,1,0:T(8,128)(2,1)S(1)}, u32[]{:S(2)}) copy-start(bf16[32,32,256]{2,1,0:T(8,128)(2,1)S(1)} %again.2) | copy-start | bytes 1572868
  48.0 7.5 %collective-permute-start.19 = (bf16[256,8192]{1,0:T(8,128)(2,1)}, bf16[256,8192]{1,0:T(8,128)(2,1)}, u32[]{:S(2)}, u32[]{:S(2)}) collective-permute-start(bf16[256,8192]{1,0:T(8,128)(2,1)} %refs_2_.1), channel_id=1, source_target_pairs={{0,1},{1,0},{2,3},{3,2},{4,5},{5,4},{6,7},{7,6},{8,9},{9,8},{10,11... | collective-permute-start | bytes 12582920 | tf_op jit(solution)/shard_map/ppermute | solution.py:189
  48.0 19.2 %all-to-all-start.1 = ((bf16[32,32,256]{2,1,0:T(8,128)(2,1)}), bf16[32,32,256]{2,1,0:T(8,128)(2,1)}, u32[]{:S(2)}, u32[]{:S(2)}) async-start(bf16[32,32,256]{2,1,0:T(8,128)(2,1)} %copy-done.2), calls=%async_computation.1 | async-start | bytes 1048576 | tf_op jit(solution)/shard_map/all_to_all | solution.py:276
  59.9 7.3 %collective-permute-start.20 = (f32[192,256]{1,0:T(8,128)}, f32[192,256]{1,0:T(8,128)}, u32[]{:S(2)}, u32[]{:S(2)}) collective-permute-start(f32[192,256]{1,0:T(8,128)} %other.1), channel_id=1, source_target_pairs={{0,1},{1,0},{2,3},{3,2},{4,5},{5,4},{6,7},{7,6},{8,9},{9,8},{10,11... | collective-permute-start | bytes 589832 | tf_op jit(solution)/shard_map/ppermute | solution.py:189
